TPU v7x, 32 devices: a whole 2x2x4 slice. The times are simulated.
32 devices in a mesh: tm: 4 (over y, x), space: 8 (over z, core).
Axes of the slice: x: 2, y: 2, z: 4, core: 2. Of those that a mesh axis runs over, the one named last changes fastest.
Arguments:
- conserved_field: float32 [16, 10, 64, 1024], P('tm', None, None, 'space'), may hold values from -6 to 6
- face_neighbours: int32 [2, 1024], P(None, 'space'), may hold values from 0 to 1023, as said below
- counterpart_group: int32 [16], P('tm'), may hold values from 0 to 7
- counterpart_shift: int32 [16], P('tm'), may hold values from 0 to 127
- volume_operator: float32 [2, 64, 64], replicated, may hold values from -0.75 to 0.75
- flux_matrix: float32 [2, 10, 10], replicated, may hold values from -2 to 2
Outputs:
- new_state: float32 [16, 10, 64, 1024], P('tm', None, None, 'space')
- last_residual: float32 [16, 10, 64, 1024], P('tm', None, None, 'space')
Inputs may be any that keep to these rules, and one draw needn't show every extreme that they name: face_neighbours[0, e] = (e - d) mod 1024 and face_neighbours[1, e] = (e + d2) mod 1024 with 1 <= d, d2 <= 4; both distances 4 occur.
All inputs are finite; a program needn't handle non-finite values.
Results may differ from a plain program's by a relative error of at most 0.0001.
Values sent between devices are 32-bit elements; how exact they have to be, the bound alone decides.
No kernel may reach another device: no remote copies, remote signals or barrier semaphores. Data moves between devices by JAX's collectives and lax.ppermute only.
A program may use at most 64 MiB of HBM per device.

v0:
```python
import jax
import jax.numpy as jnp
from jax import lax
from jax.sharding import PartitionSpec as P

SAMPLE_COUNT = 16
REACH = 4
ITERS = 2


lift_scale = 2.0
dissipation = 1.5
angular_speed = 0.5
damping_factor = 4.0
pseudo_step = 0.2


def from_behind(shard, axis, by):
    length = lax.axis_size(axis)
    return lax.ppermute(shard, axis, [(i, (i + by) % length) for i in range(length)])


def face_traces(field):
    inst_count = field.shape[0]
    var_count = field.shape[1]
    elem_count = field.shape[-1]
    cube_view = field.reshape(inst_count, var_count, 4, 4, 4, elem_count)
    lower_face = cube_view[:, :, 0].reshape(inst_count, var_count, 16, elem_count)
    upper_face = cube_view[:, :, 3].reshape(inst_count, var_count, 16, elem_count)
    slide_face = cube_view[:, :, :, :, 3].reshape(inst_count, var_count, 16, elem_count)
    return (lower_face, upper_face, slide_face)


def momentum_turning(boundary_samples, cycle_samples):
    blade_azimuth = 2.0 * jnp.pi * cycle_samples.astype(jnp.float32) / SAMPLE_COUNT
    cosine = jnp.cos(blade_azimuth)[:, None, None]
    sine = jnp.sin(blade_azimuth)[:, None, None]
    first_comp = boundary_samples[:, 1]
    second_comp = boundary_samples[:, 2]
    turned_one = cosine * first_comp - sine * second_comp
    turned_two = sine * first_comp + cosine * second_comp
    return jnp.concatenate(
        [
            boundary_samples[:, :1],
            turned_one[:, None],
            turned_two[:, None],
            boundary_samples[:, 3:],
        ],
        axis=1,
    )


def face_term(matrix, normal_sign, outside, inside):
    jump = outside - inside
    mixed = jnp.einsum("vw,twqe->tvqe", matrix, jump, precision=lax.Precision.HIGHEST)
    return 0.5 * lift_scale * (normal_sign * mixed - dissipation * jump)


def assemble(lower_term, upper_term, slide_term):
    inst_count = lower_term.shape[0]
    var_count = lower_term.shape[1]
    elem_count = lower_term.shape[-1]
    shaped = (inst_count, var_count, 4, 4, elem_count)
    corrections = jnp.zeros((inst_count, var_count, 4, 4, 4, elem_count), lower_term.dtype)
    corrections = corrections.at[:, :, 0].add(lower_term.reshape(shaped))
    corrections = corrections.at[:, :, 3].add(upper_term.reshape(shaped))
    corrections = corrections.at[:, :, :, :, 3].add(slide_term.reshape(shaped))
    return corrections.reshape(inst_count, var_count, 64, elem_count)


def spectral_operator():
    highest = lax.Precision.HIGHEST
    fourier_wavenumbers = jnp.arange(1, SAMPLE_COUNT // 2).astype(jnp.float32)
    cycle_samples = jnp.arange(SAMPLE_COUNT).astype(jnp.float32)
    rotation_angles = (
        2.0 * jnp.pi * fourier_wavenumbers[:, None] * cycle_samples[None, :] / SAMPLE_COUNT
    )
    gains = (
        2.0
        * angular_speed
        * fourier_wavenumbers
        * jnp.exp(-damping_factor * (fourier_wavenumbers / (SAMPLE_COUNT // 2)) ** 8)
        / SAMPLE_COUNT
    )
    cosine_table = jnp.cos(rotation_angles)
    sine_table = jnp.sin(rotation_angles)
    weighted_sin = gains[:, None] * sine_table
    weighted_cos = gains[:, None] * cosine_table
    return jnp.dot(cosine_table.T, weighted_sin, precision=highest) - jnp.dot(
        sine_table.T, weighted_cos, precision=highest
    )


def volume_matrix(volume_operator, flux_matrix):
    var_count = flux_matrix.shape[1]
    node_total = volume_operator.shape[1]
    joined = flux_matrix[:, :, None, :, None] * volume_operator[:, None, :, None, :]
    return jnp.sum(joined, axis=0).reshape(var_count * node_total, var_count * node_total)


def residual_of(
    field, face_neighbours, counterpart_group, counterpart_shift, volume_operator, flux_matrix
):
    sample_position = field.shape[0]
    var_count = field.shape[1]
    node_total = field.shape[2]
    elem_local = field.shape[-1]
    highest = lax.Precision.HIGHEST
    combined = volume_matrix(volume_operator, flux_matrix)
    flat_field = field.reshape(sample_position, var_count * node_total, elem_local)
    volume = jnp.einsum("ij,tje->tie", combined, flat_field, precision=highest).reshape(field.shape)
    lower_face, upper_face, slide_face = face_traces(field)
    prev_upper = from_behind(upper_face[..., elem_local - REACH :], "space", 1)
    next_lower = from_behind(lower_face[..., :REACH], "space", -1)
    element_total = elem_local * lax.axis_size("space")
    local_index = jnp.arange(elem_local, dtype=jnp.int32)
    global_index = lax.axis_index("space") * elem_local + local_index
    back_gap = (global_index - face_neighbours[0]) % element_total
    ahead_gap = (face_neighbours[1] - global_index) % element_total
    before_joined = jnp.concatenate([prev_upper, upper_face], axis=-1)
    after_joined = jnp.concatenate([lower_face, next_lower], axis=-1)
    lower_out = jnp.zeros_like(upper_face)
    upper_out = jnp.zeros_like(lower_face)
    for distance in range(1, REACH + 1):
        lower_out = jnp.where(
            back_gap == distance,
            before_joined[..., REACH - distance : REACH - distance + elem_local],
            lower_out,
        )
        upper_out = jnp.where(
            ahead_gap == distance, after_joined[..., distance : distance + elem_local], upper_out
        )
    window_start = (
        lax.axis_index("space") * elem_local + counterpart_group * elem_local + counterpart_shift
    ) % element_total
    carried = jnp.zeros_like(slide_face)
    segment = lax.all_gather(slide_face, "space", axis=3, tiled=True)
    span_rows = segment.shape[-1]
    filler = jnp.zeros(segment.shape[:-1] + (elem_local,), segment.dtype)
    padded = jnp.concatenate([filler, segment, filler], axis=-1)
    relative = window_start % element_total
    results = []
    for sample_slot in range(sample_position):
        picked_rows = carried[sample_slot]
        for offset in (relative[sample_slot], relative[sample_slot] - element_total):
            position = local_index + offset
            inside = (position >= 0) & (position < span_rows)
            begin = jnp.clip(offset + elem_local, 0, span_rows + elem_local)
            window = lax.dynamic_slice_in_dim(padded[sample_slot], begin, elem_local, 2)
            picked_rows = jnp.where(inside, window, picked_rows)
        results.append(picked_rows)
    paired_boundary = jnp.stack(results)
    cycle_samples = lax.axis_index("tm") * sample_position + jnp.arange(
        sample_position, dtype=jnp.int32
    )
    paired_boundary = momentum_turning(paired_boundary, cycle_samples)
    corrections = assemble(
        face_term(flux_matrix[0], -1.0, lower_out, lower_face),
        face_term(flux_matrix[0], 1.0, upper_out, upper_face),
        face_term(flux_matrix[1], 1.0, paired_boundary, slide_face),
    )
    operator = spectral_operator()
    gathered = lax.all_to_all(field, "tm", split_axis=2, concat_axis=0, tiled=True)
    flat = gathered.reshape(gathered.shape[0], -1)
    back_out = jnp.dot(operator, flat, precision=highest).reshape(gathered.shape)
    cyclic_signal = lax.all_to_all(back_out, "tm", split_axis=0, concat_axis=2, tiled=True)
    return volume + corrections + cyclic_signal


def per_device(
    conserved_field,
    face_neighbours,
    counterpart_group,
    counterpart_shift,
    volume_operator,
    flux_matrix,
):
    field = conserved_field
    residual = jnp.zeros_like(field)
    for sweep_index in range(ITERS):
        residual = residual_of(
            field,
            face_neighbours,
            counterpart_group,
            counterpart_shift,
            volume_operator,
            flux_matrix,
        )
        field = field - pseudo_step * residual
    return (field, residual)


def solution(mesh):
    return jax.shard_map(
        per_device,
        mesh=mesh,
        in_specs=(P("tm", None, None, "space"), P(None, "space"), P("tm"), P("tm"), P(), P()),
        out_specs=(P("tm", None, None, "space"), P("tm", None, None, "space")),
        check_vma=False,
    )
```

profile of v0, /device:TPU:1, one launch (start us, length us, event | category | flops | bytes accessed | tf_op | source)
XLA Modules:
  0.0 174.2 jit_solution(12139349933429266117)
XLA Ops:
  7.2 1.8 %slice.458 = f32[4,10,4,4,1,128]{5,4,3,2,1,0:T(1,128)S(1)} slice(f32[4,10,4,4,4,128]{5,4,3,2,1,0:T(4,128)} %bitcast.158), slice={[0:4], [0:10], [0:4], [0:4], [3:4], [0:128]} | slice | bytes 655360 | tf_op jit(solution)/shard_map/slice | solution.py:30
  9.0 0.7 copy-done.10
  9.7 0.9 copy.163
  10.7 0.9 copy.162
  11.8 1.0 slice.441
  12.8 2.6 %collective-permute-start = (f32[4,10,16,4]{3,1,2,0:T(8,128)}, f32[4,10,16,4]{3,1,2,0:T(8,128)}, u32[]{:S(2)}, u32[]{:S(2)}) collective-permute-start(f32[4,10,16,4]{3,1,2,0:T(8,128)} %slice.441), channel_id=1, source_target_pairs={{0,1},{1,2},{2,3},{3,4},{4,5},{5,6},{6,7},{7,0},{8,9},{9,10},{10,1... | collective-permute-start | bytes 30728 | tf_op jit(solution)/shard_map/ppermute | solution.py:20
  15.5 2.1 %copy.136 = f32[4,10,64,128]{3,1,0,2:T(8,128)} copy(f32[4,10,64,128]{3,2,1,0:T(8,128)S(1)} %copy-done) | data formatting | bytes 2621440 | tf_op args[0]
  17.6 5.2 %all-to-all-start = ((f32[4,10,64,128]{3,1,0,2:T(8,128)}), f32[4,10,64,128]{3,1,0,2:T(8,128)}, u32[]{:S(2)}, u32[]{:S(2)}) async-start(f32[4,10,64,128]{3,1,0,2:T(8,128)} %copy.136), calls=%async_computation | async-start | bytes 4194304 | tf_op jit(solution)/shard_map/all_to_all | solution.py:163
  22.9 0.6 fusion.112
  25.8 0.6 multiply_reduce_fusion
  26.4 4.4 %copy.125 = f32[10,64,10,64]{3,2,1,0:T(8,128)} copy(f32[10,64,10,64]{3,1,2,0:T(8,128)S(1)} %multiply_reduce_fusion) | data formatting | bytes 3276800 | tf_op jit(solution)/shard_map/reduce_sum | solution.py:98
  30.9 3.8 %reshape.388 = f32[640,640,1]{1,0,2:T(8,128)S(1)} reshape(f32[10,64,10,64]{3,2,1,0:T(8,128)} %copy.125) | data formatting | bytes 3276800 | tf_op jit(solution)/shard_map/reshape | solution.py:98
  34.8 0.6 compare_and_fusion.6
  35.4 0.6 compare_and_fusion
  36.3 0.6 compare_and_fusion.2
  37.2 0.5 broadcast_compare_fusion.4
  37.8 4.3 %fusion.113 = f32[640,4,128]{2,0,1:T(8,128)} fusion(f32[640,640,1]{1,0,2:T(8,128)S(1)} %reshape.388, f32[4,640,128]{2,1,0:T(8,128)S(1)} %bitcast.160), kind=kOutput, calls=%fused_computation.222 | convolution fusion | flops 2516582400 | bytes 4259840 | tf_op jit(solution)/shard_map/ij,tje->tie/dot_general | solution.py:111
  42.1 5.1 %all-to-all-done = f32[4,10,64,128]{3,1,0,2:T(8,128)} async-done(((f32[4,10,64,128]{3,1,0,2:T(8,128)}), f32[4,10,64,128]{3,1,0,2:T(8,128)}, u32[]{:S(2)}, u32[]{:S(2)}) %all-to-all-start) | async-done | bytes 1310752 | tf_op jit(solution)/shard_map/all_to_all | solution.py:163
  47.2 2.4 %copy.180 = f32[4,10,4,16,128]{4,3,1,0,2:T(8,128)S(1)} copy(f32[4,10,4,16,128]{4,1,0,3,2:T(8,128)} %bitcast.38) | data formatting | bytes 2621440 | tf_op jit(solution)/shard_map/all_to_all | solution.py:163
  49.6 1.3 reshape.381
  50.9 1.6 copy.167
  52.5 1.8 %fusion.4 = f32[16,10,16,128]{3,0,2,1:T(8,128)S(1)} fusion(f32[16,16,1,1]{1,0,3,2:T(8,128)S(1)} %fusion.14, f32[10,16,128,16]{2,1,0,3:T(8,128)S(1)} %bitcast.166), kind=kOutput, calls=%fused_computation.37 | convolution fusion | flops 62914560 | bytes 2622464 | tf_op jit(solution)/shard_map/dot_general | solution.py:165
  54.3 1.5 copy.139
  55.7 4.3 %all-to-all-start.1 = ((f32[16,10,16,128]{3,2,1,0:T(8,128)}), f32[16,10,16,128]{3,2,1,0:T(8,128)}, u32[]{:S(2)}, u32[]{:S(2)}) async-start(f32[16,10,16,128]{3,2,1,0:T(8,128)} %copy.139), calls=%async_computation.1 | async-start | bytes 2621440 | tf_op jit(solution)/shard_map/all_to_all | solution.py:166
  60.3 0.6 compare_and_fusion.4
  65.7 5.3 %fusion.13 = f32[4,10,16,128]{3,1,2,0:T(8,128)S(1)} fusion(f32[4,10,16,128]{3,1,2,0:T(8,128)} %bitcast.6, f32[4,10,16,128]{3,1,2,0:T(8,128)S(1)} %bitcast.180, f32[4,10,16,4]{3,1,2,0:T(8,128)} %collective-permute-done, pred[128]{0:T(512)(128)(4,1)S(1)} %get-tuple-element.111, pred[128]{0:T(512)(128)(4,1)S(1)} %get-tuple-element.110, ...), kind=kOutput, calls=%fused_computation.54 | convolution fusion | flops 11550720 | bytes 3485696 | tf_op jit(solution)/shard_map/vw,twqe->tvqe/dot_general | solution.py:55
  71.3 0.8 copy-done.13
  72.1 7.0 %fusion.6 = f32[4,10,16,128]{3,1,2,0:T(8,128)S(1)} fusion(f32[4,10,16,128]{3,1,2,0:T(8,128)S(1)} %bitcast.181, f32[4,10,16,4]{3,1,2,0:T(8,128)} %collective-permute-done.1, f32[4,10,16,128]{3,1,2,0:T(8,128)} %bitcast.6, pred[128]{0:T(512)(128)(4,1)S(1)} %copy-done.19, pred[128]{0:T(512)(128)(4,1)S(1)} %get-tuple-element.107, ...), kind=kOutput, calls=%fused_computation.45 | convolution fusion | flops 11468800 | bytes 3485696 | tf_op jit(solution)/shard_map/vw,twqe->tvqe/dot_general | solution.py:55
  79.1 2.6 %copy.140 = f32[4,4,10,16,128]{4,3,0,2,1:T(8,128)} copy(f32[4,4,10,16,128]{4,3,2,1,0:T(8,128)} %bitcast.41) | data formatting | bytes 2621440 | tf_op jit(solution)/shard_map/all_to_all | solution.py:166
  81.7 3.1 %pad_maximum_fusion.1 = f32[4,10,16,1280]{3,1,2,0:T(8,128)S(1)} fusion(f32[4,10,16,128]{3,1,2,0:T(8,128)S(1)} %broadcast.267, f32[4,10,16,1024]{3,1,2,0:T(8,128)} %all-gather.3.cloned.1.call-done), kind=kLoop, calls=%fused_computation.1 | loop fusion | flops 1638400 | bytes 6225920 | tf_op jit(solution)/shard_map/concatenate | solution.py:140
  86.9 0.7 fusion.7
  87.8 0.5 copy.135
  88.3 0.8 copy-done.2
  89.1 0.4 copy-done.3
  89.5 0.6 fusion.1
  90.0 0.3 slice.481
  90.4 1.0 copy.166
  91.4 1.9 %copy.152 = f32[4,10,64,128]{3,0,1,2:T(4,128)} copy(f32[4,10,64,128]{3,2,1,0:T(8,128)S(1)} %fusion.1) | data formatting | bytes 2621440 | tf_op jit(solution)/shard_map/sub | solution.py:189
  93.3 3.5 %all-to-all-start.2 = ((f32[4,10,64,128]{3,0,1,2:T(4,128)}), f32[4,10,64,128]{3,0,1,2:T(4,128)S(1)}, u32[]{:S(2)}, u32[]{:S(2)}) async-start(f32[4,10,64,128]{3,0,1,2:T(4,128)} %copy.152), calls=%async_computation.2 | async-start | bytes 2621440 | tf_op jit(solution)/shard_map/all_to_all | solution.py:163
  96.8 0.8 fusion.110
  97.7 1.0 slice.465
  98.7 3.0 %collective-permute-start.2 = (f32[4,10,16,4]{3,1,2,0:T(8,128)}, f32[4,10,16,4]{3,1,2,0:T(8,128)}, u32[]{:S(2)}, u32[]{:S(2)}) collective-permute-start(f32[4,10,16,4]{3,1,2,0:T(8,128)} %slice.465), channel_id=1, source_target_pairs={{0,1},{1,2},{2,3},{3,4},{4,5},{5,6},{6,7},{7,0},{8,9},{9,10},{10,1... | collective-permute-start | bytes 30728 | tf_op jit(solution)/shard_map/ppermute | solution.py:20
  101.7 11.1 %all-to-all-done.2 = f32[4,10,64,128]{3,0,1,2:T(4,128)S(1)} async-done(((f32[4,10,64,128]{3,0,1,2:T(4,128)}), f32[4,10,64,128]{3,0,1,2:T(4,128)S(1)}, u32[]{:S(2)}, u32[]{:S(2)}) %all-to-all-start.2) | async-done | bytes 1310752 | tf_op jit(solution)/shard_map/all_to_all | solution.py:163
  112.8 1.3 copy.179
  114.1 1.6 reshape.387
  115.9 1.8 %fusion.2 = f32[16,10,16,128]{3,0,2,1:T(8,128)S(1)} fusion(f32[16,16,1,1]{1,0,3,2:T(8,128)S(1)} %fusion.14, f32[10,16,128,16]{2,1,0,3:T(8,128)S(1)} %bitcast.163), kind=kOutput, calls=%fused_computation.34 | convolution fusion | flops 62914560 | bytes 2622464 | tf_op jit(solution)/shard_map/dot_general | solution.py:165
  117.8 1.5 copy.155
  119.2 3.5 %all-to-all-start.3 = ((f32[16,10,16,128]{3,2,1,0:T(8,128)}), f32[16,10,16,128]{3,2,1,0:T(8,128)S(1)}, u32[]{:S(2)}, u32[]{:S(2)}) async-start(f32[16,10,16,128]{3,2,1,0:T(8,128)} %copy.155), calls=%async_computation.3 | async-start | bytes 2621440 | tf_op jit(solution)/shard_map/all_to_all | solution.py:166
  122.8 8.8 %convolution_bitcast_fusion = f32[4,640,128]{1,2,0:T(8,128)} fusion(f32[4,640,128]{2,1,0:T(8,128)S(1)} %bitcast.157, f32[640,640,1]{1,0,2:T(8,128)} %copy-done.1), kind=kOutput, calls=%fused_computation.29 | convolution fusion | flops 2516582400 | bytes 4259840 | tf_op jit(solution)/shard_map/ij,tje->tie/dot_general | solution.py:111
  131.6 2.8 %copy.142 = f32[4,640,128]{2,1,0:T(8,128)} copy(f32[4,640,128]{1,2,0:T(8,128)} %convolution_bitcast_fusion) | data formatting | bytes 2621440 | tf_op jit(solution)/shard_map/ij,tje->tie/transpose | solution.py:111
  134.4 1.1 copy.165
  135.6 1.7 collective-permute-start.3
  137.2 5.4 %fusion.11 = f32[4,10,16,128]{3,1,2,0:T(8,128)S(1)} fusion(f32[4,10,16,128]{3,1,2,0:T(8,128)S(1)} %bitcast.193, f32[4,10,16,128]{3,1,2,0:T(8,128)S(1)} %bitcast.183, f32[4,10,16,4]{3,1,2,0:T(8,128)} %collective-permute-done.2, pred[128]{0:T(512)(128)(4,1)} %copy-done.25, pred[128]{0:T(512)(128)(4,1)S(1)} %copy-done.24, pred[128]{0:T(512)(128)(4,1)S(1)} %copy-done.22, ...), kind=kOutput, calls=%fused_computation.51 | convolution fusion | flops 11550720 | bytes 3485696 | tf_op jit(solution)/shard_map/vw,twqe->tvqe/dot_general | solution.py:55
  142.7 1.6 scatter-add.25
  144.3 6.1 %collective-permute-done.3 = f32[4,10,16,4]{3,1,2,0:T(8,128)S(1)} collective-permute-done((f32[4,10,16,4]{3,1,2,0:T(8,128)S(1)}, f32[4,10,16,4]{3,1,2,0:T(8,128)S(1)}, u32[]{:S(2)}, u32[]{:S(2)}) %collective-permute-start.3) | collective-permute-done | bytes 10272 | tf_op jit(solution)/shard_map/ppermute | solution.py:20
  150.4 2.4 %fusion.8 = f32[4,10,16,128]{3,1,2,0:T(8,128)S(1)} fusion(f32[4,10,16,128]{3,1,2,0:T(8,128)S(1)} %bitcast.184, f32[4,10,16,4]{3,1,2,0:T(8,128)S(1)} %collective-permute-done.3, f32[4,10,16,128]{3,1,2,0:T(8,128)S(1)} %bitcast.194, pred[128]{0:T(512)(128)(4,1)S(1)} %copy-done.20, pred[128]{0:T(512)(128)(4,1)S(1)} %get-tuple-element.107, ...), kind=kOutput, calls=%fused_computation.47 | convolution fusion | flops 11468800 | bytes 3485696 | tf_op jit(solution)/shard_map/vw,twqe->tvqe/dot_general | solution.py:55
  152.8 0.8 copy_dynamic-update-slice_fusion
  153.6 1.2 copy.156
  154.9 2.9 %pad_maximum_fusion = f32[4,10,16,1280]{3,1,2,0:T(8,128)S(1)} fusion(f32[4,10,16,128]{3,1,2,0:T(8,128)S(1)} %copy-done.7, f32[4,10,16,1024]{3,1,2,0:T(8,128)} %all-gather.5.cloned.1.call-done), kind=kLoop, calls=%fused_computation | loop fusion | flops 1638400 | bytes 6225920 | tf_op jit(solution)/shard_map/concatenate | solution.py:140
  159.3 0.4 copy-done.9
  159.8 0.7 fusion.9
  160.5 1.9 %fusion.43 = f32[4,10,4,4,4,128]{5,1,3,2,0,4:T(8,128)} fusion(f32[4,10,4,4,4,128]{5,1,3,2,0,4:T(8,128)} %copy_dynamic-update-slice_fusion, f32[4,10,4,4,1,128]{5,1,3,2,0,4:T(8,128)S(1)} %bitcast.185), kind=kLoop, calls=%fused_computation.86 | loop fusion | flops 81920 | bytes 1376256 | tf_op jit(solution)/shard_map/scatter-add | solution.py:67
  162.4 2.6 %copy.151 = f32[4,10,4,4,4,128]{5,4,3,2,1,0:T(4,128)S(1)} copy(f32[4,10,4,4,4,128]{5,1,3,2,0,4:T(8,128)} %fusion.43) | data formatting | bytes 2621440 | tf_op jit(solution)/shard_map/scatter-add | solution.py:67
  165.0 2.1 %multiply_subtract_fusion = (f32[4,10,64,128]{3,2,1,0:T(8,128)}, f32[4,10,64,128]{3,2,1,0:T(8,128)}) fusion(f32[4,10,64,128]{3,2,1,0:T(8,128)S(1)} %fusion.1, f32[4,4,10,16,128]{4,3,0,2,1:T(8,128)S(1)} %copy-done.5, f32[4,10,64,128]{3,2,1,0:T(8,128)S(1)} %bitcast.171, f32[4,10,64,128]{3,2,1,0:T(8,128)S(1)} %bitcast.172), kind=kLoop, calls=%fused_computation.40 | loop fusion | flops 1310720 | bytes 7864320 | tf_op jit(solution)/shard_map/sub | solution.py:189
  (95 shorter events, 5.8 us)
Async XLA Ops:
  7.2 3.5 %copy-start = (f32[4,10,64,128]{3,2,1,0:T(8,128)S(1)}, f32[4,10,64,128]{3,2,1,0:T(8,128)}, u32[]{:S(2)}) copy-start(f32[4,10,64,128]{3,2,1,0:T(8,128)} %param.18) | copy-start | bytes 3932164
  7.2 74.5 %all-gather.3.cloned.1.call-start = ((), (), s32[]{:S(2)}) async-start(), calls=%async_computation.4 | async-start | bytes 4718592 | tf_op jit(solution)/shard_map/all_gather | solution.py:137
  9.0 0.7 copy-start.10
  11.6 59.7 %collective-permute-start.1 = (f32[4,10,16,4]{3,1,2,0:T(8,128)}, f32[4,10,16,4]{3,1,2,0:T(8,128)}, u32[]{:S(2)}, u32[]{:S(2)}) collective-permute-start(f32[4,10,16,4]{3,1,2,0:T(8,128)} %bitcast.153), channel_id=1, source_target_pairs={{0,7},{1,0},{2,1},{3,2},{4,3},{5,4},{6,5},{7,6},{8,15},{9,8},{10,9... | collective-permute-start | bytes 30728 | tf_op jit(solution)/shard_map/ppermute | solution.py:20
  11.8 53.9 %copy-start.12 = (f32[4,10,1,4,4,128]{5,1,4,3,0,2:T(8,128)}, f32[4,10,1,4,4,128]{5,1,4,3,0,2:T(8,128)S(1)}, u32[]{:S(2)}) copy-start(f32[4,10,1,4,4,128]{5,1,4,3,0,2:T(8,128)S(1)} %copy.161) | copy-start | bytes 983044
  12.8 52.8 %collective-permute-start = (f32[4,10,16,4]{3,1,2,0:T(8,128)}, f32[4,10,16,4]{3,1,2,0:T(8,128)}, u32[]{:S(2)}, u32[]{:S(2)}) collective-permute-start(f32[4,10,16,4]{3,1,2,0:T(8,128)} %slice.441), channel_id=1, source_target_pairs={{0,1},{1,2},{2,3},{3,4},{4,5},{5,6},{6,7},{7,0},{8,9},{9,10},{10,1... | collective-permute-start | bytes 30728 | tf_op jit(solution)/shard_map/ppermute | solution.py:20
  17.6 5.2 %copy-start.17 = (s32[4]{0:T(128)S(1)}, s32[4]{0:T(128)}, u32[]{:S(2)}) copy-start(s32[4]{0:T(128)} %param.21) | copy-start | bytes 52
  17.6 5.2 %copy-start.18 = (s32[4]{0:T(128)S(1)}, s32[4]{0:T(128)}, u32[]{:S(2)}) copy-start(s32[4]{0:T(128)} %param.20) | copy-start | bytes 52
  17.6 8.2 %copy-start.15 = (f32[2,10,10]{2,0,1:T(2,128)S(1)}, f32[2,10,10]{2,0,1:T(2,128)}, u32[]{:S(2)}) copy-start(f32[2,10,10]{2,0,1:T(2,128)} %param.23) | copy-start | bytes 2404
  17.6 8.2 %copy-start.14 = (f32[2,64,64]{2,1,0:T(8,128)S(1)}, f32[2,64,64]{2,1,0:T(8,128)}, u32[]{:S(2)}) copy-start(f32[2,64,64]{2,1,0:T(8,128)} %param.22) | copy-start | bytes 98308
  17.6 29.6 %all-to-all-start = ((f32[4,10,64,128]{3,1,0,2:T(8,128)}), f32[4,10,64,128]{3,1,0,2:T(8,128)}, u32[]{:S(2)}, u32[]{:S(2)}) async-start(f32[4,10,64,128]{3,1,0,2:T(8,128)} %copy.136), calls=%async_computation | async-start | bytes 4194304 | tf_op jit(solution)/shard_map/all_to_all | solution.py:163
  30.9 6.3 %copy-start.16 = (s32[2,128]{1,0:T(2,128)S(1)}, s32[2,128]{1,0:T(2,128)}, u32[]{:S(2)}) copy-start(s32[2,128]{1,0:T(2,128)} %param.19) | copy-start | bytes 3076
  34.7 7.4 %copy-start.1 = (f32[640,640,1]{1,0,2:T(8,128)}, f32[640,640,1]{1,0,2:T(8,128)S(1)}, u32[]{:S(2)}) copy-start(f32[640,640,1]{1,0,2:T(8,128)S(1)} %reshape.388) | copy-start | bytes 4915204
  55.7 23.4 %all-to-all-start.1 = ((f32[16,10,16,128]{3,2,1,0:T(8,128)}), f32[16,10,16,128]{3,2,1,0:T(8,128)}, u32[]{:S(2)}, u32[]{:S(2)}) async-start(f32[16,10,16,128]{3,2,1,0:T(8,128)} %copy.139), calls=%async_computation.1 | async-start | bytes 2621440 | tf_op jit(solution)/shard_map/all_to_all | solution.py:166
  60.1 94.8 %all-gather.5.cloned.1.call-start = ((), (), s32[]{:S(2)}) async-start(), calls=%async_computation.5 | async-start | bytes 4718592 | tf_op jit(solution)/shard_map/all_gather | solution.py:137
  60.3 10.7 %copy-start.21 = (pred[128]{0:T(512)(128)(4,1)}, pred[128]{0:T(512)(128)(4,1)S(1)}, u32[]{:S(2)}) copy-start(pred[128]{0:T(512)(128)(4,1)S(1)} %get-tuple-element.109) | copy-start | bytes 388
  60.3 10.7 %copy-start.23 = (pred[128]{0:T(512)(128)(4,1)}, pred[128]{0:T(512)(128)(4,1)S(1)}, u32[]{:S(2)}) copy-start(pred[128]{0:T(512)(128)(4,1)S(1)} %get-tuple-element.110) | copy-start | bytes 388
  60.3 10.7 %copy-start.25 = (pred[128]{0:T(512)(128)(4,1)}, pred[128]{0:T(512)(128)(4,1)S(1)}, u32[]{:S(2)}) copy-start(pred[128]{0:T(512)(128)(4,1)S(1)} %get-tuple-element.111) | copy-start | bytes 388
  71.0 1.0 copy-start.13
  71.0 1.0 copy-start.19
  81.7 3.1 %copy-start.6 = (f32[4,10,16,128]{3,1,2,0:T(8,128)}, f32[4,10,16,128]{3,1,2,0:T(8,128)S(1)}, u32[]{:S(2)}) copy-start(f32[4,10,16,128]{3,1,2,0:T(8,128)S(1)} %broadcast.267) | copy-start | bytes 983044
  85.3 1.0 copy-start.11
  85.8 1.1 copy-start.8
  87.8 1.3 copy-start.2
  87.8 1.7 copy-start.3
  93.3 19.5 %all-to-all-start.2 = ((f32[4,10,64,128]{3,0,1,2:T(4,128)}), f32[4,10,64,128]{3,0,1,2:T(4,128)S(1)}, u32[]{:S(2)}, u32[]{:S(2)}) async-start(f32[4,10,64,128]{3,0,1,2:T(4,128)} %copy.152), calls=%async_computation.2 | async-start | bytes 2621440 | tf_op jit(solution)/shard_map/all_to_all | solution.py:163
  98.7 38.5 %collective-permute-start.2 = (f32[4,10,16,4]{3,1,2,0:T(8,128)}, f32[4,10,16,4]{3,1,2,0:T(8,128)}, u32[]{:S(2)}, u32[]{:S(2)}) collective-permute-start(f32[4,10,16,4]{3,1,2,0:T(8,128)} %slice.465), channel_id=1, source_target_pairs={{0,1},{1,2},{2,3},{3,4},{4,5},{5,6},{6,7},{7,0},{8,9},{9,10},{10,1... | collective-permute-start | bytes 30728 | tf_op jit(solution)/shard_map/ppermute | solution.py:20
  119.2 34.4 %all-to-all-start.3 = ((f32[16,10,16,128]{3,2,1,0:T(8,128)}), f32[16,10,16,128]{3,2,1,0:T(8,128)S(1)}, u32[]{:S(2)}, u32[]{:S(2)}) async-start(f32[16,10,16,128]{3,2,1,0:T(8,128)} %copy.155), calls=%async_computation.3 | async-start | bytes 2621440 | tf_op jit(solution)/shard_map/all_to_all | solution.py:166
  131.6 5.6 %copy-start.22 = (pred[128]{0:T(512)(128)(4,1)S(1)}, pred[128]{0:T(512)(128)(4,1)}, u32[]{:S(2)}) copy-start(pred[128]{0:T(512)(128)(4,1)} %copy-done.21) | copy-start | bytes 388
  131.6 5.6 %copy-start.24 = (pred[128]{0:T(512)(128)(4,1)S(1)}, pred[128]{0:T(512)(128)(4,1)}, u32[]{:S(2)}) copy-start(pred[128]{0:T(512)(128)(4,1)} %copy-done.23) | copy-start | bytes 388
  135.6 14.8 %collective-permute-start.3 = (f32[4,10,16,4]{3,1,2,0:T(8,128)S(1)}, f32[4,10,16,4]{3,1,2,0:T(8,128)S(1)}, u32[]{:S(2)}, u32[]{:S(2)}) collective-permute-start(f32[4,10,16,4]{3,1,2,0:T(8,128)S(1)} %bitcast.192), channel_id=1, source_target_pairs={{0,7},{1,0},{2,1},{3,2},{4,3},{5,4},{6,5},{7,6},{8,15},{9,8},{10,9... | collective-permute-start | bytes 30728 | tf_op jit(solution)/shard_map/ppermute | solution.py:20
  142.7 7.7 %copy-start.20 = (pred[128]{0:T(512)(128)(4,1)S(1)}, pred[128]{0:T(512)(128)(4,1)}, u32[]{:S(2)}) copy-start(pred[128]{0:T(512)(128)(4,1)} %get-tuple-element.108) | copy-start | bytes 388
  153.6 1.2 copy-start.7
  158.7 1.0 copy-start.9
  162.4 2.6 %copy-start.4 = (f32[4,640,128]{2,1,0:T(8,128)S(1)}, f32[4,640,128]{2,1,0:T(8,128)}, u32[]{:S(2)}) copy-start(f32[4,640,128]{2,1,0:T(8,128)} %copy.142) | copy-start | bytes 3932164
  162.4 2.6 %copy-start.5 = (f32[4,4,10,16,128]{4,3,0,2,1:T(8,128)S(1)}, f32[4,4,10,16,128]{4,3,0,2,1:T(8,128)}, u32[]{:S(2)}) copy-start(f32[4,4,10,16,128]{4,3,0,2,1:T(8,128)} %copy.156) | copy-start | bytes 3932164
Sparse Core Ops, SparseCore 0:
  10.8 58.0 all-gather.2
  91.5 57.2 all-gather.4
where the time goes:
time: 178 us; the launch traced here: 174 us
  local copies, waits for them, and re-layouts  50.1 us (28%)
  matrix products  38.9 us (22%)
  starting transfers between devices  24.1 us (14%)
  waiting for transfers between devices  22.4 us (13%)
  between operations  22 us (12%)
  other arithmetic  16.6 us (9%)
    dot_general x6, matrix products, face_term(): jnp.einsum('vw,twqe->tvqe', matrix, jump, precision=lax.Precision.HIGHEST)  21.5 us
    all_to_all x2, waiting for transfers between devices, residual_of(): lax.all_to_all(field, 'tm', split_axis=2, concat_axis=0, tiled=True)  16.3 us
    dot_general x2, matrix products, residual_of(): jnp.einsum('ij,tje->tie', combined, flat_field, precision=highest)  13.1 us
    unnamed x62, local copies, waits for them, and re-layouts  11.8 us
    all_to_all x2, starting transfers between devices, residual_of(): lax.all_to_all(field, 'tm', split_axis=2, concat_axis=0, tiled=True)  8.71 us
    all_to_all x2, starting transfers between devices, residual_of(): lax.all_to_all(back_out, 'tm', split_axis=0, concat_axis=2, tiled=True)  7.85 us
    ppermute x4, starting transfers between devices, from_behind(): lax.ppermute(shard, axis, [(i, (i + by) % length) for i in range(length)])  7.31 us
    ppermute x4, waiting for transfers between devices, from_behind(): lax.ppermute(shard, axis, [(i, (i + by) % length) for i in range(length)])  6.08 us
  transfers between devices with their start and end apart: 10, of which 3 were waited for; matrix products, arithmetic and copies ran while one was open for 46% of the time, Pallas kernels for 0%

commit v1 on v0

v1 whole, which is shorter than its diff:
```python
import functools

import jax
import jax.numpy as jnp
import numpy as np
from jax import lax
from jax.experimental import pallas as pl
from jax.experimental.pallas import tpu as pltpu
from jax.sharding import PartitionSpec as P

REACH = 4
ITERS = 2
LIFT = 2.0
DISSIPATION = 1.5
ANGULAR = 0.5
DAMPING = 4.0
STEP = 0.2
SUB = 8

VMEM = pl.BlockSpec(memory_space=pltpu.VMEM)
SMEM = pl.BlockSpec(memory_space=pltpu.SMEM)
F32 = jnp.float32
BF16 = jnp.bfloat16


class Sizes:
    def __init__(self, field_shape):
        self.L, self.V, self.Q, self.E = field_shape
        self.R = self.V * self.Q
        self.M = lax.axis_size("tm")
        self.N = lax.axis_size("space")
        self.T = self.L * self.M
        self.Z = self.N // 2
        self.RC = self.R // self.M
        self.face = self.Q // 4
        self.FR = self.V * self.face
        self.PL = self.Z // self.L
        self.CH = self.FR // self.PL
        self.H = SUB * self.L

    def z_rows(self, j):
        if j == 0:
            return 2 * self.H + self.CH
        return self.CH + self.H * ((j == 1) + (j == self.Z - 1))


def time_weights(total):
    k = np.arange(1, total // 2, dtype=np.float64)
    gains = 2.0 * ANGULAR * k * np.exp(-DAMPING * (k / (total // 2)) ** 8) / total
    lag = np.arange(total, dtype=np.float64)
    return np.sum(gains[:, None] * np.sin(2.0 * np.pi * k[:, None] * lag[None, :] / total), axis=0)


def call(body, outs, ins, scratch=(), flops=0, nbytes=0):
    return pl.pallas_call(
        body,
        out_shape=outs,
        in_specs=ins,
        out_specs=jax.tree.map(lambda _: VMEM, outs),
        scratch_shapes=list(scratch),
        cost_estimate=pl.CostEstimate(flops=flops, bytes_accessed=nbytes, transcendentals=0),
        compiler_params=pltpu.CompilerParams(vmem_limit_bytes=40 * 1024 * 1024),
    )


def lanes_of(x, index):
    return jnp.take_along_axis(x, index, axis=1, mode="promise_in_bounds")


def split(x):
    hi = x.astype(BF16)
    return hi, (x - hi.astype(F32)).astype(BF16)


def dot3(a_hi, a_lo, x):
    x_hi, x_lo = split(x)
    out = jnp.dot(a_hi, x_hi, preferred_element_type=F32)
    out += jnp.dot(a_hi, x_lo, preferred_element_type=F32)
    return out + jnp.dot(a_lo, x_hi, preferred_element_type=F32)


def iota(shape, axis):
    return lax.broadcasted_iota(jnp.int32, shape, axis)


def matrices(sz, flux, volume_operator):
    V, Q, face = sz.V, sz.Q, sz.face

    def body(flux_ref, vol_ref, in_hi, in_lo, out_hi, out_lo):
        p = iota((Q, Q), 0)
        q = iota((Q, Q), 1)
        same = p == q
        low = same & (p < face)
        up = same & (p >= Q - face)
        slide = same & (p % 4 == 3)
        fp = iota((Q, face), 0)
        fq = iota((Q, face), 1)
        to_low = fp == fq
        to_up = fp == fq + (Q - face)
        to_slide = fp == 4 * fq + 3
        vol0 = vol_ref[0]
        vol1 = vol_ref[1]
        for v in range(V):
            blocks = []
            lows, ups, slides = [], [], []
            for w in range(V):
                f0 = flux_ref[0, v, w]
                f1 = flux_ref[1, v, w]
                d = DISSIPATION if v == w else 0.0
                a_low = 0.5 * LIFT * (-f0 - d)
                a_up = 0.5 * LIFT * (f0 - d)
                a_slide = 0.5 * LIFT * (f1 - d)
                block = f0 * vol0 + f1 * vol1
                block -= jnp.where(low, a_low, 0.0)
                block -= jnp.where(up, a_up, 0.0)
                block -= jnp.where(slide, a_slide, 0.0)
                blocks.append(block)
                lows.append(jnp.where(to_low, a_low, 0.0))
                ups.append(jnp.where(to_up, a_up, 0.0))
                slides.append(jnp.where(to_slide, a_slide, 0.0))
            hi, lo = split(jnp.concatenate(blocks, axis=1))
            in_hi[pl.ds(v * Q, Q), :] = hi
            in_lo[pl.ds(v * Q, Q), :] = lo
            hi, lo = split(jnp.concatenate(lows + ups + slides, axis=1))
            out_hi[pl.ds(v * Q, Q), :] = hi
            out_lo[pl.ds(v * Q, Q), :] = lo

    inner = jax.ShapeDtypeStruct((sz.R, sz.R), BF16)
    outer = jax.ShapeDtypeStruct((sz.R, 3 * sz.FR), BF16)
    nbytes = 4 * sz.R * (sz.R + 3 * sz.FR)
    return call(body, [inner, inner, outer, outer], [SMEM, VMEM], (), nbytes, nbytes)(flux, volume_operator)


def pack_shapes(sz):
    tm = [jax.ShapeDtypeStruct((sz.L, sz.RC, sz.E), F32) for _ in range(sz.M)]
    zz = [jax.ShapeDtypeStruct((sz.z_rows(j), sz.E), F32) for j in range(sz.Z)]
    return tm + zz


def pack_scratch(sz):
    return [pltpu.VMEM((sz.Z, sz.CH, sz.E), F32)]


def pack(sz, where, u_ref, outs, stage):
    tm, zz = outs[: sz.M], outs[sz.M :]
    me, z = where[0], where[1]
    for j in range(sz.M):
        start = pl.multiple_of((me ^ j) * sz.RC, SUB)
        tm[j][...] = u_ref[:, pl.ds(start, sz.RC), :]
    for p in range(sz.Z):
        first = (p % sz.PL) * sz.CH
        stage[p] = u_ref[p // sz.PL, pl.ds(3 + 4 * first, sz.CH, stride=4), :]
    lane = iota((SUB, sz.E), 1)
    slot = lane // REACH
    last = sz.E - REACH + lane % REACH
    first = lane % REACH
    tiles = sz.face // SUB
    halos = []
    for l in range(sz.L):
        up = jnp.zeros((SUB, sz.E), F32)
        low = jnp.zeros((SUB, sz.E), F32)
        for k in range(sz.FR // SUB):
            row = (k // tiles) * sz.Q + (k % tiles) * SUB
            up = jnp.where(slot == k, lanes_of(u_ref[l, pl.ds(row + sz.Q - sz.face, SUB), :], last), up)
            low = jnp.where(slot == k, lanes_of(u_ref[l, pl.ds(row, SUB), :], first), low)
        halos.append((up, low))
    for j in range(sz.Z):
        at = 0
        for which, wanted in ((0, j in (0, 1)), (1, j in (0, sz.Z - 1))):
            if wanted:
                for l in range(sz.L):
                    zz[j][pl.ds(at, SUB), :] = halos[l][which]
                    at += SUB
        zz[j][pl.ds(at, sz.CH), :] = stage[lax.rem(z + j, sz.Z)]


def first_pack(sz, where, u):
    def body(where_ref, u_ref, *refs):
        pack(sz, where_ref, u_ref, refs[:-1], refs[-1])

    shapes = pack_shapes(sz)
    return call(body, shapes, [SMEM, VMEM], pack_scratch(sz), 0, 12 * sz.L * sz.R * sz.E)(where, u)


def inside(sz, in_hi, in_lo, u):
    pair = 2

    def body(hi_ref, lo_ref, u_ref, out_ref):
        for l in range(0, sz.L, pair):
            x = jnp.concatenate([u_ref[l + i] for i in range(pair)], axis=1)
            r = dot3(hi_ref[...], lo_ref[...], x)
            for i in range(pair):
                out_ref[l + i] = r[:, i * sz.E : (i + 1) * sz.E]

    out = jax.ShapeDtypeStruct(u.shape, F32)
    flops = 6 * sz.R * sz.R * sz.L * sz.E
    return call(body, [out], [VMEM] * 3, (), flops, 12 * u.size)(in_hi, in_lo, u)[0]


def turn_time(sz, where, parts):
    weights = [float(w) for w in time_weights(sz.T)]
    T, L, M = sz.T, sz.L, sz.M

    def body(where_ref, *refs):
        ins, outs, x_ref, y_ref = refs[:M], refs[M : 2 * M], refs[-2], refs[-1]
        me = where_ref[0]
        for j in range(M):
            x_ref[pl.ds((me ^ j) * L, L)] = ins[j][...]

        def rows(i, carry):
            at = pl.ds(pl.multiple_of(i * SUB, SUB), SUB)
            x = [x_ref[t, at, :] for t in range(T)]
            diff = {}
            for t in range(T):
                for k in range(1, T // 2):
                    a, b = (t + k) % T, (t - k) % T
                    if (b, a) not in diff:
                        diff[(a, b)] = x[a] - x[b]
            for t in range(T):
                total = None
                for k in range(1, T // 2):
                    a, b = (t + k) % T, (t - k) % T
                    term = weights[k] * diff[(a, b)] if (a, b) in diff else -weights[k] * diff[(b, a)]
                    total = term if total is None else total + term
                y_ref[t, at, :] = total
            return carry

        lax.fori_loop(0, sz.RC // SUB, rows, 0)
        for j in range(M):
            outs[j][...] = y_ref[pl.ds((me ^ j) * L, L)]

    shape = jax.ShapeDtypeStruct((L, sz.RC, sz.E), F32)
    full = pltpu.VMEM((T, sz.RC, sz.E), F32)
    size = T * sz.RC * sz.E
    return call(body, [shape] * M, [SMEM] + [VMEM] * M, [full, full], 20 * size, 8 * size)(where, *parts)


def shift_slide(sz, where, mine, theirs):
    Z, N, CH, E = sz.Z, sz.N, sz.CH, sz.E

    def body(where_ref, *refs):
        a, b, outs, x_ref = refs[:Z], refs[Z : 2 * Z], refs[2 * Z : 3 * Z], refs[-1]
        z, core = where_ref[1], where_ref[2]
        l = z // sz.PL
        group, shift = where_ref[3 + l], where_ref[3 + sz.L + l]
        for j in range(Z):
            chip = lax.rem(z + Z - j, Z)
            skip = sz.z_rows(j) - CH
            x_ref[2 * chip + core] = a[j][pl.ds(skip, CH), :]
            x_ref[2 * chip + 1 - core] = b[j][pl.ds(skip, CH), :]
        lane = iota((CH, E), 1)
        index = (lane + shift) % E
        for j in range(Z):
            block = 2 * lax.rem(z + j, Z) + core
            near = x_ref[lax.rem(block + group, N)]
            far = x_ref[lax.rem(block + group + 1, N)]
            outs[j][...] = lanes_of(jnp.where(lane < shift, far, near), index)

    out = jax.ShapeDtypeStruct((CH, E), F32)
    ins = [SMEM] + [VMEM] * (2 * Z)
    scratch = [pltpu.VMEM((N, CH, E), F32)]
    return call(body, [out] * Z, ins, scratch, 0, 12 * N * CH * E)(where, *mine, *theirs)


def finish(sz, last, where, angle, gaps, out_hi, out_lo, u, ins_part, times, slides, own, sibling, ahead, behind):
    L, E, R, FR, Q, face = sz.L, sz.E, sz.R, sz.FR, sz.Q, sz.face
    n_next = 0 if last else sz.M + sz.Z

    def body(where_ref, angle_ref, gaps_ref, hi_ref, lo_ref, u_ref, w_ref, *refs):
        time_refs, refs = refs[: sz.M], refs[sz.M :]
        slide_refs, refs = refs[: sz.Z], refs[sz.Z :]
        own_ref, sib_ref, ahead_ref, behind_ref = refs[:4]
        refs = refs[4:]
        new_ref, refs = refs[0], refs[1:]
        if last:
            res_ref, refs = refs[0], refs[1:]
        packs, refs = refs[:n_next], refs[n_next:]
        t_ref, s_ref, x_ref = refs[:3]
        me, z, core = where_ref[0], where_ref[1], where_ref[2]
        for j in range(sz.M):
            t_ref[:, pl.ds(pl.multiple_of((me ^ j) * sz.RC, SUB), sz.RC), :] = time_refs[j][...]
        for j in range(sz.Z):
            s_ref[lax.rem(z + sz.Z - j, sz.Z)] = slide_refs[j][...]
        lane = iota((SUB, E), 1)
        back = jnp.broadcast_to(gaps_ref[0:1, :], (SUB, E))
        front = jnp.broadcast_to(gaps_ref[1:2, :], (SUB, E))
        own_back = (lane + E - back) % E
        own_front = (lane + front) % E
        from_back = lane < back
        from_front = lane >= E - front
        first_core = core == 0
        tiles = face // SUB
        for l in range(L):
            prev_halo = jnp.where(first_core, behind_ref[pl.ds(l * SUB, SUB), :], sib_ref[pl.ds(l * SUB, SUB), :])
            next_halo = jnp.where(
                first_core, sib_ref[pl.ds(sz.H + l * SUB, SUB), :], ahead_ref[pl.ds(l * SUB, SUB), :]
            )
            for k in range(FR // SUB):
                row = (k // tiles) * Q + (k % tiles) * SUB
                here = lanes_of(u_ref[l, pl.ds(row + Q - face, SUB), :], own_back)
                there = lanes_of(prev_halo, (REACH * k + REACH + lane + E - back) % E)
                x_ref[pl.ds(k * SUB, SUB), pl.ds(l * E, E)] = jnp.where(from_back, there, here)
                here = lanes_of(u_ref[l, pl.ds(row, SUB), :], own_front)
                there = lanes_of(next_halo, (REACH * k + lane + front) % E)
                x_ref[pl.ds(FR + k * SUB, SUB), pl.ds(l * E, E)] = jnp.where(from_front, there, here)
            slide = [s_ref[l * sz.PL + i] for i in range(sz.PL)]
            slide = slide[0] if sz.PL == 1 else jnp.concatenate(slide, axis=0)
            x_ref[pl.ds(2 * FR, FR), pl.ds(l * E, E)] = slide
            v1 = slide[face : 2 * face]
            v2 = slide[2 * face : 3 * face]
            cosine, sine = angle_ref[0, l], angle_ref[1, l]
            x_ref[pl.ds(2 * FR + face, face), pl.ds(l * E, E)] = cosine * v1 - sine * v2
            x_ref[pl.ds(2 * FR + 2 * face, face), pl.ds(l * E, E)] = sine * v1 + cosine * v2
        pair = 2
        for l in range(0, L, pair):
            outer = dot3(hi_ref[...], lo_ref[...], x_ref[:, pl.ds(l * E, pair * E)])
            for i in range(pair):
                r = outer[:, i * E : (i + 1) * E] + w_ref[l + i] + t_ref[l + i]
                new_ref[l + i] = u_ref[l + i] - STEP * r
                if last:
                    res_ref[l + i] = r
        if not last:
            pack(sz, where_ref, new_ref, packs, refs[3])

    outs = [jax.ShapeDtypeStruct(u.shape, F32)]
    outs += [jax.ShapeDtypeStruct(u.shape, F32)] if last else pack_shapes(sz)
    scratch = [
        pltpu.VMEM((L, R, E), F32),
        pltpu.VMEM((sz.Z, sz.CH, E), F32),
        pltpu.VMEM((3 * FR, L * E), F32),
    ]
    if not last:
        scratch += pack_scratch(sz)
    ins = [SMEM, SMEM] + [VMEM] * (5 + sz.M + sz.Z + 4)
    args = (where, angle, gaps, out_hi, out_lo, u, ins_part, *times, *slides, own, sibling, ahead, behind)
    return call(body, outs, ins, scratch, 6 * R * 3 * FR * L * E, 24 * u.size)(*args)


def over_tm(x, j):
    size = lax.axis_size("tm")
    return lax.ppermute(x, "tm", [(i, i ^ j) for i in range(size)])


def over_chips(x, j):
    size = lax.axis_size("space")
    return lax.ppermute(x, "space", [(i, (i + 2 * j) % size) for i in range(size)])


def over_cores(x):
    size = lax.axis_size("space")
    return lax.ppermute(x, "space", [(i, i ^ 1) for i in range(size)])


def per_device(conserved_field, face_neighbours, counterpart_group, counterpart_shift, volume_operator, flux_matrix):
    sz = Sizes(conserved_field.shape)
    me = lax.axis_index("tm")
    s = lax.axis_index("space")
    where = jnp.concatenate([jnp.stack([me, s // 2, s % 2]), counterpart_group, counterpart_shift]).astype(jnp.int32)
    cycle = me * sz.L + jnp.arange(sz.L, dtype=jnp.int32)
    azimuth = 2.0 * jnp.pi * cycle.astype(F32) / sz.T
    angle = jnp.stack([jnp.cos(azimuth), jnp.sin(azimuth)])
    index = s * sz.E + jnp.arange(sz.E, dtype=jnp.int32)
    total = sz.E * sz.N
    gaps = jnp.stack([(index - face_neighbours[0]) % total, (face_neighbours[1] - index) % total])
    u = conserved_field.reshape(sz.L, sz.R, sz.E)
    in_hi, in_lo, out_hi, out_lo = matrices(sz, flux_matrix, volume_operator)
    packed = first_pack(sz, where, u)
    for sweep in range(ITERS):
        last = sweep == ITERS - 1
        tm, zz = packed[: sz.M], packed[sz.M :]
        parts = [tm[0]] + [over_tm(tm[j], j) for j in range(1, sz.M)]
        mine = [zz[0]] + [over_chips(zz[j], j) for j in range(1, sz.Z)]
        theirs = [over_cores(x) for x in mine]
        ins_part = inside(sz, in_hi, in_lo, u)
        times = turn_time(sz, where, parts)
        times = [times[0]] + [over_tm(times[j], j) for j in range(1, sz.M)]
        slides = shift_slide(sz, where, mine, theirs)
        slides = [slides[0]] + [over_chips(slides[j], j) for j in range(1, sz.Z)]
        done = finish(
            sz, last, where, angle, gaps, out_hi, out_lo, u, ins_part, times, slides,
            mine[0], theirs[0], theirs[sz.Z - 1], theirs[1],
        )
        u, packed = done[0], done[1:]
    shape = conserved_field.shape
    return u.reshape(shape), packed[0].reshape(shape)


def solution(mesh):
    return jax.shard_map(
        per_device,
        mesh=mesh,
        in_specs=(P("tm", None, None, "space"), P(None, "space"), P("tm"), P("tm"), P(), P()),
        out_specs=(P("tm", None, None, "space"), P("tm", None, None, "space")),
        check_vma=False,
    )
```

time: 178 us -> 93 us (0.52)
  the two profiles are of different devices: /device:TPU:1 before, /device:TPU:0 now
where the time goes in v1:
time: 93 us; the launch traced here: 92.7 us
  waiting for transfers between devices  39.1 us (42%)
  starting transfers between devices  28.2 us (30%)
  Pallas kernels  20.2 us (22%)
  local copies, waits for them, and re-layouts  2.92 us (3%)
  other arithmetic  1.36 us (1%)
    ppermute x12, waiting for transfers between devices, over_chips(): lax.ppermute(x, 'space', [(i, (i + 2 * j) % size) for i in range(size)])  26.9 us
    ppermute x12, starting transfers between devices, over_tm(): return lax.ppermute(x, 'tm', [(i, i ^ j) for i in range(size)])  16.5 us
    ppermute x12, waiting for transfers between devices, over_tm(): return lax.ppermute(x, 'tm', [(i, i ^ j) for i in range(size)])  11.2 us
    ppermute x12, starting transfers between devices, over_chips(): lax.ppermute(x, 'space', [(i, (i + 2 * j) % size) for i in range(size)])  10.6 us
    pallas_call x2, Pallas kernels, finish(): call(body, outs, ins, scratch, 6 * R * 3 * FR * L * E, 24 * u.size)(*args)  6.87 us
    pallas_call x1, Pallas kernels, matrices(): call(body, [inner, inner, outer, outer], [SMEM, VMEM], (), nbytes, nbytes)  3.52 us
    pallas_call x2, Pallas kernels, inside(): call(body, [out], [VMEM] * 3, (), flops, 12 * u.size)(in_hi, in_lo, u)[0]  3.43 us
    pallas_call x2, Pallas kernels, turn_time(): call(body, [shape] * M, [SMEM] + [VMEM] * M, [full, full], 20 * size, 8 *...  3.28 us
  transfers between devices with their start and end apart: 32, of which 14 were waited for; matrix products, arithmetic and copies ran while one was open for 1% of the time, Pallas kernels for 13%

profile of v1, /device:TPU:0, one launch (start us, length us, event | category | flops | bytes accessed | tf_op | source)
XLA Modules:
  0.0 92.7 jit_solution(17681020649157508607)
XLA Ops:
  0.7 0.7 concatenate.3.where_ref
  1.4 1.3 %copy-done = f32[4,10,64,128]{3,2,1,0:T(8,128)S(1)} copy-done((f32[4,10,64,128]{3,2,1,0:T(8,128)S(1)}, f32[4,10,64,128]{3,2,1,0:T(8,128)}, u32[]{:S(2)}) %copy-start) | copy-done | bytes 1310744
  2.7 1.6 %shard_map.79 = (f32[4,160,128]{2,1,0:T(8,128)S(1)}, f32[4,160,128]{2,1,0:T(8,128)}, f32[4,160,128]{2,1,0:T(8,128)}, f32[4,160,128]{2,1,0:T(8,128)S(1)}, f32[224...) custom-call(s32[11]{0:T(128)S(1)} %concatenate.3.where_ref, ...), custom_call_target="tpu_custom_call" | custom-call | bytes 3932160 | tf_op jit(solution)/shard_map/pallas_call | solution.py:182
  4.3 4.0 %collective-permute-start.7 = (f32[160,128]{1,0:T(8,128)S(1)}, f32[160,128]{1,0:T(8,128)S(1)}, u32[]{:S(2)}, u32[]{:S(2)}) collective-permute-start(f32[160,128]{1,0:T(8,128)S(1)} %get-tuple-element.55), channel_id=1, source_target_pairs={{0,4},{1,5},{2,6},{3,7},{4,0},{5,1},{6,2},{7,3},{8,12},{9,13},{10,... | collective-permute-start | bytes 245768 | tf_op jit(solution)/shard_map/ppermute | solution.py:346
  8.4 1.6 %collective-permute-start.6 = (f32[192,128]{1,0:T(8,128)S(1)}, f32[192,128]{1,0:T(8,128)S(1)}, u32[]{:S(2)}, u32[]{:S(2)}) collective-permute-start(f32[192,128]{1,0:T(8,128)S(1)} %get-tuple-element.54), channel_id=1, source_target_pairs={{0,2},{1,3},{2,4},{3,5},{4,6},{5,7},{6,0},{7,1},{8,10},{9,11},{10,... | collective-permute-start | bytes 294920 | tf_op jit(solution)/shard_map/ppermute | solution.py:346
  10.0 2.2 %collective-permute-start.8 = (f32[192,128]{1,0:T(8,128)S(1)}, f32[192,128]{1,0:T(8,128)S(1)}, u32[]{:S(2)}, u32[]{:S(2)}) collective-permute-start(f32[192,128]{1,0:T(8,128)S(1)} %get-tuple-element.56), channel_id=1, source_target_pairs={{0,6},{1,7},{2,0},{3,1},{4,2},{5,3},{6,4},{7,5},{8,14},{9,15},{10,... | collective-permute-start | bytes 294920 | tf_op jit(solution)/shard_map/ppermute | solution.py:346
  12.2 1.5 %collective-permute-start = (f32[4,160,128]{2,1,0:T(8,128)}, f32[4,160,128]{2,1,0:T(8,128)S(1)}, u32[]{:S(2)}, u32[]{:S(2)}) collective-permute-start(f32[4,160,128]{2,1,0:T(8,128)} %get-tuple-element.46), channel_id=1, source_target_pairs={{0,8},{8,0},{16,24},{24,16},{1,9},{9,1},{17,25},{25,17},{2,10},{10... | collective-permute-start | bytes 983048 | tf_op jit(solution)/shard_map/ppermute | solution.py:341
  13.7 1.5 %collective-permute-start.1 = (f32[4,160,128]{2,1,0:T(8,128)}, f32[4,160,128]{2,1,0:T(8,128)S(1)}, u32[]{:S(2)}, u32[]{:S(2)}) collective-permute-start(f32[4,160,128]{2,1,0:T(8,128)} %get-tuple-element.47), channel_id=1, source_target_pairs={{0,16},{8,24},{16,0},{24,8},{1,17},{9,25},{17,1},{25,9},{2,18},{10... | collective-permute-start | bytes 983048 | tf_op jit(solution)/shard_map/ppermute | solution.py:341
  15.2 0.0 collective-permute-done.7.refs_2_
  15.2 2.8 %collective-permute-start.2 = (f32[4,160,128]{2,1,0:T(8,128)S(1)}, f32[4,160,128]{2,1,0:T(8,128)S(1)}, u32[]{:S(2)}, u32[]{:S(2)}) collective-permute-start(f32[4,160,128]{2,1,0:T(8,128)S(1)} %get-tuple-element.48), channel_id=1, source_target_pairs={{0,24},{8,16},{16,8},{24,0},{1,25},{9,17},{17,9},{25,1},{2,26},{10... | collective-permute-start | bytes 983048 | tf_op jit(solution)/shard_map/ppermute | solution.py:341
  18.0 1.3 %and_select_fusion.1 = (s32[1,128]{1,0:T(1,128)}, s32[1,128]{1,0:T(1,128)}) fusion(s32[2,128]{1,0:T(2,128)} %param.7, s32[]{:T(128)S(6)} %mul.8), kind=kLoop, calls=%fused_computation.5 | loop fusion | flops 3200 | bytes 2052 | tf_op jit(solution)/shard_map/jit(remainder)/select_n | solution.py:364
  19.3 0.8 copy-done.2
  20.2 3.5 %shard_map.77 = (bf16[640,640]{1,0:T(8,128)(2,1)S(1)}, bf16[640,640]{1,0:T(8,128)(2,1)S(1)}, bf16[640,480]{1,0:T(8,128)(2,1)S(1)}, bf16[640,480]{1,0:T(8,128)(2,1)S(1)}) custom-call(f32[2,10,10]{2,1,0:T(8,128)S(1)} %copy.8.flux_ref, f32[2,64,64]{2,1,0:T(8,128)S(1)} %copy-done.2), custom_call_target="tpu_custom_call" | custom-call | flops 2867200 | bytes 2867200 | tf_op jit(solution)/shard_map/pallas_call | solution.py:131
  23.7 0.0 collective-permute-done.6.refs_1_
  23.7 0.1 collective-permute-start.9
  23.8 0.0 collective-permute-done.8.refs_3_
  23.8 0.5 collective-permute-start.11
  24.3 1.7 %shard_map.78.w_ref = f32[4,640,128]{2,1,0:T(8,128)S(1)} custom-call(bf16[640,640]{1,0:T(8,128)(2,1)S(1)} %get-tuple-element.43.hi_ref, bf16[640,640]{1,0:T(8,128)(2,1)S(1)} %get-tuple-element.44.lo_ref, f32[4,640,128]{2,1,0:T(8,128)S(1)} %bitcast.7), custom_call_target="tpu_custom_call" | custom-call | flops 1258291200 | bytes 3932160 | tf_op jit(solution)/shard_map/pallas_call | solution.py:197
  26.0 0.0 collective-permute-done.refs_1_
  26.0 0.1 collective-permute-start.10
  26.2 3.1 %collective-permute-done.1.refs_2_ = f32[4,160,128]{2,1,0:T(8,128)S(1)} collective-permute-done((f32[4,160,128]{2,1,0:T(8,128)}, f32[4,160,128]{2,1,0:T(8,128)S(1)}, u32[]{:S(2)}, u32[]{:S(2)}) %collective-permute-start.1) | collective-permute-done | bytes 327712 | tf_op jit(solution)/shard_map/ppermute | solution.py:341
  29.3 0.0 collective-permute-start.12
  29.3 0.0 collective-permute-done.2.refs_3_
  29.3 1.6 %shard_map.80 = (f32[4,160,128]{2,1,0:T(8,128)S(1)}, f32[4,160,128]{2,1,0:T(8,128)S(1)}, f32[4,160,128]{2,1,0:T(8,128)S(1)}, f32[4,160,128]{2,1,0:T(8,128)S(1)}) custom-call(s32[11]{0:T(128)S(1)} %concatenate.3.where_ref, f32[4,160,128]{2,1,0:T(8,128)S(1)} %get-tuple-element.45.refs_0_, f32[4,160,128]{2,1,0:T(8,128)S(1)} %collective-permute-done.refs_1_, ...), custom_call_target="tpu_custom_call" | custom-call | flops 6553600 | bytes 2621440 | tf_op jit(solution)/shard_map/pallas_call | solution.py:235
  30.9 1.3 %collective-permute-start.3 = (f32[4,160,128]{2,1,0:T(8,128)S(1)}, f32[4,160,128]{2,1,0:T(8,128)S(1)}, u32[]{:S(2)}, u32[]{:S(2)}) collective-permute-start(f32[4,160,128]{2,1,0:T(8,128)S(1)} %get-tuple-element.50), channel_id=1, source_target_pairs={{0,8},{8,0},{16,24},{24,16},{1,9},{9,1},{17,25},{25,17},{2,10},{10... | collective-permute-start | bytes 983048 | tf_op jit(solution)/shard_map/ppermute | solution.py:341
  32.2 0.8 collective-permute-start.4
  33.1 1.4 %collective-permute-start.5 = (f32[4,160,128]{2,1,0:T(8,128)S(1)}, f32[4,160,128]{2,1,0:T(8,128)S(1)}, u32[]{:S(2)}, u32[]{:S(2)}) collective-permute-start(f32[4,160,128]{2,1,0:T(8,128)S(1)} %get-tuple-element.52), channel_id=1, source_target_pairs={{0,24},{8,16},{16,8},{24,0},{1,25},{9,17},{17,9},{25,1},{2,26},{10... | collective-permute-start | bytes 983048 | tf_op jit(solution)/shard_map/ppermute | solution.py:341
  34.5 0.0 collective-permute-done.10.refs_5_.refs_11_
  34.5 0.0 collective-permute-done.12.refs_7_.refs_10_
  34.5 0.8 shard_map.81
  35.3 0.1 collective-permute-start.13
  35.4 0.9 collective-permute-start.14
  36.3 6.2 %collective-permute-done.13.refs_5_ = f32[160,128]{1,0:T(8,128)S(1)} collective-permute-done((f32[160,128]{1,0:T(8,128)S(1)}, f32[160,128]{1,0:T(8,128)S(1)}, u32[]{:S(2)}, u32[]{:S(2)}) %collective-permute-start.13) | collective-permute-done | bytes 81952 | tf_op jit(solution)/shard_map/ppermute | solution.py:346
  42.5 2.2 %collective-permute-done.14.refs_6_ = f32[160,128]{1,0:T(8,128)S(1)} collective-permute-done((f32[160,128]{1,0:T(8,128)S(1)}, f32[160,128]{1,0:T(8,128)S(1)}, u32[]{:S(2)}, u32[]{:S(2)}) %collective-permute-start.14) | collective-permute-done | bytes 81952 | tf_op jit(solution)/shard_map/ppermute | solution.py:346
  44.8 2.2 %collective-permute-done.15.refs_7_ = f32[160,128]{1,0:T(8,128)S(1)} collective-permute-done((f32[160,128]{1,0:T(8,128)S(1)}, f32[160,128]{1,0:T(8,128)S(1)}, u32[]{:S(2)}, u32[]{:S(2)}) %collective-permute-start.15) | collective-permute-done | bytes 81952 | tf_op jit(solution)/shard_map/ppermute | solution.py:346
  47.0 0.5 collective-permute-done.4.refs_2_
  47.5 1.6 %collective-permute-done.5.refs_3_ = f32[4,160,128]{2,1,0:T(8,128)S(1)} collective-permute-done((f32[4,160,128]{2,1,0:T(8,128)S(1)}, f32[4,160,128]{2,1,0:T(8,128)S(1)}, u32[]{:S(2)}, u32[]{:S(2)}) %collective-permute-start.5) | collective-permute-done | bytes 327712 | tf_op jit(solution)/shard_map/ppermute | solution.py:341
  49.1 2.8 %shard_map.82 = (f32[4,640,128]{2,1,0:T(8,128)S(1)}, f32[4,160,128]{2,1,0:T(8,128)S(1)}, f32[4,160,128]{2,1,0:T(8,128)S(1)}, f32[4,160,128]{2,1,0:T(8,128)S(1)},...) custom-call(s32[11]{0:T(128)S(1)} %concatenate.3.where_ref, ...), custom_call_target="tpu_custom_call" | custom-call | flops 943718400 | bytes 7864320 | tf_op jit(solution)/shard_map/pallas_call | solution.py:336
  51.9 0.9 collective-permute-start.16
  52.8 1.5 %collective-permute-start.17 = (f32[4,160,128]{2,1,0:T(8,128)S(1)}, f32[4,160,128]{2,1,0:T(8,128)S(1)}, u32[]{:S(2)}, u32[]{:S(2)}) collective-permute-start(f32[4,160,128]{2,1,0:T(8,128)S(1)} %get-tuple-element.64), channel_id=1, source_target_pairs={{0,16},{8,24},{16,0},{24,8},{1,17},{9,25},{17,1},{25,9},{2,18},{10... | collective-permute-start | bytes 983048 | tf_op jit(solution)/shard_map/ppermute | solution.py:341
  54.3 1.2 %collective-permute-start.18 = (f32[4,160,128]{2,1,0:T(8,128)S(1)}, f32[4,160,128]{2,1,0:T(8,128)S(1)}, u32[]{:S(2)}, u32[]{:S(2)}) collective-permute-start(f32[4,160,128]{2,1,0:T(8,128)S(1)} %get-tuple-element.65), channel_id=1, source_target_pairs={{0,24},{8,16},{16,8},{24,0},{1,25},{9,17},{17,9},{25,1},{2,26},{10... | collective-permute-start | bytes 983048 | tf_op jit(solution)/shard_map/ppermute | solution.py:341
  55.5 0.0 collective-permute-start.23
  55.5 0.8 collective-permute-start.22
  56.3 7.2 %collective-permute-done.23.refs_2_ = f32[160,128]{1,0:T(8,128)S(1)} collective-permute-done((f32[160,128]{1,0:T(8,128)S(1)}, f32[160,128]{1,0:T(8,128)S(1)}, u32[]{:S(2)}, u32[]{:S(2)}) %collective-permute-start.23) | collective-permute-done | bytes 81952 | tf_op jit(solution)/shard_map/ppermute | solution.py:346
  63.5 0.0 collective-permute-start.24
  63.6 5.1 %collective-permute-done.17.refs_2_ = f32[4,160,128]{2,1,0:T(8,128)S(1)} collective-permute-done((f32[4,160,128]{2,1,0:T(8,128)S(1)}, f32[4,160,128]{2,1,0:T(8,128)S(1)}, u32[]{:S(2)}, u32[]{:S(2)}) %collective-permute-start.17) | collective-permute-done | bytes 327712 | tf_op jit(solution)/shard_map/ppermute | solution.py:341
  68.7 1.6 %shard_map.84 = (f32[4,160,128]{2,1,0:T(8,128)S(1)}, f32[4,160,128]{2,1,0:T(8,128)S(1)}, f32[4,160,128]{2,1,0:T(8,128)S(1)}, f32[4,160,128]{2,1,0:T(8,128)S(1)}) custom-call(s32[11]{0:T(128)S(1)} %concatenate.3.where_ref, f32[4,160,128]{2,1,0:T(8,128)S(1)} %get-tuple-element.62.refs_0_, f32[4,160,128]{2,1,0:T(8,128)S(1)} %collective-permute-done.16.refs_1_, ...), custom_call_target="tpu_custom_call" | custom-call | flops 6553600 | bytes 2621440 | tf_op jit(solution)/shard_map/pallas_call | solution.py:235
  70.3 1.5 %collective-permute-start.19 = (f32[4,160,128]{2,1,0:T(8,128)S(1)}, f32[4,160,128]{2,1,0:T(8,128)S(1)}, u32[]{:S(2)}, u32[]{:S(2)}) collective-permute-start(f32[4,160,128]{2,1,0:T(8,128)S(1)} %get-tuple-element.67), channel_id=1, source_target_pairs={{0,8},{8,0},{16,24},{24,16},{1,9},{9,1},{17,25},{25,17},{2,10},{10... | collective-permute-start | bytes 983048 | tf_op jit(solution)/shard_map/ppermute | solution.py:341
  71.8 0.6 collective-permute-start.20
  72.4 0.0 collective-permute-done.24.refs_3_
  72.4 1.5 %collective-permute-start.21 = (f32[4,160,128]{2,1,0:T(8,128)S(1)}, f32[4,160,128]{2,1,0:T(8,128)S(1)}, u32[]{:S(2)}, u32[]{:S(2)}) collective-permute-start(f32[4,160,128]{2,1,0:T(8,128)S(1)} %get-tuple-element.69), channel_id=1, source_target_pairs={{0,24},{8,16},{16,8},{24,0},{1,25},{9,17},{17,9},{25,1},{2,26},{10... | collective-permute-start | bytes 983048 | tf_op jit(solution)/shard_map/ppermute | solution.py:341
  73.9 0.5 collective-permute-start.28
  74.4 0.8 collective-permute-done.26.refs_5_.refs_11_
  75.2 0.2 collective-permute-done.28.refs_7_.refs_10_
  75.3 0.7 shard_map.85
  76.1 0.1 collective-permute-start.29
  76.2 0.8 collective-permute-start.30
  77.0 6.3 %collective-permute-done.29.refs_5_ = f32[160,128]{1,0:T(8,128)S(1)} collective-permute-done((f32[160,128]{1,0:T(8,128)S(1)}, f32[160,128]{1,0:T(8,128)S(1)}, u32[]{:S(2)}, u32[]{:S(2)}) %collective-permute-start.29) | collective-permute-done | bytes 81952 | tf_op jit(solution)/shard_map/ppermute | solution.py:346
  83.3 0.0 collective-permute-start.31
  83.3 1.7 %shard_map.83.w_ref = f32[4,640,128]{2,1,0:T(8,128)S(1)} custom-call(bf16[640,640]{1,0:T(8,128)(2,1)S(1)} %get-tuple-element.43.hi_ref, bf16[640,640]{1,0:T(8,128)(2,1)S(1)} %get-tuple-element.44.lo_ref, f32[4,640,128]{2,1,0:T(8,128)S(1)} %get-tuple-element.61.u_ref), custom_call_target="tpu_custom_call" | custom-call | flops 1258291200 | bytes 3932160 | tf_op jit(solution)/shard_map/pallas_call | solution.py:197
  85.0 0.9 collective-permute-done.30.refs_6_
  85.9 1.8 %collective-permute-done.31.refs_7_ = f32[160,128]{1,0:T(8,128)S(1)} collective-permute-done((f32[160,128]{1,0:T(8,128)S(1)}, f32[160,128]{1,0:T(8,128)S(1)}, u32[]{:S(2)}, u32[]{:S(2)}) %collective-permute-start.31) | collective-permute-done | bytes 81952 | tf_op jit(solution)/shard_map/ppermute | solution.py:346
  87.8 0.9 collective-permute-done.20.refs_2_
  88.7 4.0 %shard_map.86 = (f32[4,640,128]{2,1,0:T(8,128)}, f32[4,640,128]{2,1,0:T(8,128)}) custom-call(s32[11]{0:T(128)S(1)} %concatenate.3.where_ref, f32[2,4]{1,0:T(2,128)S(1)} %pad_maximum_fusion.angle_ref, s32[2,128]{1,0:T(2,128)S(1)} %pad_add_fusion.gaps_ref, bf16[640,480]{1,0:T(8,128)(2,1)S(1)} %get-tuple-element.41.hi_ref, ...), custom_call_target="tpu_custom_call" | custom-call | flops 943718400 | bytes 7864320 | tf_op jit(solution)/shard_map/pallas_call | solution.py:336
  (28 shorter events, 0.1 us)
Async XLA Ops:
  0.6 18.7 %copy-start.3 = (f32[2,10,10]{2,0,1:T(2,128)S(1)}, f32[2,10,10]{2,0,1:T(2,128)}, u32[]{:S(2)}) copy-start(f32[2,10,10]{2,0,1:T(2,128)} %param.11) | copy-start | bytes 2404
  1.4 1.3 %copy-start = (f32[4,10,64,128]{3,2,1,0:T(8,128)S(1)}, f32[4,10,64,128]{3,2,1,0:T(8,128)}, u32[]{:S(2)}) copy-start(f32[4,10,64,128]{3,2,1,0:T(8,128)} %param.6) | copy-start | bytes 3932164
  2.7 21.6 %copy-start.1 = (f32[4,10,64,128]{3,2,1,0:T(8,128)S(1)}, f32[4,10,64,128]{3,2,1,0:T(8,128)}, u32[]{:S(2)}) copy-start(f32[4,10,64,128]{3,2,1,0:T(8,128)} %param.6) | copy-start | bytes 3932164
  4.3 10.9 %collective-permute-start.7 = (f32[160,128]{1,0:T(8,128)S(1)}, f32[160,128]{1,0:T(8,128)S(1)}, u32[]{:S(2)}, u32[]{:S(2)}) collective-permute-start(f32[160,128]{1,0:T(8,128)S(1)} %get-tuple-element.55), channel_id=1, source_target_pairs={{0,4},{1,5},{2,6},{3,7},{4,0},{5,1},{6,2},{7,3},{8,12},{9,13},{10,... | collective-permute-start | bytes 245768 | tf_op jit(solution)/shard_map/ppermute | solution.py:346
  8.4 15.3 %collective-permute-start.6 = (f32[192,128]{1,0:T(8,128)S(1)}, f32[192,128]{1,0:T(8,128)S(1)}, u32[]{:S(2)}, u32[]{:S(2)}) collective-permute-start(f32[192,128]{1,0:T(8,128)S(1)} %get-tuple-element.54), channel_id=1, source_target_pairs={{0,2},{1,3},{2,4},{3,5},{4,6},{5,7},{6,0},{7,1},{8,10},{9,11},{10,... | collective-permute-start | bytes 294920 | tf_op jit(solution)/shard_map/ppermute | solution.py:346
  10.0 13.8 %collective-permute-start.8 = (f32[192,128]{1,0:T(8,128)S(1)}, f32[192,128]{1,0:T(8,128)S(1)}, u32[]{:S(2)}, u32[]{:S(2)}) collective-permute-start(f32[192,128]{1,0:T(8,128)S(1)} %get-tuple-element.56), channel_id=1, source_target_pairs={{0,6},{1,7},{2,0},{3,1},{4,2},{5,3},{6,4},{7,5},{8,14},{9,15},{10,... | collective-permute-start | bytes 294920 | tf_op jit(solution)/shard_map/ppermute | solution.py:346
  12.2 13.8 %collective-permute-start = (f32[4,160,128]{2,1,0:T(8,128)}, f32[4,160,128]{2,1,0:T(8,128)S(1)}, u32[]{:S(2)}, u32[]{:S(2)}) collective-permute-start(f32[4,160,128]{2,1,0:T(8,128)} %get-tuple-element.46), channel_id=1, source_target_pairs={{0,8},{8,0},{16,24},{24,16},{1,9},{9,1},{17,25},{25,17},{2,10},{10... | collective-permute-start | bytes 983048 | tf_op jit(solution)/shard_map/ppermute | solution.py:341
  13.7 15.6 %collective-permute-start.1 = (f32[4,160,128]{2,1,0:T(8,128)}, f32[4,160,128]{2,1,0:T(8,128)S(1)}, u32[]{:S(2)}, u32[]{:S(2)}) collective-permute-start(f32[4,160,128]{2,1,0:T(8,128)} %get-tuple-element.47), channel_id=1, source_target_pairs={{0,16},{8,24},{16,0},{24,8},{1,17},{9,25},{17,1},{25,9},{2,18},{10... | collective-permute-start | bytes 983048 | tf_op jit(solution)/shard_map/ppermute | solution.py:341
  15.2 14.0 %collective-permute-start.2 = (f32[4,160,128]{2,1,0:T(8,128)S(1)}, f32[4,160,128]{2,1,0:T(8,128)S(1)}, u32[]{:S(2)}, u32[]{:S(2)}) collective-permute-start(f32[4,160,128]{2,1,0:T(8,128)S(1)} %get-tuple-element.48), channel_id=1, source_target_pairs={{0,24},{8,16},{16,8},{24,0},{1,25},{9,17},{17,9},{25,1},{2,26},{10... | collective-permute-start | bytes 983048 | tf_op jit(solution)/shard_map/ppermute | solution.py:341
  19.3 0.8 copy-start.2
  23.7 8.5 %collective-permute-start.9 = (f32[224,128]{1,0:T(8,128)S(1)}, f32[224,128]{1,0:T(8,128)S(1)}, u32[]{:S(2)}, u32[]{:S(2)}) collective-permute-start(f32[224,128]{1,0:T(8,128)S(1)} %get-tuple-element.53.refs_0_.refs_8_), channel_id=1, source_target_pairs={{0,1},{1,0},{2,3},{3,2},{4,5},{5,4},{6,7},{7,6},{8,9},{9,8},{10,11... | collective-permute-start | bytes 344072 | tf_op jit(solution)/shard_map/ppermute | solution.py:351
  23.8 9.3 %collective-permute-start.11 = (f32[160,128]{1,0:T(8,128)S(1)}, f32[160,128]{1,0:T(8,128)S(1)}, u32[]{:S(2)}, u32[]{:S(2)}) collective-permute-start(f32[160,128]{1,0:T(8,128)S(1)} %collective-permute-done.7.refs_2_), channel_id=1, source_target_pairs={{0,1},{1,0},{2,3},{3,2},{4,5},{5,4},{6,7},{7,6},{8,9},{9,8},{10,11... | collective-permute-start | bytes 245768 | tf_op jit(solution)/shard_map/ppermute | solution.py:351
  26.0 9.4 %copy-start.4 = (s32[1,128]{1,0:T(1,128)S(1)}, s32[1,128]{1,0:T(1,128)}, u32[]{:S(2)}) copy-start(s32[1,128]{1,0:T(1,128)} %get-tuple-element.80) | copy-start | bytes 1540
  26.0 9.4 %copy-start.5 = (s32[1,128]{1,0:T(1,128)S(1)}, s32[1,128]{1,0:T(1,128)}, u32[]{:S(2)}) copy-start(s32[1,128]{1,0:T(1,128)} %get-tuple-element.81) | copy-start | bytes 1540
  26.0 8.5 %collective-permute-start.10 = (f32[192,128]{1,0:T(8,128)S(1)}, f32[192,128]{1,0:T(8,128)S(1)}, u32[]{:S(2)}, u32[]{:S(2)}) collective-permute-start(f32[192,128]{1,0:T(8,128)S(1)} %collective-permute-done.6.refs_1_), channel_id=1, source_target_pairs={{0,1},{1,0},{2,3},{3,2},{4,5},{5,4},{6,7},{7,6},{8,9},{9,8},{10,11... | collective-permute-start | bytes 294920 | tf_op jit(solution)/shard_map/ppermute | solution.py:351
  29.3 5.3 %collective-permute-start.12 = (f32[192,128]{1,0:T(8,128)S(1)}, f32[192,128]{1,0:T(8,128)S(1)}, u32[]{:S(2)}, u32[]{:S(2)}) collective-permute-start(f32[192,128]{1,0:T(8,128)S(1)} %collective-permute-done.8.refs_3_), channel_id=1, source_target_pairs={{0,1},{1,0},{2,3},{3,2},{4,5},{5,4},{6,7},{7,6},{8,9},{9,8},{10,11... | collective-permute-start | bytes 294920 | tf_op jit(solution)/shard_map/ppermute | solution.py:351
  30.9 16.1 %collective-permute-start.3 = (f32[4,160,128]{2,1,0:T(8,128)S(1)}, f32[4,160,128]{2,1,0:T(8,128)S(1)}, u32[]{:S(2)}, u32[]{:S(2)}) collective-permute-start(f32[4,160,128]{2,1,0:T(8,128)S(1)} %get-tuple-element.50), channel_id=1, source_target_pairs={{0,8},{8,0},{16,24},{24,16},{1,9},{9,1},{17,25},{25,17},{2,10},{10... | collective-permute-start | bytes 983048 | tf_op jit(solution)/shard_map/ppermute | solution.py:341
  32.2 15.2 %collective-permute-start.4 = (f32[4,160,128]{2,1,0:T(8,128)S(1)}, f32[4,160,128]{2,1,0:T(8,128)S(1)}, u32[]{:S(2)}, u32[]{:S(2)}) collective-permute-start(f32[4,160,128]{2,1,0:T(8,128)S(1)} %get-tuple-element.51), channel_id=1, source_target_pairs={{0,16},{8,24},{16,0},{24,8},{1,17},{9,25},{17,1},{25,9},{2,18},{10... | collective-permute-start | bytes 983048 | tf_op jit(solution)/shard_map/ppermute | solution.py:341
  33.1 16.0 %collective-permute-start.5 = (f32[4,160,128]{2,1,0:T(8,128)S(1)}, f32[4,160,128]{2,1,0:T(8,128)S(1)}, u32[]{:S(2)}, u32[]{:S(2)}) collective-permute-start(f32[4,160,128]{2,1,0:T(8,128)S(1)} %get-tuple-element.52), channel_id=1, source_target_pairs={{0,24},{8,16},{16,8},{24,0},{1,25},{9,17},{17,9},{25,1},{2,26},{10... | collective-permute-start | bytes 983048 | tf_op jit(solution)/shard_map/ppermute | solution.py:341
  35.3 7.2 %collective-permute-start.13 = (f32[160,128]{1,0:T(8,128)S(1)}, f32[160,128]{1,0:T(8,128)S(1)}, u32[]{:S(2)}, u32[]{:S(2)}) collective-permute-start(f32[160,128]{1,0:T(8,128)S(1)} %get-tuple-element.58), channel_id=1, source_target_pairs={{0,2},{1,3},{2,4},{3,5},{4,6},{5,7},{6,0},{7,1},{8,10},{9,11},{10,... | collective-permute-start | bytes 245768 | tf_op jit(solution)/shard_map/ppermute | solution.py:346
  35.4 9.4 %collective-permute-start.14 = (f32[160,128]{1,0:T(8,128)S(1)}, f32[160,128]{1,0:T(8,128)S(1)}, u32[]{:S(2)}, u32[]{:S(2)}) collective-permute-start(f32[160,128]{1,0:T(8,128)S(1)} %get-tuple-element.59), channel_id=1, source_target_pairs={{0,4},{1,5},{2,6},{3,7},{4,0},{5,1},{6,2},{7,3},{8,12},{9,13},{10,... | collective-permute-start | bytes 245768 | tf_op jit(solution)/shard_map/ppermute | solution.py:346
  42.5 4.4 %collective-permute-start.15 = (f32[160,128]{1,0:T(8,128)S(1)}, f32[160,128]{1,0:T(8,128)S(1)}, u32[]{:S(2)}, u32[]{:S(2)}) collective-permute-start(f32[160,128]{1,0:T(8,128)S(1)} %get-tuple-element.60), channel_id=1, source_target_pairs={{0,6},{1,7},{2,0},{3,1},{4,2},{5,3},{6,4},{7,5},{8,14},{9,15},{10,... | collective-permute-start | bytes 245768 | tf_op jit(solution)/shard_map/ppermute | solution.py:346
  51.9 11.6 %collective-permute-start.16 = (f32[4,160,128]{2,1,0:T(8,128)S(1)}, f32[4,160,128]{2,1,0:T(8,128)S(1)}, u32[]{:S(2)}, u32[]{:S(2)}) collective-permute-start(f32[4,160,128]{2,1,0:T(8,128)S(1)} %get-tuple-element.63), channel_id=1, source_target_pairs={{0,8},{8,0},{16,24},{24,16},{1,9},{9,1},{17,25},{25,17},{2,10},{10... | collective-permute-start | bytes 983048 | tf_op jit(solution)/shard_map/ppermute | solution.py:341
  52.8 15.9 %collective-permute-start.17 = (f32[4,160,128]{2,1,0:T(8,128)S(1)}, f32[4,160,128]{2,1,0:T(8,128)S(1)}, u32[]{:S(2)}, u32[]{:S(2)}) collective-permute-start(f32[4,160,128]{2,1,0:T(8,128)S(1)} %get-tuple-element.64), channel_id=1, source_target_pairs={{0,16},{8,24},{16,0},{24,8},{1,17},{9,25},{17,1},{25,9},{2,18},{10... | collective-permute-start | bytes 983048 | tf_op jit(solution)/shard_map/ppermute | solution.py:341
  54.3 14.4 %collective-permute-start.18 = (f32[4,160,128]{2,1,0:T(8,128)S(1)}, f32[4,160,128]{2,1,0:T(8,128)S(1)}, u32[]{:S(2)}, u32[]{:S(2)}) collective-permute-start(f32[4,160,128]{2,1,0:T(8,128)S(1)} %get-tuple-element.65), channel_id=1, source_target_pairs={{0,24},{8,16},{16,8},{24,0},{1,25},{9,17},{17,9},{25,1},{2,26},{10... | collective-permute-start | bytes 983048 | tf_op jit(solution)/shard_map/ppermute | solution.py:341
  55.5 8.1 %collective-permute-start.23 = (f32[160,128]{1,0:T(8,128)S(1)}, f32[160,128]{1,0:T(8,128)S(1)}, u32[]{:S(2)}, u32[]{:S(2)}) collective-permute-start(f32[160,128]{1,0:T(8,128)S(1)} %get-tuple-element.72), channel_id=1, source_target_pairs={{0,4},{1,5},{2,6},{3,7},{4,0},{5,1},{6,2},{7,3},{8,12},{9,13},{10,... | collective-permute-start | bytes 245768 | tf_op jit(solution)/shard_map/ppermute | solution.py:346
  55.5 16.3 %collective-permute-start.22 = (f32[192,128]{1,0:T(8,128)S(1)}, f32[192,128]{1,0:T(8,128)S(1)}, u32[]{:S(2)}, u32[]{:S(2)}) collective-permute-start(f32[192,128]{1,0:T(8,128)S(1)} %get-tuple-element.71), channel_id=1, source_target_pairs={{0,2},{1,3},{2,4},{3,5},{4,6},{5,7},{6,0},{7,1},{8,10},{9,11},{10,... | collective-permute-start | bytes 294920 | tf_op jit(solution)/shard_map/ppermute | solution.py:346
  63.5 8.8 %collective-permute-start.24 = (f32[192,128]{1,0:T(8,128)S(1)}, f32[192,128]{1,0:T(8,128)S(1)}, u32[]{:S(2)}, u32[]{:S(2)}) collective-permute-start(f32[192,128]{1,0:T(8,128)S(1)} %get-tuple-element.73), channel_id=1, source_target_pairs={{0,6},{1,7},{2,0},{3,1},{4,2},{5,3},{6,4},{7,5},{8,14},{9,15},{10,... | collective-permute-start | bytes 294920 | tf_op jit(solution)/shard_map/ppermute | solution.py:346
  63.5 10.3 %collective-permute-start.25 = (f32[224,128]{1,0:T(8,128)S(1)}, f32[224,128]{1,0:T(8,128)S(1)}, u32[]{:S(2)}, u32[]{:S(2)}) collective-permute-start(f32[224,128]{1,0:T(8,128)S(1)} %get-tuple-element.70.refs_0_.refs_8_), channel_id=1, source_target_pairs={{0,1},{1,0},{2,3},{3,2},{4,5},{5,4},{6,7},{7,6},{8,9},{9,8},{10,11... | collective-permute-start | bytes 344072 | tf_op jit(solution)/shard_map/ppermute | solution.py:351
  68.7 5.2 %collective-permute-start.27 = (f32[160,128]{1,0:T(8,128)S(1)}, f32[160,128]{1,0:T(8,128)S(1)}, u32[]{:S(2)}, u32[]{:S(2)}) collective-permute-start(f32[160,128]{1,0:T(8,128)S(1)} %collective-permute-done.23.refs_2_), channel_id=1, source_target_pairs={{0,1},{1,0},{2,3},{3,2},{4,5},{5,4},{6,7},{7,6},{8,9},{9,8},{10,11... | collective-permute-start | bytes 245768 | tf_op jit(solution)/shard_map/ppermute | solution.py:351
  70.3 17.5 %collective-permute-start.19 = (f32[4,160,128]{2,1,0:T(8,128)S(1)}, f32[4,160,128]{2,1,0:T(8,128)S(1)}, u32[]{:S(2)}, u32[]{:S(2)}) collective-permute-start(f32[4,160,128]{2,1,0:T(8,128)S(1)} %get-tuple-element.67), channel_id=1, source_target_pairs={{0,8},{8,0},{16,24},{24,16},{1,9},{9,1},{17,25},{25,17},{2,10},{10... | collective-permute-start | bytes 983048 | tf_op jit(solution)/shard_map/ppermute | solution.py:341
  71.8 16.9 %collective-permute-start.20 = (f32[4,160,128]{2,1,0:T(8,128)S(1)}, f32[4,160,128]{2,1,0:T(8,128)S(1)}, u32[]{:S(2)}, u32[]{:S(2)}) collective-permute-start(f32[4,160,128]{2,1,0:T(8,128)S(1)} %get-tuple-element.68), channel_id=1, source_target_pairs={{0,16},{8,24},{16,0},{24,8},{1,17},{9,25},{17,1},{25,9},{2,18},{10... | collective-permute-start | bytes 983048 | tf_op jit(solution)/shard_map/ppermute | solution.py:341
  72.4 16.3 %collective-permute-start.21 = (f32[4,160,128]{2,1,0:T(8,128)S(1)}, f32[4,160,128]{2,1,0:T(8,128)S(1)}, u32[]{:S(2)}, u32[]{:S(2)}) collective-permute-start(f32[4,160,128]{2,1,0:T(8,128)S(1)} %get-tuple-element.69), channel_id=1, source_target_pairs={{0,24},{8,16},{16,8},{24,0},{1,25},{9,17},{17,9},{25,1},{2,26},{10... | collective-permute-start | bytes 983048 | tf_op jit(solution)/shard_map/ppermute | solution.py:341
  73.9 1.3 %collective-permute-start.26 = (f32[192,128]{1,0:T(8,128)S(1)}, f32[192,128]{1,0:T(8,128)S(1)}, u32[]{:S(2)}, u32[]{:S(2)}) collective-permute-start(f32[192,128]{1,0:T(8,128)S(1)} %collective-permute-done.22.refs_1_), channel_id=1, source_target_pairs={{0,1},{1,0},{2,3},{3,2},{4,5},{5,4},{6,7},{7,6},{8,9},{9,8},{10,11... | collective-permute-start | bytes 294920 | tf_op jit(solution)/shard_map/ppermute | solution.py:351
  73.9 1.5 %collective-permute-start.28 = (f32[192,128]{1,0:T(8,128)S(1)}, f32[192,128]{1,0:T(8,128)S(1)}, u32[]{:S(2)}, u32[]{:S(2)}) collective-permute-start(f32[192,128]{1,0:T(8,128)S(1)} %collective-permute-done.24.refs_3_), channel_id=1, source_target_pairs={{0,1},{1,0},{2,3},{3,2},{4,5},{5,4},{6,7},{7,6},{8,9},{9,8},{10,11... | collective-permute-start | bytes 294920 | tf_op jit(solution)/shard_map/ppermute | solution.py:351
  76.1 7.2 %collective-permute-start.29 = (f32[160,128]{1,0:T(8,128)S(1)}, f32[160,128]{1,0:T(8,128)S(1)}, u32[]{:S(2)}, u32[]{:S(2)}) collective-permute-start(f32[160,128]{1,0:T(8,128)S(1)} %get-tuple-element.75), channel_id=1, source_target_pairs={{0,2},{1,3},{2,4},{3,5},{4,6},{5,7},{6,0},{7,1},{8,10},{9,11},{10,... | collective-permute-start | bytes 245768 | tf_op jit(solution)/shard_map/ppermute | solution.py:346
  76.2 9.8 %collective-permute-start.30 = (f32[160,128]{1,0:T(8,128)S(1)}, f32[160,128]{1,0:T(8,128)S(1)}, u32[]{:S(2)}, u32[]{:S(2)}) collective-permute-start(f32[160,128]{1,0:T(8,128)S(1)} %get-tuple-element.76), channel_id=1, source_target_pairs={{0,4},{1,5},{2,6},{3,7},{4,0},{5,1},{6,2},{7,3},{8,12},{9,13},{10,... | collective-permute-start | bytes 245768 | tf_op jit(solution)/shard_map/ppermute | solution.py:346
  83.3 4.4 %collective-permute-start.31 = (f32[160,128]{1,0:T(8,128)S(1)}, f32[160,128]{1,0:T(8,128)S(1)}, u32[]{:S(2)}, u32[]{:S(2)}) collective-permute-start(f32[160,128]{1,0:T(8,128)S(1)} %get-tuple-element.77), channel_id=1, source_target_pairs={{0,6},{1,7},{2,0},{3,1},{4,2},{5,3},{6,4},{7,5},{8,14},{9,15},{10,... | collective-permute-start | bytes 245768 | tf_op jit(solution)/shard_map/ppermute | solution.py:346

commit v2 on v1

v2 whole, which is shorter than its diff:
```python
import functools

import jax
import jax.numpy as jnp
import numpy as np
from jax import lax
from jax.experimental import pallas as pl
from jax.experimental.pallas import tpu as pltpu
from jax.sharding import PartitionSpec as P

REACH = 4
LIFT = 2.0
DISSIPATION = 1.5
ANGULAR = 0.5
DAMPING = 4.0
STEP = 0.2
SUB = 8

VMEM = pl.BlockSpec(memory_space=pltpu.VMEM)
SMEM = pl.BlockSpec(memory_space=pltpu.SMEM)
F32 = jnp.float32
BF16 = jnp.bfloat16


class Sizes:
    def __init__(self, field_shape):
        self.L, self.V, self.Q, self.E = field_shape
        self.R = self.V * self.Q
        self.M = lax.axis_size("tm")
        self.N = lax.axis_size("space")
        self.T = self.L * self.M
        self.Z = self.N // 2
        self.RC = self.R // self.M
        self.face = self.Q // 4
        self.FR = self.V * self.face
        self.PL = self.Z // self.L
        self.CH = self.FR // self.PL
        self.H = SUB * self.L

    def z_rows(self, j):
        if j == 0:
            return 2 * self.H + self.CH
        return self.CH + self.H * ((j == 1) + (j == self.Z - 1))


def time_weights(total):
    k = np.arange(1, total // 2, dtype=np.float64)
    gains = 2.0 * ANGULAR * k * np.exp(-DAMPING * (k / (total // 2)) ** 8) / total
    lag = np.arange(total, dtype=np.float64)
    return np.sum(gains[:, None] * np.sin(2.0 * np.pi * k[:, None] * lag[None, :] / total), axis=0)


def call(body, outs, ins, scratch=(), flops=0, nbytes=0):
    return pl.pallas_call(
        body,
        out_shape=outs,
        in_specs=ins,
        out_specs=jax.tree.map(lambda _: VMEM, outs),
        scratch_shapes=list(scratch),
        cost_estimate=pl.CostEstimate(flops=flops, bytes_accessed=nbytes, transcendentals=0),
        compiler_params=pltpu.CompilerParams(vmem_limit_bytes=16 * 1024 * 1024),
    )


def spot():
    s = lax.axis_index("space")
    return lax.axis_index("tm"), s // 2, lax.rem(s, 2)


def turn_of(sz, l):
    me = lax.axis_index("tm")
    cosine, sine = jnp.float32(1.0), jnp.float32(0.0)
    for m in range(sz.M):
        azimuth = 2.0 * np.pi * (m * sz.L + l) / sz.T
        cosine = jnp.where(me == m, jnp.float32(np.cos(azimuth)), cosine)
        sine = jnp.where(me == m, jnp.float32(np.sin(azimuth)), sine)
    return cosine, sine


def lanes_of(x, index):
    return jnp.take_along_axis(x, index, axis=1, mode="promise_in_bounds")


def split(x):
    hi = x.astype(BF16)
    return hi, (x - hi.astype(F32)).astype(BF16)


def dot3(a_hi, a_lo, x):
    x_hi, x_lo = split(x)
    out = jnp.dot(a_hi, x_hi, preferred_element_type=F32)
    out += jnp.dot(a_hi, x_lo, preferred_element_type=F32)
    return out + jnp.dot(a_lo, x_hi, preferred_element_type=F32)


def iota(shape, axis):
    return lax.broadcasted_iota(jnp.int32, shape, axis)


def matrices(sz, flux, volume_operator):
    V, Q, face = sz.V, sz.Q, sz.face

    def body(flux_ref, vol_ref, in_hi, in_lo, out_hi, out_lo):
        p = iota((Q, Q), 0)
        q = iota((Q, Q), 1)
        same = p == q
        low = same & (p < face)
        up = same & (p >= Q - face)
        slide = same & (p % 4 == 3)
        fp = iota((Q, face), 0)
        fq = iota((Q, face), 1)
        to_low = fp == fq
        to_up = fp == fq + (Q - face)
        to_slide = fp == 4 * fq + 3
        vol0 = vol_ref[0]
        vol1 = vol_ref[1]
        for v in range(V):
            blocks = []
            lows, ups, slides = [], [], []
            for w in range(V):
                f0 = flux_ref[0, v, w]
                f1 = flux_ref[1, v, w]
                d = DISSIPATION if v == w else 0.0
                a_low = 0.5 * LIFT * (-f0 - d)
                a_up = 0.5 * LIFT * (f0 - d)
                a_slide = 0.5 * LIFT * (f1 - d)
                block = f0 * vol0 + f1 * vol1
                block -= jnp.where(low, a_low, 0.0)
                block -= jnp.where(up, a_up, 0.0)
                block -= jnp.where(slide, a_slide, 0.0)
                blocks.append(block)
                lows.append(jnp.where(to_low, a_low, 0.0))
                ups.append(jnp.where(to_up, a_up, 0.0))
                slides.append(jnp.where(to_slide, a_slide, 0.0))
            hi, lo = split(jnp.concatenate(blocks, axis=1))
            in_hi[pl.ds(v * Q, Q), :] = hi
            in_lo[pl.ds(v * Q, Q), :] = lo
            hi, lo = split(jnp.concatenate(lows + ups + slides, axis=1))
            out_hi[pl.ds(v * Q, Q), :] = hi
            out_lo[pl.ds(v * Q, Q), :] = lo

    inner = jax.ShapeDtypeStruct((sz.R, sz.R), BF16)
    outer = jax.ShapeDtypeStruct((sz.R, 3 * sz.FR), BF16)
    nbytes = 4 * sz.R * (sz.R + 3 * sz.FR)
    return call(body, [inner, inner, outer, outer], [SMEM, VMEM], (), nbytes, nbytes)(flux, volume_operator)


def tm_shapes(sz, rows):
    return [jax.ShapeDtypeStruct((sz.L, rows, sz.E), F32) for _ in range(sz.M)]


def chip_shapes(sz):
    return [jax.ShapeDtypeStruct((sz.z_rows(j), sz.E), F32) for j in range(sz.Z)]


def pack_time(sz, u):
    def body(u_ref, *refs):
        outs, sems = refs[: sz.M], refs[-1]
        me = lax.axis_index("tm")
        copies = []
        for j in list(range(1, sz.M)) + [0]:
            start = pl.multiple_of((me ^ j) * sz.RC, SUB)
            copies.append(pltpu.make_async_copy(u_ref.at[:, pl.ds(start, sz.RC), :], outs[j], sems.at[j]))
            copies[-1].start()
        for copy in copies:
            copy.wait()

    scratch = [pltpu.SemaphoreType.DMA((sz.M,))]
    source = pl.BlockSpec(memory_space=pltpu.HBM)
    return call(body, tm_shapes(sz, sz.RC), [source], scratch, 0, 8 * u.size)(u)


def chip_scratch(sz):
    return pltpu.VMEM((sz.Z, sz.CH, sz.E), F32)


def pack_chips(sz, slide_ref, halo_ref, zz, stage):
    z = spot()[1]
    for p in range(sz.Z):
        first = (p % sz.PL) * sz.CH
        stage[p] = slide_ref[p // sz.PL, pl.ds(3 + 4 * first, sz.CH, stride=4), :]
    lane = iota((SUB, sz.E), 1)
    slot = lane // REACH
    last = sz.E - REACH + lane % REACH
    first = lane % REACH
    tiles = sz.face // SUB
    halos = []
    for l in range(sz.L):
        up = jnp.zeros((SUB, sz.E), F32)
        low = jnp.zeros((SUB, sz.E), F32)
        for k in range(sz.FR // SUB):
            row = (k // tiles) * sz.Q + (k % tiles) * SUB
            up = jnp.where(slot == k, lanes_of(halo_ref[l, pl.ds(row + sz.Q - sz.face, SUB), :], last), up)
            low = jnp.where(slot == k, lanes_of(halo_ref[l, pl.ds(row, SUB), :], first), low)
        halos.append((up, low))
    for j in range(sz.Z):
        at = 0
        for which, wanted in ((0, j in (0, 1)), (1, j in (0, sz.Z - 1))):
            if wanted:
                for l in range(sz.L):
                    zz[j][pl.ds(at, SUB), :] = halos[l][which]
                    at += SUB
        zz[j][pl.ds(at, sz.CH), :] = stage[lax.rem(z + j, sz.Z)]


def pack_space(sz, u):
    def body(u_ref, *refs):
        held, sem = refs[-2], refs[-1]
        copy = pltpu.make_async_copy(u_ref, held, sem)
        copy.start()
        copy.wait()
        pack_chips(sz, held, held, refs[:-3], refs[-3])

    scratch = [chip_scratch(sz), pltpu.VMEM(u.shape, F32), pltpu.SemaphoreType.DMA]
    source = pl.BlockSpec(memory_space=pltpu.HBM)
    return call(body, chip_shapes(sz), [source], scratch, 0, 4 * u.size)(u)


def inside_part(sz, mats, u):
    E, pair = sz.E, 2

    def body(hi_ref, lo_ref, u_ref, out_ref):
        for l in range(0, sz.L, pair):
            x = jnp.concatenate([u_ref[l + i] for i in range(pair)], axis=1)
            r = dot3(hi_ref[...], lo_ref[...], x)
            for i in range(pair):
                out_ref[l + i] = r[:, i * E : (i + 1) * E]

    out = jax.ShapeDtypeStruct(u.shape, F32)
    return call(body, [out], [VMEM] * 3, (), 6 * sz.R * u.size, 12 * u.size)(*mats[:2], u)[0]


def face_part(sz, neighbours, mats, u, inner, own, sibling, ahead, behind):
    L, E, FR, Q, face = sz.L, sz.E, sz.FR, sz.Q, sz.face
    pair = 2

    def body(near_ref, ohi_ref, olo_ref, u_ref, in_ref, sib_ref, ahead_ref, behind_ref, out_ref, x_ref):
        core = spot()[2]
        lane = iota((SUB, E), 1)
        index = lax.axis_index("space") * E + lane
        total = sz.N * E
        back = index - jnp.broadcast_to(near_ref[0:1, :], (SUB, E))
        back = jnp.where(back < 0, back + total, back)
        front = jnp.broadcast_to(near_ref[1:2, :], (SUB, E)) - index
        front = jnp.where(front < 0, front + total, front)
        own_back = (lane + E - back) % E
        own_front = (lane + front) % E
        from_back = lane < back
        from_front = lane >= E - front
        first_core = core == 0
        tiles = face // SUB
        for l in range(L):
            prev_halo = jnp.where(first_core, behind_ref[pl.ds(l * SUB, SUB), :], sib_ref[pl.ds(l * SUB, SUB), :])
            next_halo = jnp.where(
                first_core, sib_ref[pl.ds(sz.H + l * SUB, SUB), :], ahead_ref[pl.ds(l * SUB, SUB), :]
            )
            for k in range(FR // SUB):
                row = (k // tiles) * Q + (k % tiles) * SUB
                here = lanes_of(u_ref[l, pl.ds(row + Q - face, SUB), :], own_back)
                there = lanes_of(prev_halo, (REACH * k + REACH + lane + E - back) % E)
                x_ref[pl.ds(k * SUB, SUB), pl.ds(l * E, E)] = jnp.where(from_back, there, here)
                here = lanes_of(u_ref[l, pl.ds(row, SUB), :], own_front)
                there = lanes_of(next_halo, (REACH * k + lane + front) % E)
                x_ref[pl.ds(FR + k * SUB, SUB), pl.ds(l * E, E)] = jnp.where(from_front, there, here)
        for l in range(0, L, pair):
            x = x_ref[:, pl.ds(l * E, pair * E)]
            r = dot3(ohi_ref[:, : 2 * FR], olo_ref[:, : 2 * FR], x)
            for i in range(pair):
                out_ref[l + i] = in_ref[l + i] + r[:, i * E : (i + 1) * E]

    out = jax.ShapeDtypeStruct(u.shape, F32)
    flops = 12 * sz.R * FR * L * E
    ins = [VMEM] * 8
    scratch = [pltpu.VMEM((2 * FR, L * E), F32)]
    args = (neighbours, *mats[2:], u, inner, sibling, ahead, behind)
    return call(body, [out], ins, scratch, flops, 12 * u.size)(*args)[0]


def turn_time(sz, parts, damp=False, carried=()):
    weights = [float(w) for w in time_weights(sz.T)]
    T, L, M = sz.T, sz.L, sz.M
    rows = parts[0].shape[1]
    padded = -(-rows // SUB) * SUB
    front = carried[0].shape[1] if carried else 0

    def body(*refs):
        ins, fronts, outs, x_ref, y_ref = refs[:M], refs[M : M + len(carried)], refs[-2 - M : -2], refs[-2], refs[-1]
        me = spot()[0]
        for j in range(len(carried)):
            outs[j][:, pl.ds(0, front), :] = fronts[j][...]
        for j in range(M):
            x_ref[pl.ds((me ^ j) * L, L), pl.ds(0, rows), :] = ins[j][...]

        def some(i, carry):
            at = pl.ds(pl.multiple_of(i * SUB, SUB), SUB)
            x = [x_ref[t, at, :] for t in range(T)]
            diff = {}
            for t in range(T):
                total = None
                for k in range(1, T // 2):
                    a, b = (t + k) % T, (t - k) % T
                    if (a, b) not in diff and (b, a) not in diff:
                        diff[(a, b)] = x[a] - x[b]
                    term = weights[k] * diff[(a, b)] if (a, b) in diff else -weights[k] * diff[(b, a)]
                    total = term if total is None else total + term
                y_ref[t, at, :] = x[t] - STEP * total if damp else total
            return carry

        lax.fori_loop(0, padded // SUB, some, 0)
        for j in range(M):
            outs[j][:, pl.ds(front, rows), :] = y_ref[pl.ds((me ^ j) * L, L), pl.ds(0, rows), :]

    full = pltpu.VMEM((T, padded, sz.E), F32)
    size = T * rows * sz.E
    ins = [VMEM] * (M + len(carried))
    shapes = tm_shapes(sz, front + rows)
    return call(body, shapes, ins, [full, full], 20 * size, 8 * size)(*parts, *carried)


def shift_slide(sz, groups, shifts, mine, theirs):
    Z, N, CH, E = sz.Z, sz.N, sz.CH, sz.E

    def body(group_ref, shift_ref, *refs):
        a, b, outs, x_ref = refs[:Z], refs[Z : 2 * Z], refs[2 * Z : 3 * Z], refs[-1]
        _, z, core = spot()
        l = z // sz.PL
        group, shift = group_ref[l], shift_ref[l]
        for j in range(Z):
            chip = lax.rem(z + Z - j, Z)
            skip = sz.z_rows(j) - CH
            x_ref[2 * chip + core] = a[j][pl.ds(skip, CH), :]
            x_ref[2 * chip + 1 - core] = b[j][pl.ds(skip, CH), :]
        lane = iota((CH, E), 1)
        index = (lane + shift) % E
        for j in range(Z):
            block = 2 * lax.rem(z + j, Z) + core
            near = x_ref[lax.rem(block + group, N)]
            far = x_ref[lax.rem(block + group + 1, N)]
            outs[j][...] = lanes_of(jnp.where(lane < shift, far, near), index)

    out = jax.ShapeDtypeStruct((CH, E), F32)
    ins = [SMEM, SMEM] + [VMEM] * (2 * Z)
    scratch = [pltpu.VMEM((N, CH, E), F32)]
    return call(body, [out] * Z, ins, scratch, 0, 12 * N * CH * E)(groups, shifts, *mine, *theirs)


def slide_rows(sz, slides, stage, x_ref):
    E, face, FR = sz.E, sz.face, sz.FR
    z = spot()[1]
    for j in range(sz.Z):
        stage[lax.rem(z + sz.Z - j, sz.Z)] = slides[j][...]
    for l in range(sz.L):
        slide = [stage[l * sz.PL + i] for i in range(sz.PL)]
        slide = slide[0] if sz.PL == 1 else jnp.concatenate(slide, axis=0)
        cols = pl.ds(l * E, E)
        x_ref[:, cols] = slide
        v1 = slide[face : 2 * face]
        v2 = slide[2 * face : 3 * face]
        cosine, sine = turn_of(sz, l)
        x_ref[pl.ds(face, face), cols] = cosine * v1 - sine * v2
        x_ref[pl.ds(2 * face, face), cols] = sine * v1 + cosine * v2


def gather_rows(sz, parts, full):
    me = spot()[0]
    for j in range(sz.M):
        full[:, pl.ds(pl.multiple_of((me ^ j) * sz.RC, SUB), sz.RC), :] = parts[j][...]


def first_slide(sz, mats, u, local, slides):
    L, E, R, FR, M = sz.L, sz.E, sz.R, sz.FR, sz.M
    CR = FR // M
    pair = 2

    def body(ohi_ref, olo_ref, u_ref, w_ref, *refs):
        slide_refs, out_ref, chunks = refs[: sz.Z], refs[sz.Z], refs[sz.Z + 1 : sz.Z + 1 + M]
        stage, x_ref, cut_ref = refs[-3:]
        slide_rows(sz, slide_refs, stage, x_ref)
        for l in range(L):
            for m in range(M):
                cut_ref[m, l] = x_ref[pl.ds(m * CR, CR), pl.ds(l * E, E)]
        for j in range(M):
            chunks[j][...] = cut_ref[spot()[0] ^ j]
        for l in range(0, L, pair):
            outer = dot3(ohi_ref[:, 2 * FR :], olo_ref[:, 2 * FR :], x_ref[:, pl.ds(l * E, pair * E)])
            for i in range(pair):
                out_ref[l + i] = u_ref[l + i] - STEP * (w_ref[l + i] + outer[:, i * E : (i + 1) * E])

    outs = [jax.ShapeDtypeStruct(u.shape, F32)] + tm_shapes(sz, CR)
    scratch = [chip_scratch(sz), pltpu.VMEM((FR, L * E), F32), pltpu.VMEM((M, L, CR, E), F32)]
    ins = [VMEM] * (4 + sz.Z)
    done = call(body, outs, ins, scratch, 6 * R * FR * L * E, 12 * u.size)(*mats[2:], u, local, *slides)
    return done[0], done[1:]


def first_step(sz, partial, times):
    def body(c_ref, *refs):
        time_refs, u_ref, v_ref = refs[: sz.M], refs[sz.M], refs[sz.M + 1]
        zz, t_ref, stage = refs[sz.M + 2 : -2], refs[-2], refs[-1]
        gather_rows(sz, time_refs, t_ref)
        for l in range(sz.L):
            t = STEP * t_ref[l]
            new = c_ref[l] - t
            u_ref[l] = new
            v_ref[l] = new - t
        pack_chips(sz, u_ref, v_ref, zz, stage)

    full = jax.ShapeDtypeStruct(partial.shape, F32)
    scratch = [pltpu.VMEM(partial.shape, F32), chip_scratch(sz)]
    ins = [VMEM] * (1 + sz.M)
    done = call(body, [full, full] + chip_shapes(sz), ins, scratch, 0, 16 * partial.size)(partial, *times)
    return done[0], done[1], done[2:]


def last_step(sz, mats, u, local, times, slides):
    L, E, R, FR, M = sz.L, sz.E, sz.R, sz.FR, sz.M
    CR = FR // M
    pair = 2

    def body(ohi_ref, olo_ref, u_ref, w_ref, *refs):
        time_refs, refs = refs[:M], refs[M:]
        slide_refs, refs = refs[: sz.Z], refs[sz.Z :]
        new_ref, res_ref, t_ref, stage, x_ref, cut_ref = refs
        me = spot()[0]
        for j in range(M):
            t_ref[me ^ j] = time_refs[j][:, pl.ds(0, sz.RC), :]
            cut_ref[me ^ j] = time_refs[j][:, pl.ds(sz.RC, CR), :]
        slide_rows(sz, slide_refs, stage, x_ref)
        for l in range(L):
            for m in range(M):
                x_ref[pl.ds(m * CR, CR), pl.ds(l * E, E)] -= STEP * cut_ref[m, l]
        for l in range(0, L, pair):
            outer = dot3(ohi_ref[:, 2 * FR :], olo_ref[:, 2 * FR :], x_ref[:, pl.ds(l * E, pair * E)])
            for i in range(pair):
                for m in range(M):
                    rows = slice(m * sz.RC, (m + 1) * sz.RC)
                    r = outer[rows, i * E : (i + 1) * E] + w_ref[l + i, rows] + t_ref[m, l + i]
                    new_ref[l + i, rows] = u_ref[l + i, rows] - STEP * r
                    res_ref[l + i, rows] = r

    full = jax.ShapeDtypeStruct(u.shape, F32)
    scratch = [pltpu.VMEM((M, L, sz.RC, E), F32)]
    scratch += [chip_scratch(sz), pltpu.VMEM((FR, L * E), F32), pltpu.VMEM((M, L, CR, E), F32)]
    ins = [VMEM] * (4 + M + sz.Z)
    args = (*mats[2:], u, local, *times, *slides)
    return call(body, [full, full], ins, scratch, 6 * R * FR * L * E, 20 * u.size)(*args)


def over_tm(x, j):
    size = lax.axis_size("tm")
    return lax.ppermute(x, "tm", [(i, i ^ j) for i in range(size)])


def over_chips(x, j):
    size = lax.axis_size("space")
    return lax.ppermute(x, "space", [(i, (i + 2 * j) % size) for i in range(size)])


def over_cores(x):
    size = lax.axis_size("space")
    return lax.ppermute(x, "space", [(i, i ^ 1) for i in range(size)])


def per_device(conserved_field, face_neighbours, counterpart_group, counterpart_shift, volume_operator, flux_matrix):
    sz = Sizes(conserved_field.shape)
    u = conserved_field.reshape(sz.L, sz.R, sz.E)

    def time_trip(parts):
        return [parts[0]] + [over_tm(parts[j], j) for j in range(1, sz.M)]

    def chip_trip(parts):
        return [parts[0]] + [over_chips(parts[j], j) for j in range(1, sz.Z)]

    def faces(field, inner, mine, theirs):
        return face_part(sz, face_neighbours, mats, field, inner, mine[0], theirs[0], theirs[sz.Z - 1], theirs[1])

    chunks = pack_time(sz, u)
    parts = time_trip(chunks)
    packed = pack_space(sz, after(u, chunks[0]))
    mats = matrices(sz, after(flux_matrix, packed[0]), volume_operator)
    packed = [*packed[:-1], after(packed[-1], mats[0])]
    mine = chip_trip(packed)
    inner = inside_part(sz, mats, u)
    turned = turn_time(sz, after(parts, inner))
    times = time_trip(turned)
    theirs = [over_cores(x) for x in mine[:1] + after(mine[1:], turned[0])]
    shifted = shift_slide(sz, counterpart_group, counterpart_shift, mine, theirs)
    slides = chip_trip(shifted)
    here = faces(after(u, shifted[0]), inner, mine, theirs)
    damped = turn_time(sz, after(turned, here), damp=True)
    partial, cuts = first_slide(sz, mats, u, after(here, damped), slides)
    cut_parts = time_trip(cuts)
    u, v, packed = first_step(sz, partial, times)
    mine = chip_trip(packed)
    inner = inside_part(sz, mats, v)
    both = turn_time(sz, after(cut_parts, inner), carried=damped)
    times = time_trip(both)
    theirs = [over_cores(x) for x in mine[:1] + after(mine[1:], both[0])]
    shifted = shift_slide(sz, counterpart_group, counterpart_shift, mine, theirs)
    slides = chip_trip(shifted)
    here = faces(after(v, shifted[0]), inner, mine, theirs)
    new, residual = last_step(sz, mats, u, here, times, slides)
    shape = conserved_field.shape
    return new.reshape(shape), residual.reshape(shape)


def after(values, anchor):
    return lax.optimization_barrier((values, anchor))[0]


def solution(mesh):
    return jax.shard_map(
        per_device,
        mesh=mesh,
        in_specs=(P("tm", None, None, "space"), P(None, "space"), P("tm"), P("tm"), P(), P()),
        out_specs=(P("tm", None, None, "space"), P("tm", None, None, "space")),
        check_vma=False,
    )
```

time: 93 us -> 76.7 us (0.82)
  waiting for transfers between devices: 39.1 us -> 18 us
  starting transfers between devices: 28.2 us -> 37.3 us
  local copies, waits for them, and re-layouts: 2.92 us -> 1.34 us
  other arithmetic: 1.36 us -> 0 us
  Pallas kernels: 20.2 us -> 19 us
    ppermute x12, waiting for transfers between devices: 26.9 us -> 10.7 us  [over_chips(): lax.ppermute(x, 'space', [(i, (i + 2 * j) % size) for i in range(size)])]
    ppermute x12, starting transfers between devices: 10.6 us -> 20.5 us  [over_chips(): lax.ppermute(x, 'space', [(i, (i + 2 * j) % size) for i in range(size)])]
    ppermute x12, waiting for transfers between devices: 11.2 us -> 5.54 us  [over_tm(): return lax.ppermute(x, 'tm', [(i, i ^ j) for i in range(size)])]
    ppermute x12, starting transfers between devices: 16.5 us -> 15.1 us  [over_tm(): return lax.ppermute(x, 'tm', [(i, i ^ j) for i in range(size)])]
    select_n x1 -> x0, other arithmetic: 1.3 us -> none  [per_device(): (index - face_neighbours[0]) % total]
    pallas_call x7 -> x12, Pallas kernels: 15.2 us -> 14 us  [the longest x2 3.7 us: face_part(): return call(body, [out], ins, scratch, flops, 12 * u.size)(*args)[0]]
    unnamed x13 -> x14, local copies, waits for them, and re-layouts: 2.17 us -> 1.34 us
  transfers between devices with their start and end apart: 32 -> 32, of which waited for: 14 -> 8; matrix products, arithmetic and copies ran while one was open for 1% -> 0% of each run, Pallas kernels for 13% -> 21%
where the time goes in v2:
time: 76.7 us; the launch traced here: 76.6 us
  starting transfers between devices  37.3 us (49%)
  Pallas kernels  19 us (25%)
  waiting for transfers between devices  18 us (23%)
  local copies, waits for them, and re-layouts  1.34 us (2%)
  between operations  0.91 us (1%)
    ppermute x12, starting transfers between devices, over_chips(): lax.ppermute(x, 'space', [(i, (i + 2 * j) % size) for i in range(size)])  20.5 us
    ppermute x12, starting transfers between devices, over_tm(): return lax.ppermute(x, 'tm', [(i, i ^ j) for i in range(size)])  15.1 us
    ppermute x12, waiting for transfers between devices, over_chips(): lax.ppermute(x, 'space', [(i, (i + 2 * j) % size) for i in range(size)])  10.7 us
    ppermute x12, waiting for transfers between devices, over_tm(): return lax.ppermute(x, 'tm', [(i, i ^ j) for i in range(size)])  5.54 us
    pallas_call x2, Pallas kernels, face_part(): return call(body, [out], ins, scratch, flops, 12 * u.size)(*args)[0]  3.7 us
    pallas_call x1, Pallas kernels, matrices(): call(body, [inner, inner, outer, outer], [SMEM, VMEM], (), nbytes, nbytes)  3.54 us
    pallas_call x2, Pallas kernels, inside_part(): call(body, [out], [VMEM] * 3, (), 6 * sz.R * u.size, 12 * u.size)  3.42 us
    pallas_call x3, Pallas kernels, turn_time(): call(body, shapes, ins, [full, full], 20 * size, 8 * size)(*parts, *carried)  2.7 us
  transfers between devices with their start and end apart: 32, of which 8 were waited for; matrix products, arithmetic and copies ran while one was open for 0% of the time, Pallas kernels for 21%

profile of v2, /device:TPU:0, one launch (start us, length us, event | category | flops | bytes accessed | tf_op | source)
XLA Modules:
  0.0 76.6 jit_solution(15659903825726456369)
XLA Ops:
  0.6 1.3 %copy-done = f32[4,10,64,128]{3,2,1,0:T(8,128)S(1)} copy-done((f32[4,10,64,128]{3,2,1,0:T(8,128)S(1)}, f32[4,10,64,128]{3,2,1,0:T(8,128)}, u32[]{:S(2)}) %copy-start) | copy-done | bytes 1310744
  2.0 0.2 shard_map.77
  2.2 3.0 %collective-permute-start.4 = (f32[4,160,128]{2,1,0:T(8,128)S(1)}, f32[4,160,128]{2,1,0:T(8,128)S(1)}, u32[]{:S(2)}, u32[]{:S(2)}) collective-permute-start(f32[4,160,128]{2,1,0:T(8,128)S(1)} %get-tuple-element.82), channel_id=1, source_target_pairs={{0,8},{8,0},{16,24},{24,16},{1,9},{9,1},{17,25},{25,17},{2,10},{10... | collective-permute-start | bytes 983048 | tf_op jit(solution)/shard_map/ppermute | solution.py:451
  5.2 1.5 %collective-permute-start.5 = (f32[4,160,128]{2,1,0:T(8,128)S(1)}, f32[4,160,128]{2,1,0:T(8,128)S(1)}, u32[]{:S(2)}, u32[]{:S(2)}) collective-permute-start(f32[4,160,128]{2,1,0:T(8,128)S(1)} %get-tuple-element.83), channel_id=1, source_target_pairs={{0,16},{8,24},{16,0},{24,8},{1,17},{9,25},{17,1},{25,9},{2,18},{10... | collective-permute-start | bytes 983048 | tf_op jit(solution)/shard_map/ppermute | solution.py:451
  6.7 0.0 collective-permute-start.6
  6.7 0.4 shard_map.78
  7.1 3.1 %collective-permute-start.1 = (f32[160,128]{1,0:T(8,128)S(1)}, f32[160,128]{1,0:T(8,128)S(1)}, u32[]{:S(2)}, u32[]{:S(2)}) collective-permute-start(f32[160,128]{1,0:T(8,128)S(1)} %get-tuple-element.78), channel_id=1, source_target_pairs={{0,4},{1,5},{2,6},{3,7},{4,0},{5,1},{6,2},{7,3},{8,12},{9,13},{10,... | collective-permute-start | bytes 245768 | tf_op jit(solution)/shard_map/ppermute | solution.py:456
  10.2 0.0 collective-permute-start.3
  10.2 3.5 %shard_map.79 = (bf16[640,640]{1,0:T(8,128)(2,1)S(1)}, bf16[640,640]{1,0:T(8,128)(2,1)S(1)}, bf16[640,480]{1,0:T(8,128)(2,1)S(1)}, bf16[640,480]{1,0:T(8,128)(2,1)S(1)}) custom-call(f32[2,10,10]{2,1,0:T(8,128)S(1)} %copy.8.flux_ref, f32[2,64,64]{2,1,0:T(8,128)S(1)} %copy-done.2), custom_call_target="tpu_custom_call" | custom-call | flops 2867200 | bytes 2867200 | tf_op jit(solution)/shard_map/pallas_call | solution.py:145
  13.8 2.1 %collective-permute-start = (f32[192,128]{1,0:T(8,128)S(1)}, f32[192,128]{1,0:T(8,128)S(1)}, u32[]{:S(2)}, u32[]{:S(2)}) collective-permute-start(f32[192,128]{1,0:T(8,128)S(1)} %get-tuple-element.77), channel_id=1, source_target_pairs={{0,2},{1,3},{2,4},{3,5},{4,6},{5,7},{6,0},{7,1},{8,10},{9,11},{10,... | collective-permute-start | bytes 294920 | tf_op jit(solution)/shard_map/ppermute | solution.py:456
  15.8 5.5 %collective-permute-done.5.refs_2_ = f32[4,160,128]{2,1,0:T(8,128)S(1)} collective-permute-done((f32[4,160,128]{2,1,0:T(8,128)S(1)}, f32[4,160,128]{2,1,0:T(8,128)S(1)}, u32[]{:S(2)}, u32[]{:S(2)}) %collective-permute-start.5) | collective-permute-done | bytes 327712 | tf_op jit(solution)/shard_map/ppermute | solution.py:451
  21.4 3.6 %collective-permute-start.2 = (f32[192,128]{1,0:T(8,128)S(1)}, f32[192,128]{1,0:T(8,128)S(1)}, u32[]{:S(2)}, u32[]{:S(2)}) collective-permute-start(f32[192,128]{1,0:T(8,128)S(1)} %get-tuple-element.81), channel_id=1, source_target_pairs={{0,6},{1,7},{2,0},{3,1},{4,2},{5,3},{6,4},{7,5},{8,14},{9,15},{10,... | collective-permute-start | bytes 294920 | tf_op jit(solution)/shard_map/ppermute | solution.py:456
  25.0 1.7 %shard_map.80.in_ref = f32[4,640,128]{2,1,0:T(8,128)S(1)} custom-call(bf16[640,640]{1,0:T(8,128)(2,1)S(1)} %get-tuple-element.80.hi_ref, bf16[640,640]{1,0:T(8,128)(2,1)S(1)} %get-tuple-element.85.lo_ref, f32[4,640,128]{2,1,0:T(8,128)S(1)} %bitcast.5), custom_call_target="tpu_custom_call" | custom-call | flops 1258291200 | bytes 3932160 | tf_op jit(solution)/shard_map/pallas_call | solution.py:230
  26.7 0.0 copy-start.4
  26.7 0.0 copy-start.5
  26.7 0.0 copy-start.3
  26.7 0.0 collective-permute-done.6.refs_3_
  26.7 1.1 %shard_map.81 = (f32[4,160,128]{2,1,0:T(8,128)S(1)}, f32[4,160,128]{2,1,0:T(8,128)S(1)}, f32[4,160,128]{2,1,0:T(8,128)S(1)}, f32[4,160,128]{2,1,0:T(8,128)S(1)}) custom-call(f32[4,160,128]{2,1,0:T(8,128)S(1)} %get-tuple-element.86.refs_0_, f32[4,160,128]{2,1,0:T(8,128)S(1)} %collective-permute-done.4.refs_1_, ...), custom_call_target="tpu_custom_call" | custom-call | flops 6553600 | bytes 2621440 | tf_op jit(solution)/shard_map/pallas_call | solution.py:317
  27.8 0.0 collective-permute-done.1.refs_2_
  27.9 0.0 collective-permute-done.2.refs_3_
  27.9 0.1 collective-permute-start.8
  28.0 0.5 collective-permute-start.7
  28.5 0.1 collective-permute-start.9
  28.5 0.0 collective-permute-start.13
  28.5 0.0 collective-permute-done.3.refs_4_.sib_ref
  28.5 2.1 %collective-permute-start.14 = (f32[4,160,128]{2,1,0:T(8,128)S(1)}, f32[4,160,128]{2,1,0:T(8,128)S(1)}, u32[]{:S(2)}, u32[]{:S(2)}) collective-permute-start(f32[4,160,128]{2,1,0:T(8,128)S(1)} %get-tuple-element.101.refs_2_), channel_id=1, source_target_pairs={{0,16},{8,24},{16,0},{24,8},{1,17},{9,25},{17,1},{25,9},{2,18},{10... | collective-permute-start | bytes 983048 | tf_op jit(solution)/shard_map/ppermute | solution.py:451
  30.6 0.0 collective-permute-done.8.refs_6_
  30.6 1.4 %collective-permute-start.15 = (f32[4,160,128]{2,1,0:T(8,128)S(1)}, f32[4,160,128]{2,1,0:T(8,128)S(1)}, u32[]{:S(2)}, u32[]{:S(2)}) collective-permute-start(f32[4,160,128]{2,1,0:T(8,128)S(1)} %get-tuple-element.102.refs_3_), channel_id=1, source_target_pairs={{0,24},{8,16},{16,8},{24,0},{1,25},{9,17},{17,9},{25,1},{2,26},{10... | collective-permute-start | bytes 983048 | tf_op jit(solution)/shard_map/ppermute | solution.py:451
  32.0 0.0 collective-permute-done.9.refs_7_.ahead_ref
  32.0 0.8 shard_map.82
  32.8 0.1 collective-permute-start.10
  32.9 3.9 %collective-permute-start.11 = (f32[160,128]{1,0:T(8,128)S(1)}, f32[160,128]{1,0:T(8,128)S(1)}, u32[]{:S(2)}, u32[]{:S(2)}) collective-permute-start(f32[160,128]{1,0:T(8,128)S(1)} %get-tuple-element.109), channel_id=1, source_target_pairs={{0,4},{1,5},{2,6},{3,7},{4,0},{5,1},{6,2},{7,3},{8,12},{9,13},{10,... | collective-permute-start | bytes 245768 | tf_op jit(solution)/shard_map/ppermute | solution.py:456
  36.8 2.8 %collective-permute-done.10.refs_1_ = f32[160,128]{1,0:T(8,128)S(1)} collective-permute-done((f32[160,128]{1,0:T(8,128)S(1)}, f32[160,128]{1,0:T(8,128)S(1)}, u32[]{:S(2)}, u32[]{:S(2)}) %collective-permute-start.10) | collective-permute-done | bytes 81952 | tf_op jit(solution)/shard_map/ppermute | solution.py:456
  39.6 1.7 %collective-permute-start.12 = (f32[160,128]{1,0:T(8,128)S(1)}, f32[160,128]{1,0:T(8,128)S(1)}, u32[]{:S(2)}, u32[]{:S(2)}) collective-permute-start(f32[160,128]{1,0:T(8,128)S(1)} %get-tuple-element.110), channel_id=1, source_target_pairs={{0,6},{1,7},{2,0},{3,1},{4,2},{5,3},{6,4},{7,5},{8,14},{9,15},{10,... | collective-permute-start | bytes 245768 | tf_op jit(solution)/shard_map/ppermute | solution.py:456
  41.3 1.9 %shard_map.83.w_ref = f32[4,640,128]{2,1,0:T(8,128)S(1)} custom-call(s32[2,128]{1,0:T(2,128)S(1)} %copy-done.3, bf16[640,480]{1,0:T(8,128)(2,1)S(1)} %get-tuple-element.75.ohi_ref, bf16[640,480]{1,0:T(8,128)(2,1)S(1)} %get-tuple-element.76.olo_ref, f32[4,640,128]{2,1,0:T(8,128)S(1)} %bitcast.6, f32[4,640,128]{2,1,0:T(8,128)S(1)} %shard_map.80.in_ref, ...), custom_call_target="tpu_custom_call" | custom-call | flops 629145600 | bytes 3932160 | tf_op jit(solution)/shard_map/pallas_call | solution.py:276
  43.1 1.2 %shard_map.84 = (f32[4,160,128]{2,1,0:T(8,128)S(1)}, f32[4,160,128]{2,1,0:T(8,128)S(1)}, f32[4,160,128]{2,1,0:T(8,128)S(1)}, f32[4,160,128]{2,1,0:T(8,128)S(1)}) custom-call(f32[4,160,128]{2,1,0:T(8,128)S(1)} %get-tuple-element.99.refs_0_, f32[4,160,128]{2,1,0:T(8,128)S(1)} %get-tuple-element.100.refs_1_, f32[4,160,128]{2,1,0:T(8,128)S(1)} %get-tuple-element.101.refs_2_, ...), custom_call_target="tpu_custom_call" | custom-call | flops 6553600 | bytes 2621440 | tf_op jit(solution)/shard_map/pallas_call | solution.py:317
  44.4 0.0 collective-permute-done.11.refs_2_
  44.4 0.8 %shard_map.85 = (f32[4,640,128]{2,1,0:T(8,128)S(1)}, f32[4,40,128]{2,1,0:T(8,128)S(1)}, f32[4,40,128]{2,1,0:T(8,128)S(1)}, f32[4,40,128]{2,1,0:T(8,128)S(1)}, f32[4,40,128]{2,1,0:T(8,128)S(1)}) custom-call(bf16[640,480]{1,0:T(8,128)(2,1)S(1)} %get-tuple-element.75.ohi_ref, bf16[640,480]{1,0:T(8,128)(2,1)S(1)} %get-tuple-element.76.olo_ref, ...), custom_call_target="tpu_custom_call" | custom-call | flops 314572800 | bytes 3932160 | tf_op jit(solution)/shard_map/pallas_call | solution.py:392
  45.2 0.5 collective-permute-start.20
  45.7 1.6 %collective-permute-start.21 = (f32[4,40,128]{2,1,0:T(8,128)S(1)}, f32[4,40,128]{2,1,0:T(8,128)S(1)}, u32[]{:S(2)}, u32[]{:S(2)}) collective-permute-start(f32[4,40,128]{2,1,0:T(8,128)S(1)} %get-tuple-element.120), channel_id=1, source_target_pairs={{0,16},{8,24},{16,0},{24,8},{1,17},{9,25},{17,1},{25,9},{2,18},{10... | collective-permute-start | bytes 245768 | tf_op jit(solution)/shard_map/ppermute | solution.py:451
  47.3 1.4 %collective-permute-start.22 = (f32[4,40,128]{2,1,0:T(8,128)S(1)}, f32[4,40,128]{2,1,0:T(8,128)S(1)}, u32[]{:S(2)}, u32[]{:S(2)}) collective-permute-start(f32[4,40,128]{2,1,0:T(8,128)S(1)} %get-tuple-element.121), channel_id=1, source_target_pairs={{0,24},{8,16},{16,8},{24,0},{1,25},{9,17},{17,9},{25,1},{2,26},{10... | collective-permute-start | bytes 245768 | tf_op jit(solution)/shard_map/ppermute | solution.py:451
  48.7 0.5 shard_map.86
  49.2 0.1 collective-permute-start.17
  49.3 3.7 %collective-permute-start.16 = (f32[192,128]{1,0:T(8,128)S(1)}, f32[192,128]{1,0:T(8,128)S(1)}, u32[]{:S(2)}, u32[]{:S(2)}) collective-permute-start(f32[192,128]{1,0:T(8,128)S(1)} %get-tuple-element.115), channel_id=1, source_target_pairs={{0,2},{1,3},{2,4},{3,5},{4,6},{5,7},{6,0},{7,1},{8,10},{9,11},{10,... | collective-permute-start | bytes 294920 | tf_op jit(solution)/shard_map/ppermute | solution.py:456
  52.9 0.2 collective-permute-start.18
  53.2 1.7 %shard_map.87.in_ref = f32[4,640,128]{2,1,0:T(8,128)S(1)} custom-call(bf16[640,640]{1,0:T(8,128)(2,1)S(1)} %get-tuple-element.80.hi_ref, bf16[640,640]{1,0:T(8,128)(2,1)S(1)} %get-tuple-element.85.lo_ref, f32[4,640,128]{2,1,0:T(8,128)S(1)} %get-tuple-element.131.u_ref), custom_call_target="tpu_custom_call" | custom-call | flops 1258291200 | bytes 3932160 | tf_op jit(solution)/shard_map/pallas_call | solution.py:230
  54.9 0.4 shard_map.88
  55.3 0.5 collective-permute-start.26
  55.8 1.6 %collective-permute-start.27 = (f32[4,200,128]{2,1,0:T(8,128)S(1)}, f32[4,200,128]{2,1,0:T(8,128)S(1)}, u32[]{:S(2)}, u32[]{:S(2)}) collective-permute-start(f32[4,200,128]{2,1,0:T(8,128)S(1)} %get-tuple-element.133), channel_id=1, source_target_pairs={{0,16},{8,24},{16,0},{24,8},{1,17},{9,25},{17,1},{25,9},{2,18},{10... | collective-permute-start | bytes 1228808 | tf_op jit(solution)/shard_map/ppermute | solution.py:451
  57.4 1.4 %collective-permute-start.28 = (f32[4,200,128]{2,1,0:T(8,128)S(1)}, f32[4,200,128]{2,1,0:T(8,128)S(1)}, u32[]{:S(2)}, u32[]{:S(2)}) collective-permute-start(f32[4,200,128]{2,1,0:T(8,128)S(1)} %get-tuple-element.134), channel_id=1, source_target_pairs={{0,24},{8,16},{16,8},{24,0},{1,25},{9,17},{17,9},{25,1},{2,26},{10... | collective-permute-start | bytes 1228808 | tf_op jit(solution)/shard_map/ppermute | solution.py:451
  58.8 0.5 collective-permute-start.24
  59.3 0.8 %collective-permute-done.19.refs_4_.sib_ref = f32[224,128]{1,0:T(8,128)S(1)} collective-permute-done((f32[224,128]{1,0:T(8,128)S(1)}, f32[224,128]{1,0:T(8,128)S(1)}, u32[]{:S(2)}, u32[]{:S(2)}) %collective-permute-start.19) | collective-permute-done | bytes 114720 | tf_op jit(solution)/shard_map/ppermute | solution.py:461
  60.1 0.2 collective-permute-start.23
  60.3 0.4 collective-permute-start.25
  60.7 0.8 %collective-permute-done.23.refs_5_.behind_ref = f32[192,128]{1,0:T(8,128)S(1)} collective-permute-done((f32[192,128]{1,0:T(8,128)S(1)}, f32[192,128]{1,0:T(8,128)S(1)}, u32[]{:S(2)}, u32[]{:S(2)}) %collective-permute-start.23) | collective-permute-done | bytes 98336 | tf_op jit(solution)/shard_map/ppermute | solution.py:461
  61.5 0.2 collective-permute-done.25.refs_7_.ahead_ref
  61.6 0.7 shard_map.89
  62.4 1.9 %collective-permute-start.29 = (f32[160,128]{1,0:T(8,128)S(1)}, f32[160,128]{1,0:T(8,128)S(1)}, u32[]{:S(2)}, u32[]{:S(2)}) collective-permute-start(f32[160,128]{1,0:T(8,128)S(1)} %get-tuple-element.135), channel_id=1, source_target_pairs={{0,2},{1,3},{2,4},{3,5},{4,6},{5,7},{6,0},{7,1},{8,10},{9,11},{10,... | collective-permute-start | bytes 245768 | tf_op jit(solution)/shard_map/ppermute | solution.py:456
  64.2 0.2 collective-permute-start.30
  64.5 5.1 %collective-permute-done.29.refs_5_ = f32[160,128]{1,0:T(8,128)S(1)} collective-permute-done((f32[160,128]{1,0:T(8,128)S(1)}, f32[160,128]{1,0:T(8,128)S(1)}, u32[]{:S(2)}, u32[]{:S(2)}) %collective-permute-start.29) | collective-permute-done | bytes 81952 | tf_op jit(solution)/shard_map/ppermute | solution.py:456
  69.6 1.9 %shard_map.90.w_ref = f32[4,640,128]{2,1,0:T(8,128)S(1)} custom-call(s32[2,128]{1,0:T(2,128)S(1)} %copy-done.3, bf16[640,480]{1,0:T(8,128)(2,1)S(1)} %get-tuple-element.75.ohi_ref, bf16[640,480]{1,0:T(8,128)(2,1)S(1)} %get-tuple-element.76.olo_ref, f32[4,640,128]{2,1,0:T(8,128)S(1)} %get-tuple-element.131.u_ref, f32[4,640,128]{2,1,0:T(8,128)S(1)} %shard_map.87.in_ref, ...), custom_call_target="tpu_custom_call" | custom-call | flops 629145600 | bytes 3932160 | tf_op jit(solution)/shard_map/pallas_call | solution.py:276
  71.5 1.1 %collective-permute-done.30.refs_6_ = f32[160,128]{1,0:T(8,128)S(1)} collective-permute-done((f32[160,128]{1,0:T(8,128)S(1)}, f32[160,128]{1,0:T(8,128)S(1)}, u32[]{:S(2)}, u32[]{:S(2)}) %collective-permute-start.30) | collective-permute-done | bytes 81952 | tf_op jit(solution)/shard_map/ppermute | solution.py:456
  72.5 1.7 %collective-permute-done.31.refs_7_ = f32[160,128]{1,0:T(8,128)S(1)} collective-permute-done((f32[160,128]{1,0:T(8,128)S(1)}, f32[160,128]{1,0:T(8,128)S(1)}, u32[]{:S(2)}, u32[]{:S(2)}) %collective-permute-start.31) | collective-permute-done | bytes 81952 | tf_op jit(solution)/shard_map/ppermute | solution.py:456
  74.2 2.4 %shard_map.91 = (f32[4,640,128]{2,1,0:T(8,128)}, f32[4,640,128]{2,1,0:T(8,128)}) custom-call(bf16[640,480]{1,0:T(8,128)(2,1)S(1)} %get-tuple-element.75.ohi_ref, bf16[640,480]{1,0:T(8,128)(2,1)S(1)} %get-tuple-element.76.olo_ref, f32[4,640,128]{2,1,0:T(8,128)S(1)} %get-tuple-element.112.u_ref, f32[4,640,128]{2,1,0:T(8,128)S(1)} %shard_map.90.w_ref, ...), custom_call_target="tpu_custom_call" | custom-call | flops 314572800 | bytes 6553600 | tf_op jit(solution)/shard_map/pallas_call | solution.py:446
  (30 shorter events, 0.1 us)
Async XLA Ops:
  0.6 1.3 %copy-start = (f32[4,10,64,128]{3,2,1,0:T(8,128)S(1)}, f32[4,10,64,128]{3,2,1,0:T(8,128)}, u32[]{:S(2)}) copy-start(f32[4,10,64,128]{3,2,1,0:T(8,128)} %param.6) | copy-start | bytes 3932164
  1.9 8.3 %copy-start.6 = (f32[2,10,10]{2,0,1:T(2,128)S(1)}, f32[2,10,10]{2,0,1:T(2,128)}, u32[]{:S(2)}) copy-start(f32[2,10,10]{2,0,1:T(2,128)} %param.11) | copy-start | bytes 2404
  1.9 8.3 %copy-start.2 = (f32[2,64,64]{2,1,0:T(8,128)S(1)}, f32[2,64,64]{2,1,0:T(8,128)}, u32[]{:S(2)}) copy-start(f32[2,64,64]{2,1,0:T(8,128)} %vol_ref.1) | copy-start | bytes 98308
  2.0 23.0 %copy-start.1 = (f32[4,10,64,128]{3,2,1,0:T(8,128)S(1)}, f32[4,10,64,128]{3,2,1,0:T(8,128)}, u32[]{:S(2)}) copy-start(f32[4,10,64,128]{3,2,1,0:T(8,128)} %param.6) | copy-start | bytes 3932164
  2.2 11.6 %collective-permute-start.4 = (f32[4,160,128]{2,1,0:T(8,128)S(1)}, f32[4,160,128]{2,1,0:T(8,128)S(1)}, u32[]{:S(2)}, u32[]{:S(2)}) collective-permute-start(f32[4,160,128]{2,1,0:T(8,128)S(1)} %get-tuple-element.82), channel_id=1, source_target_pairs={{0,8},{8,0},{16,24},{24,16},{1,9},{9,1},{17,25},{25,17},{2,10},{10... | collective-permute-start | bytes 983048 | tf_op jit(solution)/shard_map/ppermute | solution.py:451
  5.2 16.2 %collective-permute-start.5 = (f32[4,160,128]{2,1,0:T(8,128)S(1)}, f32[4,160,128]{2,1,0:T(8,128)S(1)}, u32[]{:S(2)}, u32[]{:S(2)}) collective-permute-start(f32[4,160,128]{2,1,0:T(8,128)S(1)} %get-tuple-element.83), channel_id=1, source_target_pairs={{0,16},{8,24},{16,0},{24,8},{1,17},{9,25},{17,1},{25,9},{2,18},{10... | collective-permute-start | bytes 983048 | tf_op jit(solution)/shard_map/ppermute | solution.py:451
  6.7 20.0 %collective-permute-start.6 = (f32[4,160,128]{2,1,0:T(8,128)S(1)}, f32[4,160,128]{2,1,0:T(8,128)S(1)}, u32[]{:S(2)}, u32[]{:S(2)}) collective-permute-start(f32[4,160,128]{2,1,0:T(8,128)S(1)} %get-tuple-element.84), channel_id=1, source_target_pairs={{0,24},{8,16},{16,8},{24,0},{1,25},{9,17},{17,9},{25,1},{2,26},{10... | collective-permute-start | bytes 983048 | tf_op jit(solution)/shard_map/ppermute | solution.py:451
  7.1 20.8 %collective-permute-start.1 = (f32[160,128]{1,0:T(8,128)S(1)}, f32[160,128]{1,0:T(8,128)S(1)}, u32[]{:S(2)}, u32[]{:S(2)}) collective-permute-start(f32[160,128]{1,0:T(8,128)S(1)} %get-tuple-element.78), channel_id=1, source_target_pairs={{0,4},{1,5},{2,6},{3,7},{4,0},{5,1},{6,2},{7,3},{8,12},{9,13},{10,... | collective-permute-start | bytes 245768 | tf_op jit(solution)/shard_map/ppermute | solution.py:456
  10.2 18.3 %collective-permute-start.3 = (f32[224,128]{1,0:T(8,128)S(1)}, f32[224,128]{1,0:T(8,128)S(1)}, u32[]{:S(2)}, u32[]{:S(2)}) collective-permute-start(f32[224,128]{1,0:T(8,128)S(1)} %get-tuple-element.73.refs_0_), channel_id=1, source_target_pairs={{0,1},{1,0},{2,3},{3,2},{4,5},{5,4},{6,7},{7,6},{8,9},{9,8},{10,11... | collective-permute-start | bytes 344072 | tf_op jit(solution)/shard_map/ppermute | solution.py:461
  13.8 14.1 %collective-permute-start = (f32[192,128]{1,0:T(8,128)S(1)}, f32[192,128]{1,0:T(8,128)S(1)}, u32[]{:S(2)}, u32[]{:S(2)}) collective-permute-start(f32[192,128]{1,0:T(8,128)S(1)} %get-tuple-element.77), channel_id=1, source_target_pairs={{0,2},{1,3},{2,4},{3,5},{4,6},{5,7},{6,0},{7,1},{8,10},{9,11},{10,... | collective-permute-start | bytes 294920 | tf_op jit(solution)/shard_map/ppermute | solution.py:456
  21.4 6.5 %collective-permute-start.2 = (f32[192,128]{1,0:T(8,128)S(1)}, f32[192,128]{1,0:T(8,128)S(1)}, u32[]{:S(2)}, u32[]{:S(2)}) collective-permute-start(f32[192,128]{1,0:T(8,128)S(1)} %get-tuple-element.81), channel_id=1, source_target_pairs={{0,6},{1,7},{2,0},{3,1},{4,2},{5,3},{6,4},{7,5},{8,14},{9,15},{10,... | collective-permute-start | bytes 294920 | tf_op jit(solution)/shard_map/ppermute | solution.py:456
  26.7 5.4 %copy-start.4 = (s32[4]{0:T(128)S(1)}, s32[4]{0:T(128)}, u32[]{:S(2)}) copy-start(s32[4]{0:T(128)} %group_ref.3) | copy-start | bytes 52
  26.7 5.4 %copy-start.5 = (s32[4]{0:T(128)S(1)}, s32[4]{0:T(128)}, u32[]{:S(2)}) copy-start(s32[4]{0:T(128)} %shift_ref.3) | copy-start | bytes 52
  26.7 14.6 %copy-start.3 = (s32[2,128]{1,0:T(2,128)S(1)}, s32[2,128]{1,0:T(2,128)}, u32[]{:S(2)}) copy-start(s32[2,128]{1,0:T(2,128)} %near_ref.3) | copy-start | bytes 3076
  27.9 2.7 %collective-permute-start.8 = (f32[160,128]{1,0:T(8,128)S(1)}, f32[160,128]{1,0:T(8,128)S(1)}, u32[]{:S(2)}, u32[]{:S(2)}) collective-permute-start(f32[160,128]{1,0:T(8,128)S(1)} %collective-permute-done.1.refs_2_), channel_id=1, source_target_pairs={{0,1},{1,0},{2,3},{3,2},{4,5},{5,4},{6,7},{7,6},{8,9},{9,8},{10,11... | collective-permute-start | bytes 245768 | tf_op jit(solution)/shard_map/ppermute | solution.py:461
  28.0 4.1 %collective-permute-start.7 = (f32[192,128]{1,0:T(8,128)S(1)}, f32[192,128]{1,0:T(8,128)S(1)}, u32[]{:S(2)}, u32[]{:S(2)}) collective-permute-start(f32[192,128]{1,0:T(8,128)S(1)} %collective-permute-done.refs_1_), channel_id=1, source_target_pairs={{0,1},{1,0},{2,3},{3,2},{4,5},{5,4},{6,7},{7,6},{8,9},{9,8},{10,11... | collective-permute-start | bytes 294920 | tf_op jit(solution)/shard_map/ppermute | solution.py:461
  28.5 3.6 %collective-permute-start.9 = (f32[192,128]{1,0:T(8,128)S(1)}, f32[192,128]{1,0:T(8,128)S(1)}, u32[]{:S(2)}, u32[]{:S(2)}) collective-permute-start(f32[192,128]{1,0:T(8,128)S(1)} %collective-permute-done.2.refs_3_), channel_id=1, source_target_pairs={{0,1},{1,0},{2,3},{3,2},{4,5},{5,4},{6,7},{7,6},{8,9},{9,8},{10,11... | collective-permute-start | bytes 294920 | tf_op jit(solution)/shard_map/ppermute | solution.py:461
  28.5 18.8 %collective-permute-start.13 = (f32[4,160,128]{2,1,0:T(8,128)S(1)}, f32[4,160,128]{2,1,0:T(8,128)S(1)}, u32[]{:S(2)}, u32[]{:S(2)}) collective-permute-start(f32[4,160,128]{2,1,0:T(8,128)S(1)} %get-tuple-element.100.refs_1_), channel_id=1, source_target_pairs={{0,8},{8,0},{16,24},{24,16},{1,9},{9,1},{17,25},{25,17},{2,10},{10... | collective-permute-start | bytes 983048 | tf_op jit(solution)/shard_map/ppermute | solution.py:451
  28.5 20.2 %collective-permute-start.14 = (f32[4,160,128]{2,1,0:T(8,128)S(1)}, f32[4,160,128]{2,1,0:T(8,128)S(1)}, u32[]{:S(2)}, u32[]{:S(2)}) collective-permute-start(f32[4,160,128]{2,1,0:T(8,128)S(1)} %get-tuple-element.101.refs_2_), channel_id=1, source_target_pairs={{0,16},{8,24},{16,0},{24,8},{1,17},{9,25},{17,1},{25,9},{2,18},{10... | collective-permute-start | bytes 983048 | tf_op jit(solution)/shard_map/ppermute | solution.py:451
  30.6 18.1 %collective-permute-start.15 = (f32[4,160,128]{2,1,0:T(8,128)S(1)}, f32[4,160,128]{2,1,0:T(8,128)S(1)}, u32[]{:S(2)}, u32[]{:S(2)}) collective-permute-start(f32[4,160,128]{2,1,0:T(8,128)S(1)} %get-tuple-element.102.refs_3_), channel_id=1, source_target_pairs={{0,24},{8,16},{16,8},{24,0},{1,25},{9,17},{17,9},{25,1},{2,26},{10... | collective-permute-start | bytes 983048 | tf_op jit(solution)/shard_map/ppermute | solution.py:451
  32.8 6.8 %collective-permute-start.10 = (f32[160,128]{1,0:T(8,128)S(1)}, f32[160,128]{1,0:T(8,128)S(1)}, u32[]{:S(2)}, u32[]{:S(2)}) collective-permute-start(f32[160,128]{1,0:T(8,128)S(1)} %get-tuple-element.108), channel_id=1, source_target_pairs={{0,2},{1,3},{2,4},{3,5},{4,6},{5,7},{6,0},{7,1},{8,10},{9,11},{10,... | collective-permute-start | bytes 245768 | tf_op jit(solution)/shard_map/ppermute | solution.py:456
  32.9 11.5 %collective-permute-start.11 = (f32[160,128]{1,0:T(8,128)S(1)}, f32[160,128]{1,0:T(8,128)S(1)}, u32[]{:S(2)}, u32[]{:S(2)}) collective-permute-start(f32[160,128]{1,0:T(8,128)S(1)} %get-tuple-element.109), channel_id=1, source_target_pairs={{0,4},{1,5},{2,6},{3,7},{4,0},{5,1},{6,2},{7,3},{8,12},{9,13},{10,... | collective-permute-start | bytes 245768 | tf_op jit(solution)/shard_map/ppermute | solution.py:456
  39.6 4.8 %collective-permute-start.12 = (f32[160,128]{1,0:T(8,128)S(1)}, f32[160,128]{1,0:T(8,128)S(1)}, u32[]{:S(2)}, u32[]{:S(2)}) collective-permute-start(f32[160,128]{1,0:T(8,128)S(1)} %get-tuple-element.110), channel_id=1, source_target_pairs={{0,6},{1,7},{2,0},{3,1},{4,2},{5,3},{6,4},{7,5},{8,14},{9,15},{10,... | collective-permute-start | bytes 245768 | tf_op jit(solution)/shard_map/ppermute | solution.py:456
  45.2 7.8 %collective-permute-start.20 = (f32[4,40,128]{2,1,0:T(8,128)S(1)}, f32[4,40,128]{2,1,0:T(8,128)S(1)}, u32[]{:S(2)}, u32[]{:S(2)}) collective-permute-start(f32[4,40,128]{2,1,0:T(8,128)S(1)} %get-tuple-element.119), channel_id=1, source_target_pairs={{0,8},{8,0},{16,24},{24,16},{1,9},{9,1},{17,25},{25,17},{2,10},{10... | collective-permute-start | bytes 245768 | tf_op jit(solution)/shard_map/ppermute | solution.py:451
  45.7 9.2 %collective-permute-start.21 = (f32[4,40,128]{2,1,0:T(8,128)S(1)}, f32[4,40,128]{2,1,0:T(8,128)S(1)}, u32[]{:S(2)}, u32[]{:S(2)}) collective-permute-start(f32[4,40,128]{2,1,0:T(8,128)S(1)} %get-tuple-element.120), channel_id=1, source_target_pairs={{0,16},{8,24},{16,0},{24,8},{1,17},{9,25},{17,1},{25,9},{2,18},{10... | collective-permute-start | bytes 245768 | tf_op jit(solution)/shard_map/ppermute | solution.py:451
  47.3 7.6 %collective-permute-start.22 = (f32[4,40,128]{2,1,0:T(8,128)S(1)}, f32[4,40,128]{2,1,0:T(8,128)S(1)}, u32[]{:S(2)}, u32[]{:S(2)}) collective-permute-start(f32[4,40,128]{2,1,0:T(8,128)S(1)} %get-tuple-element.121), channel_id=1, source_target_pairs={{0,24},{8,16},{16,8},{24,0},{1,25},{9,17},{17,9},{25,1},{2,26},{10... | collective-permute-start | bytes 245768 | tf_op jit(solution)/shard_map/ppermute | solution.py:451
  49.2 8.2 %collective-permute-start.17 = (f32[160,128]{1,0:T(8,128)S(1)}, f32[160,128]{1,0:T(8,128)S(1)}, u32[]{:S(2)}, u32[]{:S(2)}) collective-permute-start(f32[160,128]{1,0:T(8,128)S(1)} %get-tuple-element.116), channel_id=1, source_target_pairs={{0,4},{1,5},{2,6},{3,7},{4,0},{5,1},{6,2},{7,3},{8,12},{9,13},{10,... | collective-permute-start | bytes 245768 | tf_op jit(solution)/shard_map/ppermute | solution.py:456
  49.3 9.5 %collective-permute-start.16 = (f32[192,128]{1,0:T(8,128)S(1)}, f32[192,128]{1,0:T(8,128)S(1)}, u32[]{:S(2)}, u32[]{:S(2)}) collective-permute-start(f32[192,128]{1,0:T(8,128)S(1)} %get-tuple-element.115), channel_id=1, source_target_pairs={{0,2},{1,3},{2,4},{3,5},{4,6},{5,7},{6,0},{7,1},{8,10},{9,11},{10,... | collective-permute-start | bytes 294920 | tf_op jit(solution)/shard_map/ppermute | solution.py:456
  52.9 5.9 %collective-permute-start.18 = (f32[192,128]{1,0:T(8,128)S(1)}, f32[192,128]{1,0:T(8,128)S(1)}, u32[]{:S(2)}, u32[]{:S(2)}) collective-permute-start(f32[192,128]{1,0:T(8,128)S(1)} %get-tuple-element.117), channel_id=1, source_target_pairs={{0,6},{1,7},{2,0},{3,1},{4,2},{5,3},{6,4},{7,5},{8,14},{9,15},{10,... | collective-permute-start | bytes 294920 | tf_op jit(solution)/shard_map/ppermute | solution.py:456
  55.3 18.9 %collective-permute-start.26 = (f32[4,200,128]{2,1,0:T(8,128)S(1)}, f32[4,200,128]{2,1,0:T(8,128)S(1)}, u32[]{:S(2)}, u32[]{:S(2)}) collective-permute-start(f32[4,200,128]{2,1,0:T(8,128)S(1)} %get-tuple-element.132), channel_id=1, source_target_pairs={{0,8},{8,0},{16,24},{24,16},{1,9},{9,1},{17,25},{25,17},{2,10},{10... | collective-permute-start | bytes 1228808 | tf_op jit(solution)/shard_map/ppermute | solution.py:451
  55.8 18.4 %collective-permute-start.27 = (f32[4,200,128]{2,1,0:T(8,128)S(1)}, f32[4,200,128]{2,1,0:T(8,128)S(1)}, u32[]{:S(2)}, u32[]{:S(2)}) collective-permute-start(f32[4,200,128]{2,1,0:T(8,128)S(1)} %get-tuple-element.133), channel_id=1, source_target_pairs={{0,16},{8,24},{16,0},{24,8},{1,17},{9,25},{17,1},{25,9},{2,18},{10... | collective-permute-start | bytes 1228808 | tf_op jit(solution)/shard_map/ppermute | solution.py:451
  57.4 16.8 %collective-permute-start.28 = (f32[4,200,128]{2,1,0:T(8,128)S(1)}, f32[4,200,128]{2,1,0:T(8,128)S(1)}, u32[]{:S(2)}, u32[]{:S(2)}) collective-permute-start(f32[4,200,128]{2,1,0:T(8,128)S(1)} %get-tuple-element.134), channel_id=1, source_target_pairs={{0,24},{8,16},{16,8},{24,0},{1,25},{9,17},{17,9},{25,1},{2,26},{10... | collective-permute-start | bytes 1228808 | tf_op jit(solution)/shard_map/ppermute | solution.py:451
  58.8 1.3 %collective-permute-start.19 = (f32[224,128]{1,0:T(8,128)S(1)}, f32[224,128]{1,0:T(8,128)S(1)}, u32[]{:S(2)}, u32[]{:S(2)}) collective-permute-start(f32[224,128]{1,0:T(8,128)S(1)} %get-tuple-element.114.refs_0_), channel_id=1, source_target_pairs={{0,1},{1,0},{2,3},{3,2},{4,5},{5,4},{6,7},{7,6},{8,9},{9,8},{10,11... | collective-permute-start | bytes 344072 | tf_op jit(solution)/shard_map/ppermute | solution.py:461
  58.8 1.5 %collective-permute-start.24 = (f32[160,128]{1,0:T(8,128)S(1)}, f32[160,128]{1,0:T(8,128)S(1)}, u32[]{:S(2)}, u32[]{:S(2)}) collective-permute-start(f32[160,128]{1,0:T(8,128)S(1)} %collective-permute-done.17.refs_2_), channel_id=1, source_target_pairs={{0,1},{1,0},{2,3},{3,2},{4,5},{5,4},{6,7},{7,6},{8,9},{9,8},{10,11... | collective-permute-start | bytes 245768 | tf_op jit(solution)/shard_map/ppermute | solution.py:461
  60.1 1.3 %collective-permute-start.23 = (f32[192,128]{1,0:T(8,128)S(1)}, f32[192,128]{1,0:T(8,128)S(1)}, u32[]{:S(2)}, u32[]{:S(2)}) collective-permute-start(f32[192,128]{1,0:T(8,128)S(1)} %collective-permute-done.16.refs_1_), channel_id=1, source_target_pairs={{0,1},{1,0},{2,3},{3,2},{4,5},{5,4},{6,7},{7,6},{8,9},{9,8},{10,11... | collective-permute-start | bytes 294920 | tf_op jit(solution)/shard_map/ppermute | solution.py:461
  60.3 1.3 %collective-permute-start.25 = (f32[192,128]{1,0:T(8,128)S(1)}, f32[192,128]{1,0:T(8,128)S(1)}, u32[]{:S(2)}, u32[]{:S(2)}) collective-permute-start(f32[192,128]{1,0:T(8,128)S(1)} %collective-permute-done.18.refs_3_), channel_id=1, source_target_pairs={{0,1},{1,0},{2,3},{3,2},{4,5},{5,4},{6,7},{7,6},{8,9},{9,8},{10,11... | collective-permute-start | bytes 294920 | tf_op jit(solution)/shard_map/ppermute | solution.py:461
  62.4 7.2 %collective-permute-start.29 = (f32[160,128]{1,0:T(8,128)S(1)}, f32[160,128]{1,0:T(8,128)S(1)}, u32[]{:S(2)}, u32[]{:S(2)}) collective-permute-start(f32[160,128]{1,0:T(8,128)S(1)} %get-tuple-element.135), channel_id=1, source_target_pairs={{0,2},{1,3},{2,4},{3,5},{4,6},{5,7},{6,0},{7,1},{8,10},{9,11},{10,... | collective-permute-start | bytes 245768 | tf_op jit(solution)/shard_map/ppermute | solution.py:456
  64.2 8.3 %collective-permute-start.30 = (f32[160,128]{1,0:T(8,128)S(1)}, f32[160,128]{1,0:T(8,128)S(1)}, u32[]{:S(2)}, u32[]{:S(2)}) collective-permute-start(f32[160,128]{1,0:T(8,128)S(1)} %get-tuple-element.136), channel_id=1, source_target_pairs={{0,4},{1,5},{2,6},{3,7},{4,0},{5,1},{6,2},{7,3},{8,12},{9,13},{10,... | collective-permute-start | bytes 245768 | tf_op jit(solution)/shard_map/ppermute | solution.py:456
  69.6 4.6 %collective-permute-start.31 = (f32[160,128]{1,0:T(8,128)S(1)}, f32[160,128]{1,0:T(8,128)S(1)}, u32[]{:S(2)}, u32[]{:S(2)}) collective-permute-start(f32[160,128]{1,0:T(8,128)S(1)} %get-tuple-element.137), channel_id=1, source_target_pairs={{0,6},{1,7},{2,0},{3,1},{4,2},{5,3},{6,4},{7,5},{8,14},{9,15},{10,... | collective-permute-start | bytes 245768 | tf_op jit(solution)/shard_map/ppermute | solution.py:456

commit v3 on v2

--- a/solution.py
+++ b/solution.py
@@ -30,6 +30,7 @@
         self.N = lax.axis_size("space")
         self.T = self.L * self.M
         self.Z = self.N // 2
+        self.half = self.Z // 2
         self.RC = self.R // self.M
         self.face = self.Q // 4
         self.FR = self.V * self.face
@@ -41,6 +42,12 @@
         if j == 0:
             return 2 * self.H + self.CH
         return self.CH + self.H * ((j == 1) + (j == self.Z - 1))
+
+    def front(self, j):
+        return self.H if j == 1 else 0
+
+    def ahead(self, z, core, j):
+        return lax.rem(z + self.Z + jnp.where(core == 0, j, -j), self.Z)
 
 
 def time_weights(total):
@@ -150,7 +157,12 @@
 
 
 def chip_shapes(sz):
-    return [jax.ShapeDtypeStruct((sz.z_rows(j), sz.E), F32) for j in range(sz.Z)]
+    block = (sz.CH, sz.E)
+    return [
+        jax.ShapeDtypeStruct((sz.half + 2, *block), F32),
+        jax.ShapeDtypeStruct((sz.half, *block), F32),
+        jax.ShapeDtypeStruct(block, F32),
+    ]
 
 
 def pack_time(sz, u):
@@ -174,7 +186,37 @@
     return pltpu.VMEM((sz.Z, sz.CH, sz.E), F32)
 
 
-def pack_chips(sz, slide_ref, halo_ref, zz, stage):
+def pack_chips(sz, slide_ref, halo_ref, outs, stage):
+    swap_ref, keep_ref, far_ref = outs
+    _, z, core = spot()
+    for p in range(sz.Z):
+        first = (p % sz.PL) * sz.CH
+        stage[p] = slide_ref[p // sz.PL, pl.ds(3 + 4 * first, sz.CH, stride=4), :]
+    for j in range(sz.half):
+        swap_ref[j] = stage[sz.ahead(z, 1 - core, j)]
+        keep_ref[j] = stage[sz.ahead(z, core, j)]
+    far_ref[...] = stage[lax.rem(z + sz.half, sz.Z)]
+    lane = iota((SUB, sz.E), 1)
+    slot = lane // REACH
+    last = sz.E - REACH + lane % REACH
+    first = lane % REACH
+    tiles = sz.face // SUB
+    for l in range(sz.L):
+        up = jnp.zeros((SUB, sz.E), F32)
+        low = jnp.zeros((SUB, sz.E), F32)
+        for k in range(sz.FR // SUB):
+            row = (k // tiles) * sz.Q + (k % tiles) * SUB
+            up = jnp.where(slot == k, lanes_of(halo_ref[l, pl.ds(row + sz.Q - sz.face, SUB), :], last), up)
+            low = jnp.where(slot == k, lanes_of(halo_ref[l, pl.ds(row, SUB), :], first), low)
+        swap_ref[sz.half, pl.ds(l * SUB, SUB), :] = up
+        swap_ref[sz.half + 1, pl.ds(l * SUB, SUB), :] = low
+
+
+def ring_shapes(sz):
+    return [jax.ShapeDtypeStruct((sz.z_rows(j), sz.E), F32) for j in range(sz.Z)]
+
+
+def pack_ring(sz, slide_ref, halo_ref, zz, stage):
     z = spot()[1]
     for p in range(sz.Z):
         first = (p % sz.PL) * sz.CH
@@ -203,121 +245,7 @@
         zz[j][pl.ds(at, sz.CH), :] = stage[lax.rem(z + j, sz.Z)]
 
 
-def pack_space(sz, u):
-    def body(u_ref, *refs):
-        held, sem = refs[-2], refs[-1]
-        copy = pltpu.make_async_copy(u_ref, held, sem)
-        copy.start()
-        copy.wait()
-        pack_chips(sz, held, held, refs[:-3], refs[-3])
-
-    scratch = [chip_scratch(sz), pltpu.VMEM(u.shape, F32), pltpu.SemaphoreType.DMA]
-    source = pl.BlockSpec(memory_space=pltpu.HBM)
-    return call(body, chip_shapes(sz), [source], scratch, 0, 4 * u.size)(u)
-
-
-def inside_part(sz, mats, u):
-    E, pair = sz.E, 2
-
-    def body(hi_ref, lo_ref, u_ref, out_ref):
-        for l in range(0, sz.L, pair):
-            x = jnp.concatenate([u_ref[l + i] for i in range(pair)], axis=1)
-            r = dot3(hi_ref[...], lo_ref[...], x)
-            for i in range(pair):
-                out_ref[l + i] = r[:, i * E : (i + 1) * E]
-
-    out = jax.ShapeDtypeStruct(u.shape, F32)
-    return call(body, [out], [VMEM] * 3, (), 6 * sz.R * u.size, 12 * u.size)(*mats[:2], u)[0]
-
-
-def face_part(sz, neighbours, mats, u, inner, own, sibling, ahead, behind):
-    L, E, FR, Q, face = sz.L, sz.E, sz.FR, sz.Q, sz.face
-    pair = 2
-
-    def body(near_ref, ohi_ref, olo_ref, u_ref, in_ref, sib_ref, ahead_ref, behind_ref, out_ref, x_ref):
-        core = spot()[2]
-        lane = iota((SUB, E), 1)
-        index = lax.axis_index("space") * E + lane
-        total = sz.N * E
-        back = index - jnp.broadcast_to(near_ref[0:1, :], (SUB, E))
-        back = jnp.where(back < 0, back + total, back)
-        front = jnp.broadcast_to(near_ref[1:2, :], (SUB, E)) - index
-        front = jnp.where(front < 0, front + total, front)
-        own_back = (lane + E - back) % E
-        own_front = (lane + front) % E
-        from_back = lane < back
-        from_front = lane >= E - front
-        first_core = core == 0
-        tiles = face // SUB
-        for l in range(L):
-            prev_halo = jnp.where(first_core, behind_ref[pl.ds(l * SUB, SUB), :], sib_ref[pl.ds(l * SUB, SUB), :])
-            next_halo = jnp.where(
-                first_core, sib_ref[pl.ds(sz.H + l * SUB, SUB), :], ahead_ref[pl.ds(l * SUB, SUB), :]
-            )
-            for k in range(FR // SUB):
-                row = (k // tiles) * Q + (k % tiles) * SUB
-                here = lanes_of(u_ref[l, pl.ds(row + Q - face, SUB), :], own_back)
-                there = lanes_of(prev_halo, (REACH * k + REACH + lane + E - back) % E)
-                x_ref[pl.ds(k * SUB, SUB), pl.ds(l * E, E)] = jnp.where(from_back, there, here)
-                here = lanes_of(u_ref[l, pl.ds(row, SUB), :], own_front)
-                there = lanes_of(next_halo, (REACH * k + lane + front) % E)
-                x_ref[pl.ds(FR + k * SUB, SUB), pl.ds(l * E, E)] = jnp.where(from_front, there, here)
-        for l in range(0, L, pair):
-            x = x_ref[:, pl.ds(l * E, pair * E)]
-            r = dot3(ohi_ref[:, : 2 * FR], olo_ref[:, : 2 * FR], x)
-            for i in range(pair):
-                out_ref[l + i] = in_ref[l + i] + r[:, i * E : (i + 1) * E]
-
-    out = jax.ShapeDtypeStruct(u.shape, F32)
-    flops = 12 * sz.R * FR * L * E
-    ins = [VMEM] * 8
-    scratch = [pltpu.VMEM((2 * FR, L * E), F32)]
-    args = (neighbours, *mats[2:], u, inner, sibling, ahead, behind)
-    return call(body, [out], ins, scratch, flops, 12 * u.size)(*args)[0]
-
-
-def turn_time(sz, parts, damp=False, carried=()):
-    weights = [float(w) for w in time_weights(sz.T)]
-    T, L, M = sz.T, sz.L, sz.M
-    rows = parts[0].shape[1]
-    padded = -(-rows // SUB) * SUB
-    front = carried[0].shape[1] if carried else 0
-
-    def body(*refs):
-        ins, fronts, outs, x_ref, y_ref = refs[:M], refs[M : M + len(carried)], refs[-2 - M : -2], refs[-2], refs[-1]
-        me = spot()[0]
-        for j in range(len(carried)):
-            outs[j][:, pl.ds(0, front), :] = fronts[j][...]
-        for j in range(M):
-            x_ref[pl.ds((me ^ j) * L, L), pl.ds(0, rows), :] = ins[j][...]
-
-        def some(i, carry):
-            at = pl.ds(pl.multiple_of(i * SUB, SUB), SUB)
-            x = [x_ref[t, at, :] for t in range(T)]
-            diff = {}
-            for t in range(T):
-                total = None
-                for k in range(1, T // 2):
-                    a, b = (t + k) % T, (t - k) % T
-                    if (a, b) not in diff and (b, a) not in diff:
-                        diff[(a, b)] = x[a] - x[b]
-                    term = weights[k] * diff[(a, b)] if (a, b) in diff else -weights[k] * diff[(b, a)]
-                    total = term if total is None else total + term
-                y_ref[t, at, :] = x[t] - STEP * total if damp else total
-            return carry
-
-        lax.fori_loop(0, padded // SUB, some, 0)
-        for j in range(M):
-            outs[j][:, pl.ds(front, rows), :] = y_ref[pl.ds((me ^ j) * L, L), pl.ds(0, rows), :]
-
-    full = pltpu.VMEM((T, padded, sz.E), F32)
-    size = T * rows * sz.E
-    ins = [VMEM] * (M + len(carried))
-    shapes = tm_shapes(sz, front + rows)
-    return call(body, shapes, ins, [full, full], 20 * size, 8 * size)(*parts, *carried)
-
-
-def shift_slide(sz, groups, shifts, mine, theirs):
+def shift_ring(sz, groups, shifts, mine, theirs):
     Z, N, CH, E = sz.Z, sz.N, sz.CH, sz.E
 
     def body(group_ref, shift_ref, *refs):
@@ -344,11 +272,197 @@
     return call(body, [out] * Z, ins, scratch, 0, 12 * N * CH * E)(groups, shifts, *mine, *theirs)
 
 
-def slide_rows(sz, slides, stage, x_ref):
-    E, face, FR = sz.E, sz.face, sz.FR
-    z = spot()[1]
-    for j in range(sz.Z):
-        stage[lax.rem(z + sz.Z - j, sz.Z)] = slides[j][...]
+def join_cores(sz, keep, swapped):
+    def body(keep_ref, swap_ref, *outs):
+        core = spot()[2]
+        for j in range(1, sz.half):
+            out, front = outs[j - 1], sz.front(j)
+            if front:
+                out[pl.ds(0, front), :] = swap_ref[sz.half + core, pl.ds(0, front), :]
+            out[pl.ds(front, sz.CH), :] = keep_ref[j]
+            out[pl.ds(front + sz.CH, sz.CH), :] = swap_ref[j]
+
+    shapes = [jax.ShapeDtypeStruct((sz.front(j) + 2 * sz.CH, sz.E), F32) for j in range(1, sz.half)]
+    return call(body, shapes, [VMEM, VMEM], (), 0, 16 * sz.half * sz.CH * sz.E)(keep, swapped)
+
+
+def pack_space(sz, u):
+    def body(u_ref, *refs):
+        held, sem = refs[-2], refs[-1]
+        copy = pltpu.make_async_copy(u_ref, held, sem)
+        copy.start()
+        copy.wait()
+        pack_chips(sz, held, held, refs[:-3], refs[-3])
+
+    scratch = [chip_scratch(sz), pltpu.VMEM(u.shape, F32), pltpu.SemaphoreType.DMA]
+    source = pl.BlockSpec(memory_space=pltpu.HBM)
+    return call(body, chip_shapes(sz), [source], scratch, 0, 4 * u.size)(u)
+
+
+def inside_part(sz, mats, u):
+    E, pair = sz.E, 2
+
+    def body(hi_ref, lo_ref, u_ref, out_ref):
+        for l in range(0, sz.L, pair):
+            x = jnp.concatenate([u_ref[l + i] for i in range(pair)], axis=1)
+            r = dot3(hi_ref[...], lo_ref[...], x)
+            for i in range(pair):
+                out_ref[l + i] = r[:, i * E : (i + 1) * E]
+
+    out = jax.ShapeDtypeStruct(u.shape, F32)
+    return call(body, [out], [VMEM] * 3, (), 6 * sz.R * u.size, 12 * u.size)(*mats[:2], u)[0]
+
+
+def face_part(sz, neighbours, mats, u, inner, *halos):
+    L, E, FR, Q, face = sz.L, sz.E, sz.FR, sz.Q, sz.face
+    pair = 2
+
+    def body(near_ref, ohi_ref, olo_ref, u_ref, in_ref, *refs):
+        halo_refs, out_ref, x_ref = refs[:-2], refs[-2], refs[-1]
+        core = spot()[2]
+        lane = iota((SUB, E), 1)
+        index = lax.axis_index("space") * E + lane
+        total = sz.N * E
+        back = index - jnp.broadcast_to(near_ref[0:1, :], (SUB, E))
+        back = jnp.where(back < 0, back + total, back)
+        front = jnp.broadcast_to(near_ref[1:2, :], (SUB, E)) - index
+        front = jnp.where(front < 0, front + total, front)
+        own_back = (lane + E - back) % E
+        own_front = (lane + front) % E
+        from_back = lane < back
+        from_front = lane >= E - front
+        first_core = core == 0
+        tiles = face // SUB
+        for l in range(L):
+            at = pl.ds(l * SUB, SUB)
+            if len(halo_refs) == 2:
+                swap_ref, halo_ref = halo_refs
+                prev_halo = jnp.where(first_core, halo_ref[at, :], swap_ref[sz.half, at, :])
+                next_halo = jnp.where(first_core, swap_ref[sz.half + 1, at, :], halo_ref[at, :])
+            else:
+                sib_ref, ahead_ref, behind_ref = halo_refs
+                prev_halo = jnp.where(first_core, behind_ref[at, :], sib_ref[at, :])
+                next_halo = jnp.where(first_core, sib_ref[pl.ds(sz.H + l * SUB, SUB), :], ahead_ref[at, :])
+            for k in range(FR // SUB):
+                row = (k // tiles) * Q + (k % tiles) * SUB
+                here = lanes_of(u_ref[l, pl.ds(row + Q - face, SUB), :], own_back)
+                there = lanes_of(prev_halo, (REACH * k + REACH + lane + E - back) % E)
+                x_ref[pl.ds(k * SUB, SUB), pl.ds(l * E, E)] = jnp.where(from_back, there, here)
+                here = lanes_of(u_ref[l, pl.ds(row, SUB), :], own_front)
+                there = lanes_of(next_halo, (REACH * k + lane + front) % E)
+                x_ref[pl.ds(FR + k * SUB, SUB), pl.ds(l * E, E)] = jnp.where(from_front, there, here)
+        for l in range(0, L, pair):
+            x = x_ref[:, pl.ds(l * E, pair * E)]
+            r = dot3(ohi_ref[:, : 2 * FR], olo_ref[:, : 2 * FR], x)
+            for i in range(pair):
+                out_ref[l + i] = in_ref[l + i] + r[:, i * E : (i + 1) * E]
+
+    out = jax.ShapeDtypeStruct(u.shape, F32)
+    flops = 12 * sz.R * FR * L * E
+    ins = [VMEM] * (5 + len(halos))
+    scratch = [pltpu.VMEM((2 * FR, L * E), F32)]
+    args = (neighbours, *mats[2:], u, inner, *halos)
+    return call(body, [out], ins, scratch, flops, 12 * u.size)(*args)[0]
+
+
+def turn_time(sz, parts, damp=False, carried=()):
+    weights = [float(w) for w in time_weights(sz.T)]
+    T, L, M = sz.T, sz.L, sz.M
+    rows = parts[0].shape[1]
+    padded = -(-rows // SUB) * SUB
+    front = carried[0].shape[1] if carried else 0
+
+    def body(*refs):
+        ins, fronts, outs, x_ref, y_ref = refs[:M], refs[M : M + len(carried)], refs[-2 - M : -2], refs[-2], refs[-1]
+        me = spot()[0]
+        for j in range(len(carried)):
+            outs[j][:, pl.ds(0, front), :] = fronts[j][...]
+        for j in range(M):
+            x_ref[pl.ds((me ^ j) * L, L), pl.ds(0, rows), :] = ins[j][...]
+
+        def some(i, carry):
+            at = pl.ds(pl.multiple_of(i * SUB, SUB), SUB)
+            x = [x_ref[t, at, :] for t in range(T)]
+            diff = {}
+            for t in range(T):
+                total = None
+                for k in range(1, T // 2):
+                    a, b = (t + k) % T, (t - k) % T
+                    if (a, b) not in diff and (b, a) not in diff:
+                        diff[(a, b)] = x[a] - x[b]
+                    term = weights[k] * diff[(a, b)] if (a, b) in diff else -weights[k] * diff[(b, a)]
+                    total = term if total is None else total + term
+                y_ref[t, at, :] = x[t] - STEP * total if damp else total
+            return carry
+
+        lax.fori_loop(0, padded // SUB, some, 0)
+        for j in range(M):
+            outs[j][:, pl.ds(front, rows), :] = y_ref[pl.ds((me ^ j) * L, L), pl.ds(0, rows), :]
+
+    full = pltpu.VMEM((T, padded, sz.E), F32)
+    size = T * rows * sz.E
+    ins = [VMEM] * (M + len(carried))
+    shapes = tm_shapes(sz, front + rows)
+    return call(body, shapes, ins, [full, full], 20 * size, 8 * size)(*parts, *carried)
+
+
+def shift_slide(sz, groups, shifts, keep, swapped, mine, theirs):
+    Z, N, CH, E, half = sz.Z, sz.N, sz.CH, sz.E, sz.half
+
+    def body(group_ref, shift_ref, keep_ref, swap_ref, *refs):
+        a, b, outs, x_ref = refs[:half], refs[half : 2 * half], refs[2 * half : -1], refs[-1]
+        _, z, core = spot()
+        other = 1 - core
+        l = z // sz.PL
+        group, shift = group_ref[l], shift_ref[l]
+        x_ref[2 * z + core] = keep_ref[0]
+        x_ref[2 * z + other] = swap_ref[0]
+        for j in range(1, half):
+            one, two = pl.ds(sz.front(j), CH), pl.ds(sz.front(j) + CH, CH)
+            chip = sz.ahead(z, other, j)
+            x_ref[2 * chip + core] = a[j - 1][one, :]
+            x_ref[2 * chip + other] = a[j - 1][two, :]
+            chip = sz.ahead(z, core, j)
+            x_ref[2 * chip + other] = b[j - 1][one, :]
+            x_ref[2 * chip + core] = b[j - 1][two, :]
+        far = lax.rem(z + half, Z)
+        x_ref[2 * far + core] = a[half - 1][...]
+        x_ref[2 * far + other] = b[half - 1][...]
+        lane = iota((CH, E), 1)
+        index = (lane + shift) % E
+
+        def block(chip, which):
+            first = 2 * chip + which + group
+            near = x_ref[lax.rem(first, N)]
+            return lanes_of(jnp.where(lane < shift, x_ref[lax.rem(first + 1, N)], near), index)
+
+        outs[0][...] = block(z, core)
+        for j in range(1, half):
+            chip = sz.ahead(z, core, j)
+            outs[j][pl.ds(0, CH), :] = block(chip, core)
+            outs[j][pl.ds(CH, CH), :] = block(chip, other)
+        outs[half][...] = block(far, core)
+
+    single = jax.ShapeDtypeStruct((CH, E), F32)
+    double = jax.ShapeDtypeStruct((2 * CH, E), F32)
+    ins = [SMEM, SMEM] + [VMEM] * (2 + 2 * half)
+    scratch = [pltpu.VMEM((N, CH, E), F32)]
+    outs = [single] + [double] * (half - 1) + [single]
+    return call(body, outs, ins, scratch, 0, 12 * N * CH * E)(groups, shifts, keep, swapped, *mine, *theirs)
+
+
+def slide_rows(sz, slides, stage, x_ref, ring=False):
+    E, face, FR, half = sz.E, sz.face, sz.FR, sz.half
+    _, z, core = spot()
+    if ring:
+        for j in range(1, sz.Z):
+            stage[lax.rem(z + sz.Z - j, sz.Z)] = slides[j][...]
+    stage[z] = slides[0][...]
+    for j in range(1, 0 if ring else half):
+        stage[sz.ahead(z, 1 - core, j)] = slides[j][pl.ds(0, sz.CH), :]
+        stage[sz.ahead(z, core, j)] = slides[half + j][pl.ds(sz.CH, sz.CH), :]
+    if not ring:
+        stage[lax.rem(z + half, sz.Z)] = slides[half][...]
     for l in range(sz.L):
         slide = [stage[l * sz.PL + i] for i in range(sz.PL)]
         slide = slide[0] if sz.PL == 1 else jnp.concatenate(slide, axis=0)
@@ -403,12 +517,12 @@
             new = c_ref[l] - t
             u_ref[l] = new
             v_ref[l] = new - t
-        pack_chips(sz, u_ref, v_ref, zz, stage)
+        pack_ring(sz, u_ref, v_ref, zz, stage)
 
     full = jax.ShapeDtypeStruct(partial.shape, F32)
     scratch = [pltpu.VMEM(partial.shape, F32), chip_scratch(sz)]
     ins = [VMEM] * (1 + sz.M)
-    done = call(body, [full, full] + chip_shapes(sz), ins, scratch, 0, 16 * partial.size)(partial, *times)
+    done = call(body, [full, full] + ring_shapes(sz), ins, scratch, 0, 16 * partial.size)(partial, *times)
     return done[0], done[1], done[2:]
 
 
@@ -425,7 +539,7 @@
         for j in range(M):
             t_ref[me ^ j] = time_refs[j][:, pl.ds(0, sz.RC), :]
             cut_ref[me ^ j] = time_refs[j][:, pl.ds(sz.RC, CR), :]
-        slide_rows(sz, slide_refs, stage, x_ref)
+        slide_rows(sz, slide_refs, stage, x_ref, ring=True)
         for l in range(L):
             for m in range(M):
                 x_ref[pl.ds(m * CR, CR), pl.ds(l * E, E)] -= STEP * cut_ref[m, l]
@@ -453,6 +567,12 @@
 
 def over_chips(x, j):
     size = lax.axis_size("space")
+    pairs = [(i, (i + (2 * j if i % 2 == 0 else -2 * j)) % size) for i in range(size)]
+    return lax.ppermute(x, "space", pairs)
+
+
+def over_ring(x, j):
+    size = lax.axis_size("space")
     return lax.ppermute(x, "space", [(i, (i + 2 * j) % size) for i in range(size)])
 
 
@@ -468,37 +588,38 @@
     def time_trip(parts):
         return [parts[0]] + [over_tm(parts[j], j) for j in range(1, sz.M)]
 
-    def chip_trip(parts):
-        return [parts[0]] + [over_chips(parts[j], j) for j in range(1, sz.Z)]
-
-    def faces(field, inner, mine, theirs):
-        return face_part(sz, face_neighbours, mats, field, inner, mine[0], theirs[0], theirs[sz.Z - 1], theirs[1])
+    def ring_trip(parts):
+        return [parts[0]] + [over_ring(parts[j], j) for j in range(1, sz.Z)]
 
     chunks = pack_time(sz, u)
     parts = time_trip(chunks)
-    packed = pack_space(sz, after(u, chunks[0]))
-    mats = matrices(sz, after(flux_matrix, packed[0]), volume_operator)
-    packed = [*packed[:-1], after(packed[-1], mats[0])]
-    mine = chip_trip(packed)
+    swap, keep, far = pack_space(sz, after(u, chunks[0]))
+    swapped = over_cores(swap)
+    joined = join_cores(sz, keep, swapped)
+    mine = [over_chips(joined[j - 1], j) for j in range(1, sz.half)] + [over_chips(far, sz.half)]
+    mats = matrices(sz, after(flux_matrix, joined[0]), volume_operator)
     inner = inside_part(sz, mats, u)
-    turned = turn_time(sz, after(parts, inner))
+    theirs = [over_cores(x) for x in after(mine, inner)]
+    shifted = shift_slide(sz, counterpart_group, counterpart_shift, keep, swapped, mine, theirs)
+    slides = [shifted[0]] + [over_chips(shifted[j], j) for j in range(1, sz.half + 1)]
+    slides += [over_cores(x) for x in slides[1 : sz.half]]
+    turned = turn_time(sz, after(parts, shifted[0]))
     times = time_trip(turned)
-    theirs = [over_cores(x) for x in mine[:1] + after(mine[1:], turned[0])]
-    shifted = shift_slide(sz, counterpart_group, counterpart_shift, mine, theirs)
-    slides = chip_trip(shifted)
-    here = faces(after(u, shifted[0]), inner, mine, theirs)
+    here = face_part(sz, face_neighbours, mats, after(u, turned[0]), inner, swapped, mine[0])
     damped = turn_time(sz, after(turned, here), damp=True)
     partial, cuts = first_slide(sz, mats, u, after(here, damped), slides)
     cut_parts = time_trip(cuts)
     u, v, packed = first_step(sz, partial, times)
-    mine = chip_trip(packed)
+    mine = ring_trip(packed)
     inner = inside_part(sz, mats, v)
     both = turn_time(sz, after(cut_parts, inner), carried=damped)
     times = time_trip(both)
     theirs = [over_cores(x) for x in mine[:1] + after(mine[1:], both[0])]
-    shifted = shift_slide(sz, counterpart_group, counterpart_shift, mine, theirs)
-    slides = chip_trip(shifted)
-    here = faces(after(v, shifted[0]), inner, mine, theirs)
+    shifted = shift_ring(sz, counterpart_group, counterpart_shift, mine, theirs)
+    slides = ring_trip(shifted)
+    here = face_part(
+        sz, face_neighbours, mats, after(v, shifted[0]), inner, theirs[0], theirs[sz.Z - 1], theirs[1]
+    )
     new, residual = last_step(sz, mats, u, here, times, slides)
     shape = conserved_field.shape
     return new.reshape(shape), residual.reshape(shape)

time: 76.7 us -> 74.1 us (0.966)
  starting transfers between devices: 37.3 us -> 28.9 us
  waiting for transfers between devices: 18 us -> 23.8 us
    ppermute x12 -> x10, starting transfers between devices: 20.5 us -> 12.4 us  [the longest x4 6.81 us: over_chips(): return lax.ppermute(x, 'space', pairs)]
    ppermute x12, waiting for transfers between devices: 5.54 us -> 8.6 us  [over_tm(): return lax.ppermute(x, 'tm', [(i, i ^ j) for i in range(size)])]
    ppermute x8, waiting for transfers between devices: 1.77 us -> 4.04 us  [over_cores(): return lax.ppermute(x, 'space', [(i, i ^ 1) for i in range(size)])]
    ppermute x12 -> x10, waiting for transfers between devices: 10.7 us -> 11.2 us  [the longest x6 8.34 us: over_ring(): lax.ppermute(x, 'space', [(i, (i + 2 * j) % size) for i in range(size)])]
    pallas_call x3 -> x4, Pallas kernels: 1.95 us -> 1.96 us  [the longest x1 0.75 us: shift_slide(): call(body, outs, ins, scratch, 0, 12 * N * CH * E)]
  transfers between devices with their start and end apart: 32 -> 30, of which waited for: 8 -> 14; matrix products, arithmetic and copies ran while one was open for 0% -> 0% of each run, Pallas kernels for 21% -> 22%
where the time goes in v3:
time: 74.1 us; the launch traced here: 73.9 us
  starting transfers between devices  28.9 us (39%)
  waiting for transfers between devices  23.8 us (32%)
  Pallas kernels  19 us (26%)
  local copies, waits for them, and re-layouts  1.35 us (2%)
  between operations  0.87 us (1%)
    ppermute x12, starting transfers between devices, over_tm(): return lax.ppermute(x, 'tm', [(i, i ^ j) for i in range(size)])  14.4 us
    ppermute x12, waiting for transfers between devices, over_tm(): return lax.ppermute(x, 'tm', [(i, i ^ j) for i in range(size)])  8.6 us
    ppermute x6, waiting for transfers between devices, over_ring(): lax.ppermute(x, 'space', [(i, (i + 2 * j) % size) for i in range(size)])  8.34 us
    ppermute x4, starting transfers between devices, over_chips(): return lax.ppermute(x, 'space', pairs)  6.81 us
    ppermute x6, starting transfers between devices, over_ring(): lax.ppermute(x, 'space', [(i, (i + 2 * j) % size) for i in range(size)])  5.55 us
    ppermute x8, waiting for transfers between devices, over_cores(): return lax.ppermute(x, 'space', [(i, i ^ 1) for i in range(size)])  4.04 us
    pallas_call x2, Pallas kernels, face_part(): return call(body, [out], ins, scratch, flops, 12 * u.size)(*args)[0]  3.7 us
    pallas_call x1, Pallas kernels, matrices(): call(body, [inner, inner, outer, outer], [SMEM, VMEM], (), nbytes, nbytes)  3.52 us
  transfers between devices with their start and end apart: 30, of which 14 were waited for; matrix products, arithmetic and copies ran while one was open for 0% of the time, Pallas kernels for 22%

profile of v3, /device:TPU:0, one launch (start us, length us, event | category | flops | bytes accessed | tf_op | source)
XLA Modules:
  0.0 73.9 jit_solution(15977916794915983509)
XLA Ops:
  0.6 0.0 copy-start
  0.6 1.3 %copy-done = f32[4,10,64,128]{3,2,1,0:T(8,128)S(1)} copy-done((f32[4,10,64,128]{3,2,1,0:T(8,128)S(1)}, f32[4,10,64,128]{3,2,1,0:T(8,128)}, u32[]{:S(2)}) %copy-start) | copy-done | bytes 1310744
  1.9 0.2 shard_map.77
  2.2 0.0 copy-start.6
  2.2 0.0 copy-start.2
  2.2 0.4 shard_map.78
  2.6 0.5 collective-permute-start
  3.1 1.3 %collective-permute-done.swap_ref.refs_0_ = f32[4,160,128]{2,1,0:T(8,128)S(1)} collective-permute-done((f32[4,160,128]{2,1,0:T(8,128)S(1)}, f32[4,160,128]{2,1,0:T(8,128)S(1)}, u32[]{:S(2)}, u32[]{:S(2)}) %collective-permute-start) | collective-permute-done | bytes 327712 | tf_op jit(solution)/shard_map/ppermute | solution.py:581
  4.4 3.0 %collective-permute-start.4 = (f32[352,128]{1,0:T(8,128)S(1)}, f32[352,128]{1,0:T(8,128)S(1)}, u32[]{:S(2)}, u32[]{:S(2)}) collective-permute-start(f32[352,128]{1,0:T(8,128)S(1)} %shard_map.79), channel_id=1, source_target_pairs={{0,2},{1,7},{2,4},{3,1},{4,6},{5,3},{6,0},{7,5},{8,10},{9,15},{10,... | collective-permute-start | bytes 540680 | tf_op jit(solution)/shard_map/ppermute | solution.py:571
  7.4 1.5 %collective-permute-start.1 = (f32[4,160,128]{2,1,0:T(8,128)S(1)}, f32[4,160,128]{2,1,0:T(8,128)S(1)}, u32[]{:S(2)}, u32[]{:S(2)}) collective-permute-start(f32[4,160,128]{2,1,0:T(8,128)S(1)} %get-tuple-element.74), channel_id=1, source_target_pairs={{0,8},{8,0},{16,24},{24,16},{1,9},{9,1},{17,25},{25,17},{2,10},{10... | collective-permute-start | bytes 983048 | tf_op jit(solution)/shard_map/ppermute | solution.py:565
  8.9 1.5 %collective-permute-start.2 = (f32[4,160,128]{2,1,0:T(8,128)S(1)}, f32[4,160,128]{2,1,0:T(8,128)S(1)}, u32[]{:S(2)}, u32[]{:S(2)}) collective-permute-start(f32[4,160,128]{2,1,0:T(8,128)S(1)} %get-tuple-element.75), channel_id=1, source_target_pairs={{0,16},{8,24},{16,0},{24,8},{1,17},{9,25},{17,1},{25,9},{2,18},{10... | collective-permute-start | bytes 983048 | tf_op jit(solution)/shard_map/ppermute | solution.py:565
  10.4 0.5 collective-permute-start.3
  10.9 2.6 %collective-permute-start.5 = (f32[160,128]{1,0:T(8,128)S(1)}, f32[160,128]{1,0:T(8,128)S(1)}, u32[]{:S(2)}, u32[]{:S(2)}) collective-permute-start(f32[160,128]{1,0:T(8,128)S(1)} %get-tuple-element.77), channel_id=1, source_target_pairs={{0,4},{1,5},{2,6},{3,7},{4,0},{5,1},{6,2},{7,3},{8,12},{9,13},{10,... | collective-permute-start | bytes 245768 | tf_op jit(solution)/shard_map/ppermute | solution.py:571
  13.5 3.5 %shard_map.80 = (bf16[640,640]{1,0:T(8,128)(2,1)S(1)}, bf16[640,640]{1,0:T(8,128)(2,1)S(1)}, bf16[640,480]{1,0:T(8,128)(2,1)S(1)}, bf16[640,480]{1,0:T(8,128)(2,1)S(1)}) custom-call(f32[2,10,10]{2,1,0:T(8,128)S(1)} %copy.8.flux_ref, f32[2,64,64]{2,1,0:T(8,128)S(1)} %copy-done.2), custom_call_target="tpu_custom_call" | custom-call | flops 2867200 | bytes 2867200 | tf_op jit(solution)/shard_map/pallas_call | solution.py:152
  17.0 0.0 copy-start.4
  17.0 0.0 copy-start.5
  17.0 1.7 %shard_map.81.in_ref = f32[4,640,128]{2,1,0:T(8,128)S(1)} custom-call(bf16[640,640]{1,0:T(8,128)(2,1)S(1)} %get-tuple-element.78.hi_ref, bf16[640,640]{1,0:T(8,128)(2,1)S(1)} %get-tuple-element.79.lo_ref, f32[4,640,128]{2,1,0:T(8,128)S(1)} %bitcast.5), custom_call_target="tpu_custom_call" | custom-call | flops 1258291200 | bytes 3932160 | tf_op jit(solution)/shard_map/pallas_call | solution.py:313
  18.7 0.0 copy-start.3
  18.8 0.1 collective-permute-start.6
  18.8 0.5 collective-permute-start.7
  19.3 1.0 %collective-permute-done.7.refs_3_ = f32[160,128]{1,0:T(8,128)S(1)} collective-permute-done((f32[160,128]{1,0:T(8,128)S(1)}, f32[160,128]{1,0:T(8,128)S(1)}, u32[]{:S(2)}, u32[]{:S(2)}) %collective-permute-start.7) | collective-permute-done | bytes 81952 | tf_op jit(solution)/shard_map/ppermute | solution.py:581
  20.4 0.7 %shard_map.82 = (f32[160,128]{1,0:T(8,128)S(1)}, f32[320,128]{1,0:T(8,128)S(1)}, f32[160,128]{1,0:T(8,128)S(1)}) custom-call(s32[4]{0:T(128)S(1)} %copy-done.4, s32[4]{0:T(128)S(1)} %copy-done.5, f32[2,160,128]{2,1,0:T(8,128)S(1)} %get-tuple-element.69.keep_ref, f32[4,160,128]{2,1,0:T(8,128)S(1)} %collective-permute-done.swap_ref.refs_0_, ...), custom_call_target="tpu_custom_call" | custom-call | bytes 1966080 | tf_op jit(solution)/shard_map/pallas_call | solution.py:451
  21.1 0.1 collective-permute-start.8
  21.3 3.7 %collective-permute-done.2.refs_2_ = f32[4,160,128]{2,1,0:T(8,128)S(1)} collective-permute-done((f32[4,160,128]{2,1,0:T(8,128)S(1)}, f32[4,160,128]{2,1,0:T(8,128)S(1)}, u32[]{:S(2)}, u32[]{:S(2)}) %collective-permute-start.2) | collective-permute-done | bytes 327712 | tf_op jit(solution)/shard_map/ppermute | solution.py:565
  24.9 0.2 collective-permute-done.3.refs_3_
  25.1 1.1 %shard_map.83 = (f32[4,160,128]{2,1,0:T(8,128)S(1)}, f32[4,160,128]{2,1,0:T(8,128)S(1)}, f32[4,160,128]{2,1,0:T(8,128)S(1)}, f32[4,160,128]{2,1,0:T(8,128)S(1)}) custom-call(f32[4,160,128]{2,1,0:T(8,128)S(1)} %get-tuple-element.83.refs_0_, f32[4,160,128]{2,1,0:T(8,128)S(1)} %collective-permute-done.1.refs_1_, ...), custom_call_target="tpu_custom_call" | custom-call | flops 6553600 | bytes 2621440 | tf_op jit(solution)/shard_map/pallas_call | solution.py:406
  26.2 1.5 %collective-permute-start.11 = (f32[4,160,128]{2,1,0:T(8,128)S(1)}, f32[4,160,128]{2,1,0:T(8,128)S(1)}, u32[]{:S(2)}, u32[]{:S(2)}) collective-permute-start(f32[4,160,128]{2,1,0:T(8,128)S(1)} %get-tuple-element.93.refs_1_), channel_id=1, source_target_pairs={{0,8},{8,0},{16,24},{24,16},{1,9},{9,1},{17,25},{25,17},{2,10},{10... | collective-permute-start | bytes 983048 | tf_op jit(solution)/shard_map/ppermute | solution.py:565
  27.7 1.0 %collective-permute-start.12 = (f32[4,160,128]{2,1,0:T(8,128)S(1)}, f32[4,160,128]{2,1,0:T(8,128)S(1)}, u32[]{:S(2)}, u32[]{:S(2)}) collective-permute-start(f32[4,160,128]{2,1,0:T(8,128)S(1)} %get-tuple-element.94.refs_2_), channel_id=1, source_target_pairs={{0,16},{8,24},{16,0},{24,8},{1,17},{9,25},{17,1},{25,9},{2,18},{10... | collective-permute-start | bytes 983048 | tf_op jit(solution)/shard_map/ppermute | solution.py:565
  28.7 1.4 %collective-permute-start.13 = (f32[4,160,128]{2,1,0:T(8,128)S(1)}, f32[4,160,128]{2,1,0:T(8,128)S(1)}, u32[]{:S(2)}, u32[]{:S(2)}) collective-permute-start(f32[4,160,128]{2,1,0:T(8,128)S(1)} %get-tuple-element.95.refs_3_), channel_id=1, source_target_pairs={{0,24},{8,16},{16,8},{24,0},{1,25},{9,17},{17,9},{25,1},{2,26},{10... | collective-permute-start | bytes 983048 | tf_op jit(solution)/shard_map/ppermute | solution.py:565
  30.1 0.1 collective-permute-start.10
  30.1 1.1 %collective-permute-start.9 = (f32[160,128]{1,0:T(8,128)S(1)}, f32[160,128]{1,0:T(8,128)S(1)}, u32[]{:S(2)}, u32[]{:S(2)}) collective-permute-start(f32[160,128]{1,0:T(8,128)S(1)} %get-tuple-element.102), channel_id=1, source_target_pairs={{0,4},{1,5},{2,6},{3,7},{4,0},{5,1},{6,2},{7,3},{8,12},{9,13},{10,... | collective-permute-start | bytes 245768 | tf_op jit(solution)/shard_map/ppermute | solution.py:571
  31.2 1.9 %shard_map.84.w_ref = f32[4,640,128]{2,1,0:T(8,128)S(1)} custom-call(s32[2,128]{1,0:T(2,128)S(1)} %copy-done.3, bf16[640,480]{1,0:T(8,128)(2,1)S(1)} %get-tuple-element.72.ohi_ref, bf16[640,480]{1,0:T(8,128)(2,1)S(1)} %get-tuple-element.73.olo_ref, f32[4,640,128]{2,1,0:T(8,128)S(1)} %bitcast.6, f32[4,640,128]{2,1,0:T(8,128)S(1)} %shard_map.81.in_ref, ...), custom_call_target="tpu_custom_call" | custom-call | flops 629145600 | bytes 3932160 | tf_op jit(solution)/shard_map/pallas_call | solution.py:365
  33.1 1.2 %shard_map.85 = (f32[4,160,128]{2,1,0:T(8,128)S(1)}, f32[4,160,128]{2,1,0:T(8,128)S(1)}, f32[4,160,128]{2,1,0:T(8,128)S(1)}, f32[4,160,128]{2,1,0:T(8,128)S(1)}) custom-call(f32[4,160,128]{2,1,0:T(8,128)S(1)} %get-tuple-element.92.refs_0_, f32[4,160,128]{2,1,0:T(8,128)S(1)} %get-tuple-element.93.refs_1_, f32[4,160,128]{2,1,0:T(8,128)S(1)} %get-tuple-element.94.refs_2_, ...), custom_call_target="tpu_custom_call" | custom-call | flops 6553600 | bytes 2621440 | tf_op jit(solution)/shard_map/pallas_call | solution.py:406
  34.3 2.8 %collective-permute-done.9.refs_2_ = f32[160,128]{1,0:T(8,128)S(1)} collective-permute-done((f32[160,128]{1,0:T(8,128)S(1)}, f32[160,128]{1,0:T(8,128)S(1)}, u32[]{:S(2)}, u32[]{:S(2)}) %collective-permute-start.9) | collective-permute-done | bytes 81952 | tf_op jit(solution)/shard_map/ppermute | solution.py:571
  37.1 0.8 %shard_map.86 = (f32[4,640,128]{2,1,0:T(8,128)S(1)}, f32[4,40,128]{2,1,0:T(8,128)S(1)}, f32[4,40,128]{2,1,0:T(8,128)S(1)}, f32[4,40,128]{2,1,0:T(8,128)S(1)}, f32[4,40,128]{2,1,0:T(8,128)S(1)}) custom-call(bf16[640,480]{1,0:T(8,128)(2,1)S(1)} %get-tuple-element.72.ohi_ref, bf16[640,480]{1,0:T(8,128)(2,1)S(1)} %get-tuple-element.73.olo_ref, ...), custom_call_target="tpu_custom_call" | custom-call | flops 314572800 | bytes 3932160 | tf_op jit(solution)/shard_map/pallas_call | solution.py:506
  37.9 1.3 %collective-permute-start.18 = (f32[4,40,128]{2,1,0:T(8,128)S(1)}, f32[4,40,128]{2,1,0:T(8,128)S(1)}, u32[]{:S(2)}, u32[]{:S(2)}) collective-permute-start(f32[4,40,128]{2,1,0:T(8,128)S(1)} %get-tuple-element.111), channel_id=1, source_target_pairs={{0,8},{8,0},{16,24},{24,16},{1,9},{9,1},{17,25},{25,17},{2,10},{10... | collective-permute-start | bytes 245768 | tf_op jit(solution)/shard_map/ppermute | solution.py:565
  39.2 0.8 %collective-permute-start.19 = (f32[4,40,128]{2,1,0:T(8,128)S(1)}, f32[4,40,128]{2,1,0:T(8,128)S(1)}, u32[]{:S(2)}, u32[]{:S(2)}) collective-permute-start(f32[4,40,128]{2,1,0:T(8,128)S(1)} %get-tuple-element.112), channel_id=1, source_target_pairs={{0,16},{8,24},{16,0},{24,8},{1,17},{9,25},{17,1},{25,9},{2,18},{10... | collective-permute-start | bytes 245768 | tf_op jit(solution)/shard_map/ppermute | solution.py:565
  40.0 1.4 %collective-permute-start.20 = (f32[4,40,128]{2,1,0:T(8,128)S(1)}, f32[4,40,128]{2,1,0:T(8,128)S(1)}, u32[]{:S(2)}, u32[]{:S(2)}) collective-permute-start(f32[4,40,128]{2,1,0:T(8,128)S(1)} %get-tuple-element.113), channel_id=1, source_target_pairs={{0,24},{8,16},{16,8},{24,0},{1,25},{9,17},{17,9},{25,1},{2,26},{10... | collective-permute-start | bytes 245768 | tf_op jit(solution)/shard_map/ppermute | solution.py:565
  41.5 2.1 %collective-permute-done.12.refs_2_ = f32[4,160,128]{2,1,0:T(8,128)S(1)} collective-permute-done((f32[4,160,128]{2,1,0:T(8,128)S(1)}, f32[4,160,128]{2,1,0:T(8,128)S(1)}, u32[]{:S(2)}, u32[]{:S(2)}) %collective-permute-start.12) | collective-permute-done | bytes 327712 | tf_op jit(solution)/shard_map/ppermute | solution.py:565
  43.6 2.0 %collective-permute-done.13.refs_3_ = f32[4,160,128]{2,1,0:T(8,128)S(1)} collective-permute-done((f32[4,160,128]{2,1,0:T(8,128)S(1)}, f32[4,160,128]{2,1,0:T(8,128)S(1)}, u32[]{:S(2)}, u32[]{:S(2)}) %collective-permute-start.13) | collective-permute-done | bytes 327712 | tf_op jit(solution)/shard_map/ppermute | solution.py:565
  45.6 0.5 shard_map.87
  46.1 0.2 collective-permute-start.15
  46.3 3.0 %collective-permute-start.14 = (f32[192,128]{1,0:T(8,128)S(1)}, f32[192,128]{1,0:T(8,128)S(1)}, u32[]{:S(2)}, u32[]{:S(2)}) collective-permute-start(f32[192,128]{1,0:T(8,128)S(1)} %get-tuple-element.107), channel_id=1, source_target_pairs={{0,2},{1,3},{2,4},{3,5},{4,6},{5,7},{6,0},{7,1},{8,10},{9,11},{10,... | collective-permute-start | bytes 294920 | tf_op jit(solution)/shard_map/ppermute | solution.py:576
  49.3 0.8 %collective-permute-start.16 = (f32[192,128]{1,0:T(8,128)S(1)}, f32[192,128]{1,0:T(8,128)S(1)}, u32[]{:S(2)}, u32[]{:S(2)}) collective-permute-start(f32[192,128]{1,0:T(8,128)S(1)} %get-tuple-element.109), channel_id=1, source_target_pairs={{0,6},{1,7},{2,0},{3,1},{4,2},{5,3},{6,4},{7,5},{8,14},{9,15},{10,... | collective-permute-start | bytes 294920 | tf_op jit(solution)/shard_map/ppermute | solution.py:576
  50.1 1.7 %shard_map.88.in_ref = f32[4,640,128]{2,1,0:T(8,128)S(1)} custom-call(bf16[640,640]{1,0:T(8,128)(2,1)S(1)} %get-tuple-element.78.hi_ref, bf16[640,640]{1,0:T(8,128)(2,1)S(1)} %get-tuple-element.79.lo_ref, f32[4,640,128]{2,1,0:T(8,128)S(1)} %get-tuple-element.123.u_ref), custom_call_target="tpu_custom_call" | custom-call | flops 1258291200 | bytes 3932160 | tf_op jit(solution)/shard_map/pallas_call | solution.py:313
  51.8 0.4 shard_map.89
  52.2 0.3 collective-permute-start.24
  52.5 2.2 %collective-permute-start.25 = (f32[4,200,128]{2,1,0:T(8,128)S(1)}, f32[4,200,128]{2,1,0:T(8,128)S(1)}, u32[]{:S(2)}, u32[]{:S(2)}) collective-permute-start(f32[4,200,128]{2,1,0:T(8,128)S(1)} %get-tuple-element.125), channel_id=1, source_target_pairs={{0,16},{8,24},{16,0},{24,8},{1,17},{9,25},{17,1},{25,9},{2,18},{10... | collective-permute-start | bytes 1228808 | tf_op jit(solution)/shard_map/ppermute | solution.py:565
  54.7 1.0 %collective-permute-start.26 = (f32[4,200,128]{2,1,0:T(8,128)S(1)}, f32[4,200,128]{2,1,0:T(8,128)S(1)}, u32[]{:S(2)}, u32[]{:S(2)}) collective-permute-start(f32[4,200,128]{2,1,0:T(8,128)S(1)} %get-tuple-element.126), channel_id=1, source_target_pairs={{0,24},{8,16},{16,8},{24,0},{1,25},{9,17},{17,9},{25,1},{2,26},{10... | collective-permute-start | bytes 1228808 | tf_op jit(solution)/shard_map/ppermute | solution.py:565
  55.8 0.5 collective-permute-start.22
  56.3 0.8 %collective-permute-done.17.refs_4_.refs_0_ = f32[224,128]{1,0:T(8,128)S(1)} collective-permute-done((f32[224,128]{1,0:T(8,128)S(1)}, f32[224,128]{1,0:T(8,128)S(1)}, u32[]{:S(2)}, u32[]{:S(2)}) %collective-permute-start.17) | collective-permute-done | bytes 114720 | tf_op jit(solution)/shard_map/ppermute | solution.py:581
  57.1 0.2 collective-permute-start.21
  57.2 0.4 collective-permute-start.23
  57.6 0.8 %collective-permute-done.21.refs_5_.refs_2_ = f32[192,128]{1,0:T(8,128)S(1)} collective-permute-done((f32[192,128]{1,0:T(8,128)S(1)}, f32[192,128]{1,0:T(8,128)S(1)}, u32[]{:S(2)}, u32[]{:S(2)}) %collective-permute-start.21) | collective-permute-done | bytes 98336 | tf_op jit(solution)/shard_map/ppermute | solution.py:581
  58.4 0.2 collective-permute-done.23.refs_7_.refs_1_
  58.6 0.7 %shard_map.90 = (f32[160,128]{1,0:T(8,128)S(1)}, f32[160,128]{1,0:T(8,128)S(1)}, f32[160,128]{1,0:T(8,128)S(1)}, f32[160,128]{1,0:T(8,128)S(1)}) custom-call(s32[4]{0:T(128)S(1)} %copy-done.4, s32[4]{0:T(128)S(1)} %copy-done.5, f32[224,128]{1,0:T(8,128)S(1)} %get-tuple-element.106.refs_0_, f32[192,128]{1,0:T(8,128)S(1)} %collective-permute-done.14.refs_1_, ...), custom_call_target="tpu_custom_call" | custom-call | bytes 1966080 | tf_op jit(solution)/shard_map/pallas_call | solution.py:272
  59.3 1.3 %collective-permute-start.27 = (f32[160,128]{1,0:T(8,128)S(1)}, f32[160,128]{1,0:T(8,128)S(1)}, u32[]{:S(2)}, u32[]{:S(2)}) collective-permute-start(f32[160,128]{1,0:T(8,128)S(1)} %get-tuple-element.127), channel_id=1, source_target_pairs={{0,2},{1,3},{2,4},{3,5},{4,6},{5,7},{6,0},{7,1},{8,10},{9,11},{10,... | collective-permute-start | bytes 245768 | tf_op jit(solution)/shard_map/ppermute | solution.py:576
  60.6 0.2 collective-permute-start.28
  60.8 5.7 %collective-permute-done.27.refs_5_ = f32[160,128]{1,0:T(8,128)S(1)} collective-permute-done((f32[160,128]{1,0:T(8,128)S(1)}, f32[160,128]{1,0:T(8,128)S(1)}, u32[]{:S(2)}, u32[]{:S(2)}) %collective-permute-start.27) | collective-permute-done | bytes 81952 | tf_op jit(solution)/shard_map/ppermute | solution.py:576
  66.5 1.9 %shard_map.91.w_ref = f32[4,640,128]{2,1,0:T(8,128)S(1)} custom-call(s32[2,128]{1,0:T(2,128)S(1)} %copy-done.3, bf16[640,480]{1,0:T(8,128)(2,1)S(1)} %get-tuple-element.72.ohi_ref, bf16[640,480]{1,0:T(8,128)(2,1)S(1)} %get-tuple-element.73.olo_ref, f32[4,640,128]{2,1,0:T(8,128)S(1)} %get-tuple-element.123.u_ref, f32[4,640,128]{2,1,0:T(8,128)S(1)} %shard_map.88.in_ref, ...), custom_call_target="tpu_custom_call" | custom-call | flops 629145600 | bytes 3932160 | tf_op jit(solution)/shard_map/pallas_call | solution.py:365
  68.4 1.1 %collective-permute-done.28.refs_6_ = f32[160,128]{1,0:T(8,128)S(1)} collective-permute-done((f32[160,128]{1,0:T(8,128)S(1)}, f32[160,128]{1,0:T(8,128)S(1)}, u32[]{:S(2)}, u32[]{:S(2)}) %collective-permute-start.28) | collective-permute-done | bytes 81952 | tf_op jit(solution)/shard_map/ppermute | solution.py:576
  69.5 1.5 %collective-permute-done.29.refs_7_ = f32[160,128]{1,0:T(8,128)S(1)} collective-permute-done((f32[160,128]{1,0:T(8,128)S(1)}, f32[160,128]{1,0:T(8,128)S(1)}, u32[]{:S(2)}, u32[]{:S(2)}) %collective-permute-start.29) | collective-permute-done | bytes 81952 | tf_op jit(solution)/shard_map/ppermute | solution.py:576
  71.0 0.6 collective-permute-done.25.refs_2_
  71.6 2.3 %shard_map.92 = (f32[4,640,128]{2,1,0:T(8,128)}, f32[4,640,128]{2,1,0:T(8,128)}) custom-call(bf16[640,480]{1,0:T(8,128)(2,1)S(1)} %get-tuple-element.72.ohi_ref, bf16[640,480]{1,0:T(8,128)(2,1)S(1)} %get-tuple-element.73.olo_ref, f32[4,640,128]{2,1,0:T(8,128)S(1)} %get-tuple-element.104.u_ref, f32[4,640,128]{2,1,0:T(8,128)S(1)} %shard_map.91.w_ref, ...), custom_call_target="tpu_custom_call" | custom-call | flops 314572800 | bytes 6553600 | tf_op jit(solution)/shard_map/pallas_call | solution.py:560
  (27 shorter events, 0.1 us)
Async XLA Ops:
  0.6 1.3 %copy-start = (f32[4,10,64,128]{3,2,1,0:T(8,128)S(1)}, f32[4,10,64,128]{3,2,1,0:T(8,128)}, u32[]{:S(2)}) copy-start(f32[4,10,64,128]{3,2,1,0:T(8,128)} %param.6) | copy-start | bytes 3932164
  2.2 11.3 %copy-start.6 = (f32[2,10,10]{2,0,1:T(2,128)S(1)}, f32[2,10,10]{2,0,1:T(2,128)}, u32[]{:S(2)}) copy-start(f32[2,10,10]{2,0,1:T(2,128)} %param.11) | copy-start | bytes 2404
  2.2 11.3 %copy-start.2 = (f32[2,64,64]{2,1,0:T(8,128)S(1)}, f32[2,64,64]{2,1,0:T(8,128)}, u32[]{:S(2)}) copy-start(f32[2,64,64]{2,1,0:T(8,128)} %vol_ref.1) | copy-start | bytes 98308
  2.2 14.8 %copy-start.1 = (f32[4,10,64,128]{3,2,1,0:T(8,128)S(1)}, f32[4,10,64,128]{3,2,1,0:T(8,128)}, u32[]{:S(2)}) copy-start(f32[4,10,64,128]{3,2,1,0:T(8,128)} %param.6) | copy-start | bytes 3932164
  2.6 1.8 %collective-permute-start = (f32[4,160,128]{2,1,0:T(8,128)S(1)}, f32[4,160,128]{2,1,0:T(8,128)S(1)}, u32[]{:S(2)}, u32[]{:S(2)}) collective-permute-start(f32[4,160,128]{2,1,0:T(8,128)S(1)} %get-tuple-element.70), channel_id=1, source_target_pairs={{0,1},{1,0},{2,3},{3,2},{4,5},{5,4},{6,7},{7,6},{8,9},{9,8},{10,11... | collective-permute-start | bytes 983048 | tf_op jit(solution)/shard_map/ppermute | solution.py:581
  4.4 14.4 %collective-permute-start.4 = (f32[352,128]{1,0:T(8,128)S(1)}, f32[352,128]{1,0:T(8,128)S(1)}, u32[]{:S(2)}, u32[]{:S(2)}) collective-permute-start(f32[352,128]{1,0:T(8,128)S(1)} %shard_map.79), channel_id=1, source_target_pairs={{0,2},{1,7},{2,4},{3,1},{4,6},{5,3},{6,0},{7,5},{8,10},{9,15},{10,... | collective-permute-start | bytes 540680 | tf_op jit(solution)/shard_map/ppermute | solution.py:571
  7.4 13.9 %collective-permute-start.1 = (f32[4,160,128]{2,1,0:T(8,128)S(1)}, f32[4,160,128]{2,1,0:T(8,128)S(1)}, u32[]{:S(2)}, u32[]{:S(2)}) collective-permute-start(f32[4,160,128]{2,1,0:T(8,128)S(1)} %get-tuple-element.74), channel_id=1, source_target_pairs={{0,8},{8,0},{16,24},{24,16},{1,9},{9,1},{17,25},{25,17},{2,10},{10... | collective-permute-start | bytes 983048 | tf_op jit(solution)/shard_map/ppermute | solution.py:565
  8.9 16.1 %collective-permute-start.2 = (f32[4,160,128]{2,1,0:T(8,128)S(1)}, f32[4,160,128]{2,1,0:T(8,128)S(1)}, u32[]{:S(2)}, u32[]{:S(2)}) collective-permute-start(f32[4,160,128]{2,1,0:T(8,128)S(1)} %get-tuple-element.75), channel_id=1, source_target_pairs={{0,16},{8,24},{16,0},{24,8},{1,17},{9,25},{17,1},{25,9},{2,18},{10... | collective-permute-start | bytes 983048 | tf_op jit(solution)/shard_map/ppermute | solution.py:565
  10.4 14.8 %collective-permute-start.3 = (f32[4,160,128]{2,1,0:T(8,128)S(1)}, f32[4,160,128]{2,1,0:T(8,128)S(1)}, u32[]{:S(2)}, u32[]{:S(2)}) collective-permute-start(f32[4,160,128]{2,1,0:T(8,128)S(1)} %get-tuple-element.76), channel_id=1, source_target_pairs={{0,24},{8,16},{16,8},{24,0},{1,25},{9,17},{17,9},{25,1},{2,26},{10... | collective-permute-start | bytes 983048 | tf_op jit(solution)/shard_map/ppermute | solution.py:565
  10.9 7.9 %collective-permute-start.5 = (f32[160,128]{1,0:T(8,128)S(1)}, f32[160,128]{1,0:T(8,128)S(1)}, u32[]{:S(2)}, u32[]{:S(2)}) collective-permute-start(f32[160,128]{1,0:T(8,128)S(1)} %get-tuple-element.77), channel_id=1, source_target_pairs={{0,4},{1,5},{2,6},{3,7},{4,0},{5,1},{6,2},{7,3},{8,12},{9,13},{10,... | collective-permute-start | bytes 245768 | tf_op jit(solution)/shard_map/ppermute | solution.py:571
  17.0 3.4 %copy-start.4 = (s32[4]{0:T(128)S(1)}, s32[4]{0:T(128)}, u32[]{:S(2)}) copy-start(s32[4]{0:T(128)} %group_ref.3) | copy-start | bytes 52
  17.0 3.4 %copy-start.5 = (s32[4]{0:T(128)S(1)}, s32[4]{0:T(128)}, u32[]{:S(2)}) copy-start(s32[4]{0:T(128)} %shift_ref.3) | copy-start | bytes 52
  18.7 12.5 %copy-start.3 = (s32[2,128]{1,0:T(2,128)S(1)}, s32[2,128]{1,0:T(2,128)}, u32[]{:S(2)}) copy-start(s32[2,128]{1,0:T(2,128)} %near_ref.3) | copy-start | bytes 3076
  18.8 1.6 %collective-permute-start.6 = (f32[352,128]{1,0:T(8,128)S(1)}, f32[352,128]{1,0:T(8,128)S(1)}, u32[]{:S(2)}, u32[]{:S(2)}) collective-permute-start(f32[352,128]{1,0:T(8,128)S(1)} %collective-permute-done.4.refs_0_.refs_1_), channel_id=1, source_target_pairs={{0,1},{1,0},{2,3},{3,2},{4,5},{5,4},{6,7},{7,6},{8,9},{9,8},{10,11... | collective-permute-start | bytes 540680 | tf_op jit(solution)/shard_map/ppermute | solution.py:581
  18.8 1.5 %collective-permute-start.7 = (f32[160,128]{1,0:T(8,128)S(1)}, f32[160,128]{1,0:T(8,128)S(1)}, u32[]{:S(2)}, u32[]{:S(2)}) collective-permute-start(f32[160,128]{1,0:T(8,128)S(1)} %collective-permute-done.5.refs_1_), channel_id=1, source_target_pairs={{0,1},{1,0},{2,3},{3,2},{4,5},{5,4},{6,7},{7,6},{8,9},{9,8},{10,11... | collective-permute-start | bytes 245768 | tf_op jit(solution)/shard_map/ppermute | solution.py:581
  21.1 8.9 %collective-permute-start.8 = (f32[320,128]{1,0:T(8,128)S(1)}, f32[320,128]{1,0:T(8,128)S(1)}, u32[]{:S(2)}, u32[]{:S(2)}) collective-permute-start(f32[320,128]{1,0:T(8,128)S(1)} %get-tuple-element.101), channel_id=1, source_target_pairs={{0,2},{1,7},{2,4},{3,1},{4,6},{5,3},{6,0},{7,5},{8,10},{9,15},{10,... | collective-permute-start | bytes 491528 | tf_op jit(solution)/shard_map/ppermute | solution.py:571
  26.2 13.8 %collective-permute-start.11 = (f32[4,160,128]{2,1,0:T(8,128)S(1)}, f32[4,160,128]{2,1,0:T(8,128)S(1)}, u32[]{:S(2)}, u32[]{:S(2)}) collective-permute-start(f32[4,160,128]{2,1,0:T(8,128)S(1)} %get-tuple-element.93.refs_1_), channel_id=1, source_target_pairs={{0,8},{8,0},{16,24},{24,16},{1,9},{9,1},{17,25},{25,17},{2,10},{10... | collective-permute-start | bytes 983048 | tf_op jit(solution)/shard_map/ppermute | solution.py:565
  27.7 15.9 %collective-permute-start.12 = (f32[4,160,128]{2,1,0:T(8,128)S(1)}, f32[4,160,128]{2,1,0:T(8,128)S(1)}, u32[]{:S(2)}, u32[]{:S(2)}) collective-permute-start(f32[4,160,128]{2,1,0:T(8,128)S(1)} %get-tuple-element.94.refs_2_), channel_id=1, source_target_pairs={{0,16},{8,24},{16,0},{24,8},{1,17},{9,25},{17,1},{25,9},{2,18},{10... | collective-permute-start | bytes 983048 | tf_op jit(solution)/shard_map/ppermute | solution.py:565
  28.7 16.9 %collective-permute-start.13 = (f32[4,160,128]{2,1,0:T(8,128)S(1)}, f32[4,160,128]{2,1,0:T(8,128)S(1)}, u32[]{:S(2)}, u32[]{:S(2)}) collective-permute-start(f32[4,160,128]{2,1,0:T(8,128)S(1)} %get-tuple-element.95.refs_3_), channel_id=1, source_target_pairs={{0,24},{8,16},{16,8},{24,0},{1,25},{9,17},{17,9},{25,1},{2,26},{10... | collective-permute-start | bytes 983048 | tf_op jit(solution)/shard_map/ppermute | solution.py:565
  30.1 7.1 %collective-permute-start.10 = (f32[320,128]{1,0:T(8,128)S(1)}, f32[320,128]{1,0:T(8,128)S(1)}, u32[]{:S(2)}, u32[]{:S(2)}) collective-permute-start(f32[320,128]{1,0:T(8,128)S(1)} %collective-permute-done.8.refs_1_), channel_id=1, source_target_pairs={{0,1},{1,0},{2,3},{3,2},{4,5},{5,4},{6,7},{7,6},{8,9},{9,8},{10,11... | collective-permute-start | bytes 491528 | tf_op jit(solution)/shard_map/ppermute | solution.py:581
  30.1 7.0 %collective-permute-start.9 = (f32[160,128]{1,0:T(8,128)S(1)}, f32[160,128]{1,0:T(8,128)S(1)}, u32[]{:S(2)}, u32[]{:S(2)}) collective-permute-start(f32[160,128]{1,0:T(8,128)S(1)} %get-tuple-element.102), channel_id=1, source_target_pairs={{0,4},{1,5},{2,6},{3,7},{4,0},{5,1},{6,2},{7,3},{8,12},{9,13},{10,... | collective-permute-start | bytes 245768 | tf_op jit(solution)/shard_map/ppermute | solution.py:571
  37.9 11.4 %collective-permute-start.18 = (f32[4,40,128]{2,1,0:T(8,128)S(1)}, f32[4,40,128]{2,1,0:T(8,128)S(1)}, u32[]{:S(2)}, u32[]{:S(2)}) collective-permute-start(f32[4,40,128]{2,1,0:T(8,128)S(1)} %get-tuple-element.111), channel_id=1, source_target_pairs={{0,8},{8,0},{16,24},{24,16},{1,9},{9,1},{17,25},{25,17},{2,10},{10... | collective-permute-start | bytes 245768 | tf_op jit(solution)/shard_map/ppermute | solution.py:565
  39.2 12.6 %collective-permute-start.19 = (f32[4,40,128]{2,1,0:T(8,128)S(1)}, f32[4,40,128]{2,1,0:T(8,128)S(1)}, u32[]{:S(2)}, u32[]{:S(2)}) collective-permute-start(f32[4,40,128]{2,1,0:T(8,128)S(1)} %get-tuple-element.112), channel_id=1, source_target_pairs={{0,16},{8,24},{16,0},{24,8},{1,17},{9,25},{17,1},{25,9},{2,18},{10... | collective-permute-start | bytes 245768 | tf_op jit(solution)/shard_map/ppermute | solution.py:565
  40.0 11.8 %collective-permute-start.20 = (f32[4,40,128]{2,1,0:T(8,128)S(1)}, f32[4,40,128]{2,1,0:T(8,128)S(1)}, u32[]{:S(2)}, u32[]{:S(2)}) collective-permute-start(f32[4,40,128]{2,1,0:T(8,128)S(1)} %get-tuple-element.113), channel_id=1, source_target_pairs={{0,24},{8,16},{16,8},{24,0},{1,25},{9,17},{17,9},{25,1},{2,26},{10... | collective-permute-start | bytes 245768 | tf_op jit(solution)/shard_map/ppermute | solution.py:565
  46.1 8.7 %collective-permute-start.15 = (f32[160,128]{1,0:T(8,128)S(1)}, f32[160,128]{1,0:T(8,128)S(1)}, u32[]{:S(2)}, u32[]{:S(2)}) collective-permute-start(f32[160,128]{1,0:T(8,128)S(1)} %get-tuple-element.108), channel_id=1, source_target_pairs={{0,4},{1,5},{2,6},{3,7},{4,0},{5,1},{6,2},{7,3},{8,12},{9,13},{10,... | collective-permute-start | bytes 245768 | tf_op jit(solution)/shard_map/ppermute | solution.py:576
  46.3 9.5 %collective-permute-start.14 = (f32[192,128]{1,0:T(8,128)S(1)}, f32[192,128]{1,0:T(8,128)S(1)}, u32[]{:S(2)}, u32[]{:S(2)}) collective-permute-start(f32[192,128]{1,0:T(8,128)S(1)} %get-tuple-element.107), channel_id=1, source_target_pairs={{0,2},{1,3},{2,4},{3,5},{4,6},{5,7},{6,0},{7,1},{8,10},{9,11},{10,... | collective-permute-start | bytes 294920 | tf_op jit(solution)/shard_map/ppermute | solution.py:576
  49.3 6.5 %collective-permute-start.16 = (f32[192,128]{1,0:T(8,128)S(1)}, f32[192,128]{1,0:T(8,128)S(1)}, u32[]{:S(2)}, u32[]{:S(2)}) collective-permute-start(f32[192,128]{1,0:T(8,128)S(1)} %get-tuple-element.109), channel_id=1, source_target_pairs={{0,6},{1,7},{2,0},{3,1},{4,2},{5,3},{6,4},{7,5},{8,14},{9,15},{10,... | collective-permute-start | bytes 294920 | tf_op jit(solution)/shard_map/ppermute | solution.py:576
  52.2 18.8 %collective-permute-start.24 = (f32[4,200,128]{2,1,0:T(8,128)S(1)}, f32[4,200,128]{2,1,0:T(8,128)S(1)}, u32[]{:S(2)}, u32[]{:S(2)}) collective-permute-start(f32[4,200,128]{2,1,0:T(8,128)S(1)} %get-tuple-element.124), channel_id=1, source_target_pairs={{0,8},{8,0},{16,24},{24,16},{1,9},{9,1},{17,25},{25,17},{2,10},{10... | collective-permute-start | bytes 1228808 | tf_op jit(solution)/shard_map/ppermute | solution.py:565
  52.5 19.1 %collective-permute-start.25 = (f32[4,200,128]{2,1,0:T(8,128)S(1)}, f32[4,200,128]{2,1,0:T(8,128)S(1)}, u32[]{:S(2)}, u32[]{:S(2)}) collective-permute-start(f32[4,200,128]{2,1,0:T(8,128)S(1)} %get-tuple-element.125), channel_id=1, source_target_pairs={{0,16},{8,24},{16,0},{24,8},{1,17},{9,25},{17,1},{25,9},{2,18},{10... | collective-permute-start | bytes 1228808 | tf_op jit(solution)/shard_map/ppermute | solution.py:565
  54.7 16.9 %collective-permute-start.26 = (f32[4,200,128]{2,1,0:T(8,128)S(1)}, f32[4,200,128]{2,1,0:T(8,128)S(1)}, u32[]{:S(2)}, u32[]{:S(2)}) collective-permute-start(f32[4,200,128]{2,1,0:T(8,128)S(1)} %get-tuple-element.126), channel_id=1, source_target_pairs={{0,24},{8,16},{16,8},{24,0},{1,25},{9,17},{17,9},{25,1},{2,26},{10... | collective-permute-start | bytes 1228808 | tf_op jit(solution)/shard_map/ppermute | solution.py:565
  55.8 1.3 %collective-permute-start.17 = (f32[224,128]{1,0:T(8,128)S(1)}, f32[224,128]{1,0:T(8,128)S(1)}, u32[]{:S(2)}, u32[]{:S(2)}) collective-permute-start(f32[224,128]{1,0:T(8,128)S(1)} %get-tuple-element.106.refs_0_), channel_id=1, source_target_pairs={{0,1},{1,0},{2,3},{3,2},{4,5},{5,4},{6,7},{7,6},{8,9},{9,8},{10,11... | collective-permute-start | bytes 344072 | tf_op jit(solution)/shard_map/ppermute | solution.py:581
  55.8 1.5 %collective-permute-start.22 = (f32[160,128]{1,0:T(8,128)S(1)}, f32[160,128]{1,0:T(8,128)S(1)}, u32[]{:S(2)}, u32[]{:S(2)}) collective-permute-start(f32[160,128]{1,0:T(8,128)S(1)} %collective-permute-done.15.refs_2_), channel_id=1, source_target_pairs={{0,1},{1,0},{2,3},{3,2},{4,5},{5,4},{6,7},{7,6},{8,9},{9,8},{10,11... | collective-permute-start | bytes 245768 | tf_op jit(solution)/shard_map/ppermute | solution.py:581
  57.1 1.3 %collective-permute-start.21 = (f32[192,128]{1,0:T(8,128)S(1)}, f32[192,128]{1,0:T(8,128)S(1)}, u32[]{:S(2)}, u32[]{:S(2)}) collective-permute-start(f32[192,128]{1,0:T(8,128)S(1)} %collective-permute-done.14.refs_1_), channel_id=1, source_target_pairs={{0,1},{1,0},{2,3},{3,2},{4,5},{5,4},{6,7},{7,6},{8,9},{9,8},{10,11... | collective-permute-start | bytes 294920 | tf_op jit(solution)/shard_map/ppermute | solution.py:581
  57.2 1.3 %collective-permute-start.23 = (f32[192,128]{1,0:T(8,128)S(1)}, f32[192,128]{1,0:T(8,128)S(1)}, u32[]{:S(2)}, u32[]{:S(2)}) collective-permute-start(f32[192,128]{1,0:T(8,128)S(1)} %collective-permute-done.16.refs_3_), channel_id=1, source_target_pairs={{0,1},{1,0},{2,3},{3,2},{4,5},{5,4},{6,7},{7,6},{8,9},{9,8},{10,11... | collective-permute-start | bytes 294920 | tf_op jit(solution)/shard_map/ppermute | solution.py:581
  59.3 7.2 %collective-permute-start.27 = (f32[160,128]{1,0:T(8,128)S(1)}, f32[160,128]{1,0:T(8,128)S(1)}, u32[]{:S(2)}, u32[]{:S(2)}) collective-permute-start(f32[160,128]{1,0:T(8,128)S(1)} %get-tuple-element.127), channel_id=1, source_target_pairs={{0,2},{1,3},{2,4},{3,5},{4,6},{5,7},{6,0},{7,1},{8,10},{9,11},{10,... | collective-permute-start | bytes 245768 | tf_op jit(solution)/shard_map/ppermute | solution.py:576
  60.6 8.9 %collective-permute-start.28 = (f32[160,128]{1,0:T(8,128)S(1)}, f32[160,128]{1,0:T(8,128)S(1)}, u32[]{:S(2)}, u32[]{:S(2)}) collective-permute-start(f32[160,128]{1,0:T(8,128)S(1)} %get-tuple-element.128), channel_id=1, source_target_pairs={{0,4},{1,5},{2,6},{3,7},{4,0},{5,1},{6,2},{7,3},{8,12},{9,13},{10,... | collective-permute-start | bytes 245768 | tf_op jit(solution)/shard_map/ppermute | solution.py:576
  66.5 4.5 %collective-permute-start.29 = (f32[160,128]{1,0:T(8,128)S(1)}, f32[160,128]{1,0:T(8,128)S(1)}, u32[]{:S(2)}, u32[]{:S(2)}) collective-permute-start(f32[160,128]{1,0:T(8,128)S(1)} %get-tuple-element.129), channel_id=1, source_target_pairs={{0,6},{1,7},{2,0},{3,1},{4,2},{5,3},{6,4},{7,5},{8,14},{9,15},{10,... | collective-permute-start | bytes 245768 | tf_op jit(solution)/shard_map/ppermute | solution.py:576

commit v4 on v3

--- a/solution.py
+++ b/solution.py
@@ -586,7 +586,8 @@
     u = conserved_field.reshape(sz.L, sz.R, sz.E)
 
     def time_trip(parts):
-        return [parts[0]] + [over_tm(parts[j], j) for j in range(1, sz.M)]
+        moved = {j: over_tm(parts[j], j) for j in reversed(range(1, sz.M))}
+        return [parts[0]] + [moved[j] for j in range(1, sz.M)]
 
     def ring_trip(parts):
         return [parts[0]] + [over_ring(parts[j], j) for j in range(1, sz.Z)]

time: 74.1 us -> 74.1 us (level)
  no operation moved by 1% of the time
where the time goes in v4:
time: 74.1 us; the launch traced here: 73.9 us
  starting transfers between devices  28.9 us (39%)
  waiting for transfers between devices  23.8 us (32%)
  Pallas kernels  19 us (26%)
  local copies, waits for them, and re-layouts  1.35 us (2%)
  between operations  0.87 us (1%)
    ppermute x12, starting transfers between devices, over_tm(): return lax.ppermute(x, 'tm', [(i, i ^ j) for i in range(size)])  14.4 us
    ppermute x12, waiting for transfers between devices, over_tm(): return lax.ppermute(x, 'tm', [(i, i ^ j) for i in range(size)])  8.6 us
    ppermute x6, waiting for transfers between devices, over_ring(): lax.ppermute(x, 'space', [(i, (i + 2 * j) % size) for i in range(size)])  8.34 us
    ppermute x4, starting transfers between devices, over_chips(): return lax.ppermute(x, 'space', pairs)  6.81 us
    ppermute x6, starting transfers between devices, over_ring(): lax.ppermute(x, 'space', [(i, (i + 2 * j) % size) for i in range(size)])  5.55 us
    ppermute x8, waiting for transfers between devices, over_cores(): return lax.ppermute(x, 'space', [(i, i ^ 1) for i in range(size)])  4.04 us
    pallas_call x2, Pallas kernels, face_part(): return call(body, [out], ins, scratch, flops, 12 * u.size)(*args)[0]  3.7 us
    pallas_call x1, Pallas kernels, matrices(): call(body, [inner, inner, outer, outer], [SMEM, VMEM], (), nbytes, nbytes)  3.52 us
  transfers between devices with their start and end apart: 30, of which 14 were waited for; matrix products, arithmetic and copies ran while one was open for 0% of the time, Pallas kernels for 22%

profile of v4, /device:TPU:0, one launch (start us, length us, event | category | flops | bytes accessed | tf_op | source)
XLA Modules:
  0.0 73.9 jit_solution(15977916794915983509)
XLA Ops:
  0.6 0.0 copy-start
  0.6 1.3 %copy-done = f32[4,10,64,128]{3,2,1,0:T(8,128)S(1)} copy-done((f32[4,10,64,128]{3,2,1,0:T(8,128)S(1)}, f32[4,10,64,128]{3,2,1,0:T(8,128)}, u32[]{:S(2)}) %copy-start) | copy-done | bytes 1310744
  1.9 0.2 shard_map.77
  2.2 0.0 copy-start.6
  2.2 0.0 copy-start.2
  2.2 0.4 shard_map.78
  2.6 0.5 collective-permute-start
  3.1 1.3 %collective-permute-done.swap_ref.refs_0_ = f32[4,160,128]{2,1,0:T(8,128)S(1)} collective-permute-done((f32[4,160,128]{2,1,0:T(8,128)S(1)}, f32[4,160,128]{2,1,0:T(8,128)S(1)}, u32[]{:S(2)}, u32[]{:S(2)}) %collective-permute-start) | collective-permute-done | bytes 327712 | tf_op jit(solution)/shard_map/ppermute | solution.py:581
  4.4 3.0 %collective-permute-start.4 = (f32[352,128]{1,0:T(8,128)S(1)}, f32[352,128]{1,0:T(8,128)S(1)}, u32[]{:S(2)}, u32[]{:S(2)}) collective-permute-start(f32[352,128]{1,0:T(8,128)S(1)} %shard_map.79), channel_id=1, source_target_pairs={{0,2},{1,7},{2,4},{3,1},{4,6},{5,3},{6,0},{7,5},{8,10},{9,15},{10,... | collective-permute-start | bytes 540680 | tf_op jit(solution)/shard_map/ppermute | solution.py:571
  7.4 1.5 %collective-permute-start.1 = (f32[4,160,128]{2,1,0:T(8,128)S(1)}, f32[4,160,128]{2,1,0:T(8,128)S(1)}, u32[]{:S(2)}, u32[]{:S(2)}) collective-permute-start(f32[4,160,128]{2,1,0:T(8,128)S(1)} %get-tuple-element.74), channel_id=1, source_target_pairs={{0,8},{8,0},{16,24},{24,16},{1,9},{9,1},{17,25},{25,17},{2,10},{10... | collective-permute-start | bytes 983048 | tf_op jit(solution)/shard_map/ppermute | solution.py:565
  8.9 1.5 %collective-permute-start.2 = (f32[4,160,128]{2,1,0:T(8,128)S(1)}, f32[4,160,128]{2,1,0:T(8,128)S(1)}, u32[]{:S(2)}, u32[]{:S(2)}) collective-permute-start(f32[4,160,128]{2,1,0:T(8,128)S(1)} %get-tuple-element.75), channel_id=1, source_target_pairs={{0,16},{8,24},{16,0},{24,8},{1,17},{9,25},{17,1},{25,9},{2,18},{10... | collective-permute-start | bytes 983048 | tf_op jit(solution)/shard_map/ppermute | solution.py:565
  10.4 0.5 collective-permute-start.3
  10.9 2.6 %collective-permute-start.5 = (f32[160,128]{1,0:T(8,128)S(1)}, f32[160,128]{1,0:T(8,128)S(1)}, u32[]{:S(2)}, u32[]{:S(2)}) collective-permute-start(f32[160,128]{1,0:T(8,128)S(1)} %get-tuple-element.77), channel_id=1, source_target_pairs={{0,4},{1,5},{2,6},{3,7},{4,0},{5,1},{6,2},{7,3},{8,12},{9,13},{10,... | collective-permute-start | bytes 245768 | tf_op jit(solution)/shard_map/ppermute | solution.py:571
  13.5 3.5 %shard_map.80 = (bf16[640,640]{1,0:T(8,128)(2,1)S(1)}, bf16[640,640]{1,0:T(8,128)(2,1)S(1)}, bf16[640,480]{1,0:T(8,128)(2,1)S(1)}, bf16[640,480]{1,0:T(8,128)(2,1)S(1)}) custom-call(f32[2,10,10]{2,1,0:T(8,128)S(1)} %copy.8.flux_ref, f32[2,64,64]{2,1,0:T(8,128)S(1)} %copy-done.2), custom_call_target="tpu_custom_call" | custom-call | flops 2867200 | bytes 2867200 | tf_op jit(solution)/shard_map/pallas_call | solution.py:152
  17.0 0.0 copy-start.4
  17.0 0.0 copy-start.5
  17.0 1.7 %shard_map.81.in_ref = f32[4,640,128]{2,1,0:T(8,128)S(1)} custom-call(bf16[640,640]{1,0:T(8,128)(2,1)S(1)} %get-tuple-element.78.hi_ref, bf16[640,640]{1,0:T(8,128)(2,1)S(1)} %get-tuple-element.79.lo_ref, f32[4,640,128]{2,1,0:T(8,128)S(1)} %bitcast.5), custom_call_target="tpu_custom_call" | custom-call | flops 1258291200 | bytes 3932160 | tf_op jit(solution)/shard_map/pallas_call | solution.py:313
  18.7 0.0 copy-start.3
  18.8 0.1 collective-permute-start.6
  18.8 0.5 collective-permute-start.7
  19.3 1.0 %collective-permute-done.7.refs_3_ = f32[160,128]{1,0:T(8,128)S(1)} collective-permute-done((f32[160,128]{1,0:T(8,128)S(1)}, f32[160,128]{1,0:T(8,128)S(1)}, u32[]{:S(2)}, u32[]{:S(2)}) %collective-permute-start.7) | collective-permute-done | bytes 81952 | tf_op jit(solution)/shard_map/ppermute | solution.py:581
  20.4 0.7 %shard_map.82 = (f32[160,128]{1,0:T(8,128)S(1)}, f32[320,128]{1,0:T(8,128)S(1)}, f32[160,128]{1,0:T(8,128)S(1)}) custom-call(s32[4]{0:T(128)S(1)} %copy-done.4, s32[4]{0:T(128)S(1)} %copy-done.5, f32[2,160,128]{2,1,0:T(8,128)S(1)} %get-tuple-element.69.keep_ref, f32[4,160,128]{2,1,0:T(8,128)S(1)} %collective-permute-done.swap_ref.refs_0_, ...), custom_call_target="tpu_custom_call" | custom-call | bytes 1966080 | tf_op jit(solution)/shard_map/pallas_call | solution.py:451
  21.1 0.1 collective-permute-start.8
  21.3 3.7 %collective-permute-done.2.refs_2_ = f32[4,160,128]{2,1,0:T(8,128)S(1)} collective-permute-done((f32[4,160,128]{2,1,0:T(8,128)S(1)}, f32[4,160,128]{2,1,0:T(8,128)S(1)}, u32[]{:S(2)}, u32[]{:S(2)}) %collective-permute-start.2) | collective-permute-done | bytes 327712 | tf_op jit(solution)/shard_map/ppermute | solution.py:565
  24.9 0.2 collective-permute-done.3.refs_3_
  25.1 1.1 %shard_map.83 = (f32[4,160,128]{2,1,0:T(8,128)S(1)}, f32[4,160,128]{2,1,0:T(8,128)S(1)}, f32[4,160,128]{2,1,0:T(8,128)S(1)}, f32[4,160,128]{2,1,0:T(8,128)S(1)}) custom-call(f32[4,160,128]{2,1,0:T(8,128)S(1)} %get-tuple-element.83.refs_0_, f32[4,160,128]{2,1,0:T(8,128)S(1)} %collective-permute-done.1.refs_1_, ...), custom_call_target="tpu_custom_call" | custom-call | flops 6553600 | bytes 2621440 | tf_op jit(solution)/shard_map/pallas_call | solution.py:406
  26.2 1.5 %collective-permute-start.11 = (f32[4,160,128]{2,1,0:T(8,128)S(1)}, f32[4,160,128]{2,1,0:T(8,128)S(1)}, u32[]{:S(2)}, u32[]{:S(2)}) collective-permute-start(f32[4,160,128]{2,1,0:T(8,128)S(1)} %get-tuple-element.93.refs_1_), channel_id=1, source_target_pairs={{0,8},{8,0},{16,24},{24,16},{1,9},{9,1},{17,25},{25,17},{2,10},{10... | collective-permute-start | bytes 983048 | tf_op jit(solution)/shard_map/ppermute | solution.py:565
  27.7 1.0 %collective-permute-start.12 = (f32[4,160,128]{2,1,0:T(8,128)S(1)}, f32[4,160,128]{2,1,0:T(8,128)S(1)}, u32[]{:S(2)}, u32[]{:S(2)}) collective-permute-start(f32[4,160,128]{2,1,0:T(8,128)S(1)} %get-tuple-element.94.refs_2_), channel_id=1, source_target_pairs={{0,16},{8,24},{16,0},{24,8},{1,17},{9,25},{17,1},{25,9},{2,18},{10... | collective-permute-start | bytes 983048 | tf_op jit(solution)/shard_map/ppermute | solution.py:565
  28.7 1.4 %collective-permute-start.13 = (f32[4,160,128]{2,1,0:T(8,128)S(1)}, f32[4,160,128]{2,1,0:T(8,128)S(1)}, u32[]{:S(2)}, u32[]{:S(2)}) collective-permute-start(f32[4,160,128]{2,1,0:T(8,128)S(1)} %get-tuple-element.95.refs_3_), channel_id=1, source_target_pairs={{0,24},{8,16},{16,8},{24,0},{1,25},{9,17},{17,9},{25,1},{2,26},{10... | collective-permute-start | bytes 983048 | tf_op jit(solution)/shard_map/ppermute | solution.py:565
  30.1 0.1 collective-permute-start.10
  30.1 1.1 %collective-permute-start.9 = (f32[160,128]{1,0:T(8,128)S(1)}, f32[160,128]{1,0:T(8,128)S(1)}, u32[]{:S(2)}, u32[]{:S(2)}) collective-permute-start(f32[160,128]{1,0:T(8,128)S(1)} %get-tuple-element.102), channel_id=1, source_target_pairs={{0,4},{1,5},{2,6},{3,7},{4,0},{5,1},{6,2},{7,3},{8,12},{9,13},{10,... | collective-permute-start | bytes 245768 | tf_op jit(solution)/shard_map/ppermute | solution.py:571
  31.2 1.9 %shard_map.84.w_ref = f32[4,640,128]{2,1,0:T(8,128)S(1)} custom-call(s32[2,128]{1,0:T(2,128)S(1)} %copy-done.3, bf16[640,480]{1,0:T(8,128)(2,1)S(1)} %get-tuple-element.72.ohi_ref, bf16[640,480]{1,0:T(8,128)(2,1)S(1)} %get-tuple-element.73.olo_ref, f32[4,640,128]{2,1,0:T(8,128)S(1)} %bitcast.6, f32[4,640,128]{2,1,0:T(8,128)S(1)} %shard_map.81.in_ref, ...), custom_call_target="tpu_custom_call" | custom-call | flops 629145600 | bytes 3932160 | tf_op jit(solution)/shard_map/pallas_call | solution.py:365
  33.1 1.2 %shard_map.85 = (f32[4,160,128]{2,1,0:T(8,128)S(1)}, f32[4,160,128]{2,1,0:T(8,128)S(1)}, f32[4,160,128]{2,1,0:T(8,128)S(1)}, f32[4,160,128]{2,1,0:T(8,128)S(1)}) custom-call(f32[4,160,128]{2,1,0:T(8,128)S(1)} %get-tuple-element.92.refs_0_, f32[4,160,128]{2,1,0:T(8,128)S(1)} %get-tuple-element.93.refs_1_, f32[4,160,128]{2,1,0:T(8,128)S(1)} %get-tuple-element.94.refs_2_, ...), custom_call_target="tpu_custom_call" | custom-call | flops 6553600 | bytes 2621440 | tf_op jit(solution)/shard_map/pallas_call | solution.py:406
  34.3 2.8 %collective-permute-done.9.refs_2_ = f32[160,128]{1,0:T(8,128)S(1)} collective-permute-done((f32[160,128]{1,0:T(8,128)S(1)}, f32[160,128]{1,0:T(8,128)S(1)}, u32[]{:S(2)}, u32[]{:S(2)}) %collective-permute-start.9) | collective-permute-done | bytes 81952 | tf_op jit(solution)/shard_map/ppermute | solution.py:571
  37.1 0.8 %shard_map.86 = (f32[4,640,128]{2,1,0:T(8,128)S(1)}, f32[4,40,128]{2,1,0:T(8,128)S(1)}, f32[4,40,128]{2,1,0:T(8,128)S(1)}, f32[4,40,128]{2,1,0:T(8,128)S(1)}, f32[4,40,128]{2,1,0:T(8,128)S(1)}) custom-call(bf16[640,480]{1,0:T(8,128)(2,1)S(1)} %get-tuple-element.72.ohi_ref, bf16[640,480]{1,0:T(8,128)(2,1)S(1)} %get-tuple-element.73.olo_ref, ...), custom_call_target="tpu_custom_call" | custom-call | flops 314572800 | bytes 3932160 | tf_op jit(solution)/shard_map/pallas_call | solution.py:506
  37.9 1.3 %collective-permute-start.18 = (f32[4,40,128]{2,1,0:T(8,128)S(1)}, f32[4,40,128]{2,1,0:T(8,128)S(1)}, u32[]{:S(2)}, u32[]{:S(2)}) collective-permute-start(f32[4,40,128]{2,1,0:T(8,128)S(1)} %get-tuple-element.111), channel_id=1, source_target_pairs={{0,8},{8,0},{16,24},{24,16},{1,9},{9,1},{17,25},{25,17},{2,10},{10... | collective-permute-start | bytes 245768 | tf_op jit(solution)/shard_map/ppermute | solution.py:565
  39.2 0.8 %collective-permute-start.19 = (f32[4,40,128]{2,1,0:T(8,128)S(1)}, f32[4,40,128]{2,1,0:T(8,128)S(1)}, u32[]{:S(2)}, u32[]{:S(2)}) collective-permute-start(f32[4,40,128]{2,1,0:T(8,128)S(1)} %get-tuple-element.112), channel_id=1, source_target_pairs={{0,16},{8,24},{16,0},{24,8},{1,17},{9,25},{17,1},{25,9},{2,18},{10... | collective-permute-start | bytes 245768 | tf_op jit(solution)/shard_map/ppermute | solution.py:565
  40.0 1.4 %collective-permute-start.20 = (f32[4,40,128]{2,1,0:T(8,128)S(1)}, f32[4,40,128]{2,1,0:T(8,128)S(1)}, u32[]{:S(2)}, u32[]{:S(2)}) collective-permute-start(f32[4,40,128]{2,1,0:T(8,128)S(1)} %get-tuple-element.113), channel_id=1, source_target_pairs={{0,24},{8,16},{16,8},{24,0},{1,25},{9,17},{17,9},{25,1},{2,26},{10... | collective-permute-start | bytes 245768 | tf_op jit(solution)/shard_map/ppermute | solution.py:565
  41.5 2.1 %collective-permute-done.12.refs_2_ = f32[4,160,128]{2,1,0:T(8,128)S(1)} collective-permute-done((f32[4,160,128]{2,1,0:T(8,128)S(1)}, f32[4,160,128]{2,1,0:T(8,128)S(1)}, u32[]{:S(2)}, u32[]{:S(2)}) %collective-permute-start.12) | collective-permute-done | bytes 327712 | tf_op jit(solution)/shard_map/ppermute | solution.py:565
  43.6 2.0 %collective-permute-done.13.refs_3_ = f32[4,160,128]{2,1,0:T(8,128)S(1)} collective-permute-done((f32[4,160,128]{2,1,0:T(8,128)S(1)}, f32[4,160,128]{2,1,0:T(8,128)S(1)}, u32[]{:S(2)}, u32[]{:S(2)}) %collective-permute-start.13) | collective-permute-done | bytes 327712 | tf_op jit(solution)/shard_map/ppermute | solution.py:565
  45.6 0.5 shard_map.87
  46.1 0.2 collective-permute-start.15
  46.3 3.0 %collective-permute-start.14 = (f32[192,128]{1,0:T(8,128)S(1)}, f32[192,128]{1,0:T(8,128)S(1)}, u32[]{:S(2)}, u32[]{:S(2)}) collective-permute-start(f32[192,128]{1,0:T(8,128)S(1)} %get-tuple-element.107), channel_id=1, source_target_pairs={{0,2},{1,3},{2,4},{3,5},{4,6},{5,7},{6,0},{7,1},{8,10},{9,11},{10,... | collective-permute-start | bytes 294920 | tf_op jit(solution)/shard_map/ppermute | solution.py:576
  49.3 0.8 %collective-permute-start.16 = (f32[192,128]{1,0:T(8,128)S(1)}, f32[192,128]{1,0:T(8,128)S(1)}, u32[]{:S(2)}, u32[]{:S(2)}) collective-permute-start(f32[192,128]{1,0:T(8,128)S(1)} %get-tuple-element.109), channel_id=1, source_target_pairs={{0,6},{1,7},{2,0},{3,1},{4,2},{5,3},{6,4},{7,5},{8,14},{9,15},{10,... | collective-permute-start | bytes 294920 | tf_op jit(solution)/shard_map/ppermute | solution.py:576
  50.1 1.7 %shard_map.88.in_ref = f32[4,640,128]{2,1,0:T(8,128)S(1)} custom-call(bf16[640,640]{1,0:T(8,128)(2,1)S(1)} %get-tuple-element.78.hi_ref, bf16[640,640]{1,0:T(8,128)(2,1)S(1)} %get-tuple-element.79.lo_ref, f32[4,640,128]{2,1,0:T(8,128)S(1)} %get-tuple-element.123.u_ref), custom_call_target="tpu_custom_call" | custom-call | flops 1258291200 | bytes 3932160 | tf_op jit(solution)/shard_map/pallas_call | solution.py:313
  51.8 0.4 shard_map.89
  52.2 0.3 collective-permute-start.24
  52.5 2.2 %collective-permute-start.25 = (f32[4,200,128]{2,1,0:T(8,128)S(1)}, f32[4,200,128]{2,1,0:T(8,128)S(1)}, u32[]{:S(2)}, u32[]{:S(2)}) collective-permute-start(f32[4,200,128]{2,1,0:T(8,128)S(1)} %get-tuple-element.125), channel_id=1, source_target_pairs={{0,16},{8,24},{16,0},{24,8},{1,17},{9,25},{17,1},{25,9},{2,18},{10... | collective-permute-start | bytes 1228808 | tf_op jit(solution)/shard_map/ppermute | solution.py:565
  54.7 1.0 %collective-permute-start.26 = (f32[4,200,128]{2,1,0:T(8,128)S(1)}, f32[4,200,128]{2,1,0:T(8,128)S(1)}, u32[]{:S(2)}, u32[]{:S(2)}) collective-permute-start(f32[4,200,128]{2,1,0:T(8,128)S(1)} %get-tuple-element.126), channel_id=1, source_target_pairs={{0,24},{8,16},{16,8},{24,0},{1,25},{9,17},{17,9},{25,1},{2,26},{10... | collective-permute-start | bytes 1228808 | tf_op jit(solution)/shard_map/ppermute | solution.py:565
  55.8 0.5 collective-permute-start.22
  56.3 0.8 %collective-permute-done.17.refs_4_.refs_0_ = f32[224,128]{1,0:T(8,128)S(1)} collective-permute-done((f32[224,128]{1,0:T(8,128)S(1)}, f32[224,128]{1,0:T(8,128)S(1)}, u32[]{:S(2)}, u32[]{:S(2)}) %collective-permute-start.17) | collective-permute-done | bytes 114720 | tf_op jit(solution)/shard_map/ppermute | solution.py:581
  57.1 0.2 collective-permute-start.21
  57.2 0.4 collective-permute-start.23
  57.6 0.8 %collective-permute-done.21.refs_5_.refs_2_ = f32[192,128]{1,0:T(8,128)S(1)} collective-permute-done((f32[192,128]{1,0:T(8,128)S(1)}, f32[192,128]{1,0:T(8,128)S(1)}, u32[]{:S(2)}, u32[]{:S(2)}) %collective-permute-start.21) | collective-permute-done | bytes 98336 | tf_op jit(solution)/shard_map/ppermute | solution.py:581
  58.4 0.2 collective-permute-done.23.refs_7_.refs_1_
  58.6 0.7 %shard_map.90 = (f32[160,128]{1,0:T(8,128)S(1)}, f32[160,128]{1,0:T(8,128)S(1)}, f32[160,128]{1,0:T(8,128)S(1)}, f32[160,128]{1,0:T(8,128)S(1)}) custom-call(s32[4]{0:T(128)S(1)} %copy-done.4, s32[4]{0:T(128)S(1)} %copy-done.5, f32[224,128]{1,0:T(8,128)S(1)} %get-tuple-element.106.refs_0_, f32[192,128]{1,0:T(8,128)S(1)} %collective-permute-done.14.refs_1_, ...), custom_call_target="tpu_custom_call" | custom-call | bytes 1966080 | tf_op jit(solution)/shard_map/pallas_call | solution.py:272
  59.3 1.3 %collective-permute-start.27 = (f32[160,128]{1,0:T(8,128)S(1)}, f32[160,128]{1,0:T(8,128)S(1)}, u32[]{:S(2)}, u32[]{:S(2)}) collective-permute-start(f32[160,128]{1,0:T(8,128)S(1)} %get-tuple-element.127), channel_id=1, source_target_pairs={{0,2},{1,3},{2,4},{3,5},{4,6},{5,7},{6,0},{7,1},{8,10},{9,11},{10,... | collective-permute-start | bytes 245768 | tf_op jit(solution)/shard_map/ppermute | solution.py:576
  60.6 0.2 collective-permute-start.28
  60.8 5.7 %collective-permute-done.27.refs_5_ = f32[160,128]{1,0:T(8,128)S(1)} collective-permute-done((f32[160,128]{1,0:T(8,128)S(1)}, f32[160,128]{1,0:T(8,128)S(1)}, u32[]{:S(2)}, u32[]{:S(2)}) %collective-permute-start.27) | collective-permute-done | bytes 81952 | tf_op jit(solution)/shard_map/ppermute | solution.py:576
  66.5 1.9 %shard_map.91.w_ref = f32[4,640,128]{2,1,0:T(8,128)S(1)} custom-call(s32[2,128]{1,0:T(2,128)S(1)} %copy-done.3, bf16[640,480]{1,0:T(8,128)(2,1)S(1)} %get-tuple-element.72.ohi_ref, bf16[640,480]{1,0:T(8,128)(2,1)S(1)} %get-tuple-element.73.olo_ref, f32[4,640,128]{2,1,0:T(8,128)S(1)} %get-tuple-element.123.u_ref, f32[4,640,128]{2,1,0:T(8,128)S(1)} %shard_map.88.in_ref, ...), custom_call_target="tpu_custom_call" | custom-call | flops 629145600 | bytes 3932160 | tf_op jit(solution)/shard_map/pallas_call | solution.py:365
  68.4 1.1 %collective-permute-done.28.refs_6_ = f32[160,128]{1,0:T(8,128)S(1)} collective-permute-done((f32[160,128]{1,0:T(8,128)S(1)}, f32[160,128]{1,0:T(8,128)S(1)}, u32[]{:S(2)}, u32[]{:S(2)}) %collective-permute-start.28) | collective-permute-done | bytes 81952 | tf_op jit(solution)/shard_map/ppermute | solution.py:576
  69.5 1.5 %collective-permute-done.29.refs_7_ = f32[160,128]{1,0:T(8,128)S(1)} collective-permute-done((f32[160,128]{1,0:T(8,128)S(1)}, f32[160,128]{1,0:T(8,128)S(1)}, u32[]{:S(2)}, u32[]{:S(2)}) %collective-permute-start.29) | collective-permute-done | bytes 81952 | tf_op jit(solution)/shard_map/ppermute | solution.py:576
  71.0 0.6 collective-permute-done.25.refs_2_
  71.6 2.3 %shard_map.92 = (f32[4,640,128]{2,1,0:T(8,128)}, f32[4,640,128]{2,1,0:T(8,128)}) custom-call(bf16[640,480]{1,0:T(8,128)(2,1)S(1)} %get-tuple-element.72.ohi_ref, bf16[640,480]{1,0:T(8,128)(2,1)S(1)} %get-tuple-element.73.olo_ref, f32[4,640,128]{2,1,0:T(8,128)S(1)} %get-tuple-element.104.u_ref, f32[4,640,128]{2,1,0:T(8,128)S(1)} %shard_map.91.w_ref, ...), custom_call_target="tpu_custom_call" | custom-call | flops 314572800 | bytes 6553600 | tf_op jit(solution)/shard_map/pallas_call | solution.py:560
  (27 shorter events, 0.1 us)
Async XLA Ops:
  0.6 1.3 %copy-start = (f32[4,10,64,128]{3,2,1,0:T(8,128)S(1)}, f32[4,10,64,128]{3,2,1,0:T(8,128)}, u32[]{:S(2)}) copy-start(f32[4,10,64,128]{3,2,1,0:T(8,128)} %param.6) | copy-start | bytes 3932164
  2.2 11.3 %copy-start.6 = (f32[2,10,10]{2,0,1:T(2,128)S(1)}, f32[2,10,10]{2,0,1:T(2,128)}, u32[]{:S(2)}) copy-start(f32[2,10,10]{2,0,1:T(2,128)} %param.11) | copy-start | bytes 2404
  2.2 11.3 %copy-start.2 = (f32[2,64,64]{2,1,0:T(8,128)S(1)}, f32[2,64,64]{2,1,0:T(8,128)}, u32[]{:S(2)}) copy-start(f32[2,64,64]{2,1,0:T(8,128)} %vol_ref.1) | copy-start | bytes 98308
  2.2 14.8 %copy-start.1 = (f32[4,10,64,128]{3,2,1,0:T(8,128)S(1)}, f32[4,10,64,128]{3,2,1,0:T(8,128)}, u32[]{:S(2)}) copy-start(f32[4,10,64,128]{3,2,1,0:T(8,128)} %param.6) | copy-start | bytes 3932164
  2.6 1.8 %collective-permute-start = (f32[4,160,128]{2,1,0:T(8,128)S(1)}, f32[4,160,128]{2,1,0:T(8,128)S(1)}, u32[]{:S(2)}, u32[]{:S(2)}) collective-permute-start(f32[4,160,128]{2,1,0:T(8,128)S(1)} %get-tuple-element.70), channel_id=1, source_target_pairs={{0,1},{1,0},{2,3},{3,2},{4,5},{5,4},{6,7},{7,6},{8,9},{9,8},{10,11... | collective-permute-start | bytes 983048 | tf_op jit(solution)/shard_map/ppermute | solution.py:581
  4.4 14.4 %collective-permute-start.4 = (f32[352,128]{1,0:T(8,128)S(1)}, f32[352,128]{1,0:T(8,128)S(1)}, u32[]{:S(2)}, u32[]{:S(2)}) collective-permute-start(f32[352,128]{1,0:T(8,128)S(1)} %shard_map.79), channel_id=1, source_target_pairs={{0,2},{1,7},{2,4},{3,1},{4,6},{5,3},{6,0},{7,5},{8,10},{9,15},{10,... | collective-permute-start | bytes 540680 | tf_op jit(solution)/shard_map/ppermute | solution.py:571
  7.4 13.9 %collective-permute-start.1 = (f32[4,160,128]{2,1,0:T(8,128)S(1)}, f32[4,160,128]{2,1,0:T(8,128)S(1)}, u32[]{:S(2)}, u32[]{:S(2)}) collective-permute-start(f32[4,160,128]{2,1,0:T(8,128)S(1)} %get-tuple-element.74), channel_id=1, source_target_pairs={{0,8},{8,0},{16,24},{24,16},{1,9},{9,1},{17,25},{25,17},{2,10},{10... | collective-permute-start | bytes 983048 | tf_op jit(solution)/shard_map/ppermute | solution.py:565
  8.9 16.1 %collective-permute-start.2 = (f32[4,160,128]{2,1,0:T(8,128)S(1)}, f32[4,160,128]{2,1,0:T(8,128)S(1)}, u32[]{:S(2)}, u32[]{:S(2)}) collective-permute-start(f32[4,160,128]{2,1,0:T(8,128)S(1)} %get-tuple-element.75), channel_id=1, source_target_pairs={{0,16},{8,24},{16,0},{24,8},{1,17},{9,25},{17,1},{25,9},{2,18},{10... | collective-permute-start | bytes 983048 | tf_op jit(solution)/shard_map/ppermute | solution.py:565
  10.4 14.8 %collective-permute-start.3 = (f32[4,160,128]{2,1,0:T(8,128)S(1)}, f32[4,160,128]{2,1,0:T(8,128)S(1)}, u32[]{:S(2)}, u32[]{:S(2)}) collective-permute-start(f32[4,160,128]{2,1,0:T(8,128)S(1)} %get-tuple-element.76), channel_id=1, source_target_pairs={{0,24},{8,16},{16,8},{24,0},{1,25},{9,17},{17,9},{25,1},{2,26},{10... | collective-permute-start | bytes 983048 | tf_op jit(solution)/shard_map/ppermute | solution.py:565
  10.9 7.9 %collective-permute-start.5 = (f32[160,128]{1,0:T(8,128)S(1)}, f32[160,128]{1,0:T(8,128)S(1)}, u32[]{:S(2)}, u32[]{:S(2)}) collective-permute-start(f32[160,128]{1,0:T(8,128)S(1)} %get-tuple-element.77), channel_id=1, source_target_pairs={{0,4},{1,5},{2,6},{3,7},{4,0},{5,1},{6,2},{7,3},{8,12},{9,13},{10,... | collective-permute-start | bytes 245768 | tf_op jit(solution)/shard_map/ppermute | solution.py:571
  17.0 3.4 %copy-start.4 = (s32[4]{0:T(128)S(1)}, s32[4]{0:T(128)}, u32[]{:S(2)}) copy-start(s32[4]{0:T(128)} %group_ref.3) | copy-start | bytes 52
  17.0 3.4 %copy-start.5 = (s32[4]{0:T(128)S(1)}, s32[4]{0:T(128)}, u32[]{:S(2)}) copy-start(s32[4]{0:T(128)} %shift_ref.3) | copy-start | bytes 52
  18.7 12.5 %copy-start.3 = (s32[2,128]{1,0:T(2,128)S(1)}, s32[2,128]{1,0:T(2,128)}, u32[]{:S(2)}) copy-start(s32[2,128]{1,0:T(2,128)} %near_ref.3) | copy-start | bytes 3076
  18.8 1.6 %collective-permute-start.6 = (f32[352,128]{1,0:T(8,128)S(1)}, f32[352,128]{1,0:T(8,128)S(1)}, u32[]{:S(2)}, u32[]{:S(2)}) collective-permute-start(f32[352,128]{1,0:T(8,128)S(1)} %collective-permute-done.4.refs_0_.refs_1_), channel_id=1, source_target_pairs={{0,1},{1,0},{2,3},{3,2},{4,5},{5,4},{6,7},{7,6},{8,9},{9,8},{10,11... | collective-permute-start | bytes 540680 | tf_op jit(solution)/shard_map/ppermute | solution.py:581
  18.8 1.5 %collective-permute-start.7 = (f32[160,128]{1,0:T(8,128)S(1)}, f32[160,128]{1,0:T(8,128)S(1)}, u32[]{:S(2)}, u32[]{:S(2)}) collective-permute-start(f32[160,128]{1,0:T(8,128)S(1)} %collective-permute-done.5.refs_1_), channel_id=1, source_target_pairs={{0,1},{1,0},{2,3},{3,2},{4,5},{5,4},{6,7},{7,6},{8,9},{9,8},{10,11... | collective-permute-start | bytes 245768 | tf_op jit(solution)/shard_map/ppermute | solution.py:581
  21.1 8.9 %collective-permute-start.8 = (f32[320,128]{1,0:T(8,128)S(1)}, f32[320,128]{1,0:T(8,128)S(1)}, u32[]{:S(2)}, u32[]{:S(2)}) collective-permute-start(f32[320,128]{1,0:T(8,128)S(1)} %get-tuple-element.101), channel_id=1, source_target_pairs={{0,2},{1,7},{2,4},{3,1},{4,6},{5,3},{6,0},{7,5},{8,10},{9,15},{10,... | collective-permute-start | bytes 491528 | tf_op jit(solution)/shard_map/ppermute | solution.py:571
  26.2 13.8 %collective-permute-start.11 = (f32[4,160,128]{2,1,0:T(8,128)S(1)}, f32[4,160,128]{2,1,0:T(8,128)S(1)}, u32[]{:S(2)}, u32[]{:S(2)}) collective-permute-start(f32[4,160,128]{2,1,0:T(8,128)S(1)} %get-tuple-element.93.refs_1_), channel_id=1, source_target_pairs={{0,8},{8,0},{16,24},{24,16},{1,9},{9,1},{17,25},{25,17},{2,10},{10... | collective-permute-start | bytes 983048 | tf_op jit(solution)/shard_map/ppermute | solution.py:565
  27.7 15.9 %collective-permute-start.12 = (f32[4,160,128]{2,1,0:T(8,128)S(1)}, f32[4,160,128]{2,1,0:T(8,128)S(1)}, u32[]{:S(2)}, u32[]{:S(2)}) collective-permute-start(f32[4,160,128]{2,1,0:T(8,128)S(1)} %get-tuple-element.94.refs_2_), channel_id=1, source_target_pairs={{0,16},{8,24},{16,0},{24,8},{1,17},{9,25},{17,1},{25,9},{2,18},{10... | collective-permute-start | bytes 983048 | tf_op jit(solution)/shard_map/ppermute | solution.py:565
  28.7 16.9 %collective-permute-start.13 = (f32[4,160,128]{2,1,0:T(8,128)S(1)}, f32[4,160,128]{2,1,0:T(8,128)S(1)}, u32[]{:S(2)}, u32[]{:S(2)}) collective-permute-start(f32[4,160,128]{2,1,0:T(8,128)S(1)} %get-tuple-element.95.refs_3_), channel_id=1, source_target_pairs={{0,24},{8,16},{16,8},{24,0},{1,25},{9,17},{17,9},{25,1},{2,26},{10... | collective-permute-start | bytes 983048 | tf_op jit(solution)/shard_map/ppermute | solution.py:565
  30.1 7.1 %collective-permute-start.10 = (f32[320,128]{1,0:T(8,128)S(1)}, f32[320,128]{1,0:T(8,128)S(1)}, u32[]{:S(2)}, u32[]{:S(2)}) collective-permute-start(f32[320,128]{1,0:T(8,128)S(1)} %collective-permute-done.8.refs_1_), channel_id=1, source_target_pairs={{0,1},{1,0},{2,3},{3,2},{4,5},{5,4},{6,7},{7,6},{8,9},{9,8},{10,11... | collective-permute-start | bytes 491528 | tf_op jit(solution)/shard_map/ppermute | solution.py:581
  30.1 7.0 %collective-permute-start.9 = (f32[160,128]{1,0:T(8,128)S(1)}, f32[160,128]{1,0:T(8,128)S(1)}, u32[]{:S(2)}, u32[]{:S(2)}) collective-permute-start(f32[160,128]{1,0:T(8,128)S(1)} %get-tuple-element.102), channel_id=1, source_target_pairs={{0,4},{1,5},{2,6},{3,7},{4,0},{5,1},{6,2},{7,3},{8,12},{9,13},{10,... | collective-permute-start | bytes 245768 | tf_op jit(solution)/shard_map/ppermute | solution.py:571
  37.9 11.4 %collective-permute-start.18 = (f32[4,40,128]{2,1,0:T(8,128)S(1)}, f32[4,40,128]{2,1,0:T(8,128)S(1)}, u32[]{:S(2)}, u32[]{:S(2)}) collective-permute-start(f32[4,40,128]{2,1,0:T(8,128)S(1)} %get-tuple-element.111), channel_id=1, source_target_pairs={{0,8},{8,0},{16,24},{24,16},{1,9},{9,1},{17,25},{25,17},{2,10},{10... | collective-permute-start | bytes 245768 | tf_op jit(solution)/shard_map/ppermute | solution.py:565
  39.2 12.6 %collective-permute-start.19 = (f32[4,40,128]{2,1,0:T(8,128)S(1)}, f32[4,40,128]{2,1,0:T(8,128)S(1)}, u32[]{:S(2)}, u32[]{:S(2)}) collective-permute-start(f32[4,40,128]{2,1,0:T(8,128)S(1)} %get-tuple-element.112), channel_id=1, source_target_pairs={{0,16},{8,24},{16,0},{24,8},{1,17},{9,25},{17,1},{25,9},{2,18},{10... | collective-permute-start | bytes 245768 | tf_op jit(solution)/shard_map/ppermute | solution.py:565
  40.0 11.8 %collective-permute-start.20 = (f32[4,40,128]{2,1,0:T(8,128)S(1)}, f32[4,40,128]{2,1,0:T(8,128)S(1)}, u32[]{:S(2)}, u32[]{:S(2)}) collective-permute-start(f32[4,40,128]{2,1,0:T(8,128)S(1)} %get-tuple-element.113), channel_id=1, source_target_pairs={{0,24},{8,16},{16,8},{24,0},{1,25},{9,17},{17,9},{25,1},{2,26},{10... | collective-permute-start | bytes 245768 | tf_op jit(solution)/shard_map/ppermute | solution.py:565
  46.1 8.7 %collective-permute-start.15 = (f32[160,128]{1,0:T(8,128)S(1)}, f32[160,128]{1,0:T(8,128)S(1)}, u32[]{:S(2)}, u32[]{:S(2)}) collective-permute-start(f32[160,128]{1,0:T(8,128)S(1)} %get-tuple-element.108), channel_id=1, source_target_pairs={{0,4},{1,5},{2,6},{3,7},{4,0},{5,1},{6,2},{7,3},{8,12},{9,13},{10,... | collective-permute-start | bytes 245768 | tf_op jit(solution)/shard_map/ppermute | solution.py:576
  46.3 9.5 %collective-permute-start.14 = (f32[192,128]{1,0:T(8,128)S(1)}, f32[192,128]{1,0:T(8,128)S(1)}, u32[]{:S(2)}, u32[]{:S(2)}) collective-permute-start(f32[192,128]{1,0:T(8,128)S(1)} %get-tuple-element.107), channel_id=1, source_target_pairs={{0,2},{1,3},{2,4},{3,5},{4,6},{5,7},{6,0},{7,1},{8,10},{9,11},{10,... | collective-permute-start | bytes 294920 | tf_op jit(solution)/shard_map/ppermute | solution.py:576
  49.3 6.5 %collective-permute-start.16 = (f32[192,128]{1,0:T(8,128)S(1)}, f32[192,128]{1,0:T(8,128)S(1)}, u32[]{:S(2)}, u32[]{:S(2)}) collective-permute-start(f32[192,128]{1,0:T(8,128)S(1)} %get-tuple-element.109), channel_id=1, source_target_pairs={{0,6},{1,7},{2,0},{3,1},{4,2},{5,3},{6,4},{7,5},{8,14},{9,15},{10,... | collective-permute-start | bytes 294920 | tf_op jit(solution)/shard_map/ppermute | solution.py:576
  52.2 18.8 %collective-permute-start.24 = (f32[4,200,128]{2,1,0:T(8,128)S(1)}, f32[4,200,128]{2,1,0:T(8,128)S(1)}, u32[]{:S(2)}, u32[]{:S(2)}) collective-permute-start(f32[4,200,128]{2,1,0:T(8,128)S(1)} %get-tuple-element.124), channel_id=1, source_target_pairs={{0,8},{8,0},{16,24},{24,16},{1,9},{9,1},{17,25},{25,17},{2,10},{10... | collective-permute-start | bytes 1228808 | tf_op jit(solution)/shard_map/ppermute | solution.py:565
  52.5 19.1 %collective-permute-start.25 = (f32[4,200,128]{2,1,0:T(8,128)S(1)}, f32[4,200,128]{2,1,0:T(8,128)S(1)}, u32[]{:S(2)}, u32[]{:S(2)}) collective-permute-start(f32[4,200,128]{2,1,0:T(8,128)S(1)} %get-tuple-element.125), channel_id=1, source_target_pairs={{0,16},{8,24},{16,0},{24,8},{1,17},{9,25},{17,1},{25,9},{2,18},{10... | collective-permute-start | bytes 1228808 | tf_op jit(solution)/shard_map/ppermute | solution.py:565
  54.7 16.9 %collective-permute-start.26 = (f32[4,200,128]{2,1,0:T(8,128)S(1)}, f32[4,200,128]{2,1,0:T(8,128)S(1)}, u32[]{:S(2)}, u32[]{:S(2)}) collective-permute-start(f32[4,200,128]{2,1,0:T(8,128)S(1)} %get-tuple-element.126), channel_id=1, source_target_pairs={{0,24},{8,16},{16,8},{24,0},{1,25},{9,17},{17,9},{25,1},{2,26},{10... | collective-permute-start | bytes 1228808 | tf_op jit(solution)/shard_map/ppermute | solution.py:565
  55.8 1.3 %collective-permute-start.17 = (f32[224,128]{1,0:T(8,128)S(1)}, f32[224,128]{1,0:T(8,128)S(1)}, u32[]{:S(2)}, u32[]{:S(2)}) collective-permute-start(f32[224,128]{1,0:T(8,128)S(1)} %get-tuple-element.106.refs_0_), channel_id=1, source_target_pairs={{0,1},{1,0},{2,3},{3,2},{4,5},{5,4},{6,7},{7,6},{8,9},{9,8},{10,11... | collective-permute-start | bytes 344072 | tf_op jit(solution)/shard_map/ppermute | solution.py:581
  55.8 1.5 %collective-permute-start.22 = (f32[160,128]{1,0:T(8,128)S(1)}, f32[160,128]{1,0:T(8,128)S(1)}, u32[]{:S(2)}, u32[]{:S(2)}) collective-permute-start(f32[160,128]{1,0:T(8,128)S(1)} %collective-permute-done.15.refs_2_), channel_id=1, source_target_pairs={{0,1},{1,0},{2,3},{3,2},{4,5},{5,4},{6,7},{7,6},{8,9},{9,8},{10,11... | collective-permute-start | bytes 245768 | tf_op jit(solution)/shard_map/ppermute | solution.py:581
  57.1 1.3 %collective-permute-start.21 = (f32[192,128]{1,0:T(8,128)S(1)}, f32[192,128]{1,0:T(8,128)S(1)}, u32[]{:S(2)}, u32[]{:S(2)}) collective-permute-start(f32[192,128]{1,0:T(8,128)S(1)} %collective-permute-done.14.refs_1_), channel_id=1, source_target_pairs={{0,1},{1,0},{2,3},{3,2},{4,5},{5,4},{6,7},{7,6},{8,9},{9,8},{10,11... | collective-permute-start | bytes 294920 | tf_op jit(solution)/shard_map/ppermute | solution.py:581
  57.2 1.3 %collective-permute-start.23 = (f32[192,128]{1,0:T(8,128)S(1)}, f32[192,128]{1,0:T(8,128)S(1)}, u32[]{:S(2)}, u32[]{:S(2)}) collective-permute-start(f32[192,128]{1,0:T(8,128)S(1)} %collective-permute-done.16.refs_3_), channel_id=1, source_target_pairs={{0,1},{1,0},{2,3},{3,2},{4,5},{5,4},{6,7},{7,6},{8,9},{9,8},{10,11... | collective-permute-start | bytes 294920 | tf_op jit(solution)/shard_map/ppermute | solution.py:581
  59.3 7.2 %collective-permute-start.27 = (f32[160,128]{1,0:T(8,128)S(1)}, f32[160,128]{1,0:T(8,128)S(1)}, u32[]{:S(2)}, u32[]{:S(2)}) collective-permute-start(f32[160,128]{1,0:T(8,128)S(1)} %get-tuple-element.127), channel_id=1, source_target_pairs={{0,2},{1,3},{2,4},{3,5},{4,6},{5,7},{6,0},{7,1},{8,10},{9,11},{10,... | collective-permute-start | bytes 245768 | tf_op jit(solution)/shard_map/ppermute | solution.py:576
  60.6 8.9 %collective-permute-start.28 = (f32[160,128]{1,0:T(8,128)S(1)}, f32[160,128]{1,0:T(8,128)S(1)}, u32[]{:S(2)}, u32[]{:S(2)}) collective-permute-start(f32[160,128]{1,0:T(8,128)S(1)} %get-tuple-element.128), channel_id=1, source_target_pairs={{0,4},{1,5},{2,6},{3,7},{4,0},{5,1},{6,2},{7,3},{8,12},{9,13},{10,... | collective-permute-start | bytes 245768 | tf_op jit(solution)/shard_map/ppermute | solution.py:576
  66.5 4.5 %collective-permute-start.29 = (f32[160,128]{1,0:T(8,128)S(1)}, f32[160,128]{1,0:T(8,128)S(1)}, u32[]{:S(2)}, u32[]{:S(2)}) collective-permute-start(f32[160,128]{1,0:T(8,128)S(1)} %get-tuple-element.129), channel_id=1, source_target_pairs={{0,6},{1,7},{2,0},{3,1},{4,2},{5,3},{6,4},{7,5},{8,14},{9,15},{10,... | collective-permute-start | bytes 245768 | tf_op jit(solution)/shard_map/ppermute | solution.py:576
